TPU v7x, 32 devices: a whole 2x2x4 slice. The times are simulated.
32 devices in a mesh: gx: 4 (over y, core), gy: 4 (over z), gz: 2 (over x).
Axes of the slice: x: 2, y: 2, z: 4, core: 2. Of those that a mesh axis runs over, the one named last changes fastest.
Arguments:
- les_state: float32 [5, 32, 32, 256], P(None, 'gx', 'gy', 'gz'), may hold values from -0.4 to 0.4
- acoustic_state: float32 [4, 32, 32, 256], P(None, 'gx', 'gy', 'gz'), may hold values from -0.04 to 0.04
- mean_flow: float32 [3, 32, 32, 256], P(None, 'gx', 'gy', 'gz'), may hold values from -0.5 to 0.5
- projection: float32 [8, 8], replicated, may hold values from -0.3 to 1.3, as said below
- target_owner: int32 [4, 4, 32], P('gx', 'gy', 'gz'), may hold values from 0 to 3, as said below
- target_slot: int32 [4, 4, 32], P('gx', 'gy', 'gz'), may hold values from 0 to 15
Outputs:
- les_next: float32 [5, 32, 32, 256], P(None, 'gx', 'gy', 'gz')
- source_nodes: float32 [3, 32, 32, 256], P(None, 'gx', 'gy', 'gz')
- acoustic_next: float32 [4, 32, 32, 256], P(None, 'gx', 'gy', 'gz')
Inputs may be any that keep to these rules, and one draw needn't show every extreme that they name: `target_owner`: the blocks of the device with index i along gx name as owners exactly the 4 consecutive indices from (i * (4 - 3)) // 4 on, each for exactly 4 blocks. `projection`: diagonal entries lie in 0.7 to 1.3, the others in -0.3 to 0.3.
All inputs are finite; a program needn't handle non-finite values.
Results may differ from a plain program's by a relative error of at most 0.00011.
Values sent between devices are 32-bit elements; how exact they have to be, the bound alone decides.
No kernel may reach another device: no remote copies, remote signals or barrier semaphores. Data moves between devices by JAX's collectives and lax.ppermute only.
A program may use at most 64 MiB of HBM per device.

v0:
```python
import functools

import jax
import jax.numpy as jnp
import numpy as np
from jax import lax
from jax.experimental import pallas as pl
from jax.experimental.pallas import tpu as pltpu
from jax.sharding import PartitionSpec as P

lobatto_points = np.array(
    [
        -1.0,
        -0.8717401485096066,
        -0.5917001814331423,
        -0.2092992179024789,
        0.2092992179024789,
        0.5917001814331423,
        0.8717401485096066,
        1.0,
    ]
)
flux_half = 0.08
gamma_less = 0.4
acoustic_step = 0.01
upwind_speed = 1.5
face_lift = 28.0
free_stream = (1.0, 0.0, 0.0, 0.0, 2.5)
axes = ("gx", "gy", "gz")
window = 4
f32 = jnp.float32


def derivative_matrix():
    points = lobatto_points
    products = [np.prod([points[i] - points[j] for j in range(8) if j != i]) for i in range(8)]
    matrix = np.zeros((8, 8))
    for i in range(8):
        for j in range(8):
            if j != i:
                matrix[i, j] = products[i] / (products[j] * (points[i] - points[j]))
        matrix[i, i] = -np.sum(matrix[i])
    return matrix


def sublane(shape):
    return lax.broadcasted_iota(jnp.int32, shape, len(shape) - 2)


def lane(shape):
    return lax.broadcasted_iota(jnp.int32, shape, len(shape) - 1)


def rolled(tile, amount, axis):
    amount = amount % tile.shape[axis]
    return pltpu.roll(tile, amount, axis) if amount else tile


def shifted(field, axis, step, outer=None):
    if axis == 0:
        outer = jnp.zeros((8, 128), f32) if outer is None else outer
        if step == 1:
            return jnp.concatenate([field[1:], outer[None]], axis=0)
        return jnp.concatenate([outer[None], field[:-1]], axis=0)
    count = (8, 128)[axis - 1]
    edge = count - 1 if step == 1 else 0
    at_edge = (sublane if axis == 1 else lane)((8, 128)) == edge
    planes = []
    for x in range(8):
        layer = 0.0 if outer is None else rolled(outer, edge - axis * x, axis - 1)
        planes.append(jnp.where(at_edge, layer, rolled(field[x], -step, axis - 1)))
    return jnp.stack(planes, axis=0)


def fluid(state):
    density, mx, my, mz, energy = [s + r for s, r in zip(state, free_stream)]
    inverse = 1.0 / density
    momentum = (mx, my, mz)
    velocity = [m * inverse for m in momentum]
    pressure = gamma_less * (
        energy - 0.5 * (mx * velocity[0] + my * velocity[1] + mz * velocity[2])
    )
    return momentum, velocity, pressure, energy + pressure


def split_flux(state, parts, axis, sign):
    momentum, velocity, pressure, enthalpy = parts
    speed = velocity[axis]
    flux = [momentum[axis]]
    for c in range(3):
        term = momentum[c] * speed
        flux.append(term + pressure if c == axis else term)
    flux.append(enthalpy * speed)
    if sign > 0:
        return [flux_half * (s + f) for s, f in zip(state, flux)]
    return [flux_half * (s - f) for s, f in zip(state, flux)]


def les_rate(state, halos):
    parts = fluid(state)
    total = [-6.0 * flux_half * s for s in state]
    for axis in range(3):
        ahead = split_flux(state, parts, axis, -1)
        behind = split_flux(state, parts, axis, 1)
        ahead_outer = behind_outer = [None] * 5
        if halos is not None:
            before, after = halos[axis]
            ahead_outer = split_flux(after, fluid(after), axis, -1)
            behind_outer = split_flux(before, fluid(before), axis, 1)
        for c in range(5):
            total[c] = total[c] + (
                shifted(ahead[c], axis, 1, ahead_outer[c])
                + shifted(behind[c], axis, -1, behind_outer[c])
            )
    return total


def les_outer(halos):
    return [
        halo
        and (
            split_flux(halo[0], fluid(halo[0]), axis, 1),
            split_flux(halo[1], fluid(halo[1]), axis, -1),
        )
        for axis, halo in enumerate(halos)
    ]


def with_layers(field, layers):
    row, column = sublane((8, 128)), lane((8, 128))
    along_z = layers[2]
    if along_z is not None:
        along_z = jnp.where(lax.rem(column, 2) == 0, along_z[0], rolled(along_z[1], -1, 1))
    planes = []
    for x in range(8):
        plane = field[x]
        if layers[0] is not None and x in (0, 7):
            plane = plane + layers[0][x // 7]
        if layers[1] is not None:
            low, high = layers[1]
            plane = plane + jnp.where(
                row == 0, rolled(low, -x, 0), jnp.where(row == 7, rolled(high, 7 - x, 0), 0.0)
            )
        if along_z is not None:
            ends = (column == 0) | (column == 127)
            plane = plane + jnp.where(ends, rolled(along_z, -2 * x, 1), 0.0)
        planes.append(plane)
    return planes


def wave_flux(state, mean, axis):
    speed = mean[axis]
    pressure = state[0]
    rows = [speed * pressure + state[1 + axis]]
    for c in range(3):
        term = speed * state[1 + c]
        rows.append(term + pressure if c == axis else term)
    return rows


def dot3(left, right):
    high = left.astype(jnp.bfloat16)
    low = (left - high.astype(f32)).astype(jnp.bfloat16)
    dot = functools.partial(jnp.dot, preferred_element_type=f32)
    return dot(high, right[0]) + (dot(low, right[0]) + dot(high, right[1]))


def acoustic_rate(state, mean, halos, deriv, along_z):
    shape = state[0].shape
    table = derivative_matrix()
    flux = wave_flux(state, mean, 0)
    if halos is None:
        halos = [([jnp.zeros((8, 128), f32)] * 4,) * 2] + [([None] * 4,) * 2] * 2
    before, after = halos[0]
    low_mean, high_mean = [m[0] for m in mean], [m[7] for m in mean]
    low_jump = [b - s[0] for b, s in zip(before, state)]
    high_jump = [a - s[7] for a, s in zip(after, state)]
    low_flux = wave_flux(low_jump, low_mean, 0)
    high_flux = wave_flux(high_jump, high_mean, 0)
    half, lift = 0.5 * face_lift, 0.5 * face_lift * upwind_speed
    total = []
    for c in range(4):
        planes = []
        for i in range(8):
            plane = -float(table[i, 0]) * flux[c][0]
            for a in range(1, 8):
                if abs(table[i, a]) > 1e-12:
                    plane = plane - float(table[i, a]) * flux[c][a]
            if i == 0:
                plane = plane + (half * low_flux[c] + lift * low_jump[c])
            if i == 7:
                plane = plane - (half * high_flux[c] - lift * high_jump[c])
            planes.append(plane)
        total.append(jnp.stack(planes, axis=0))
    flux = wave_flux(state, mean, 1)
    before, after = halos[1]
    row = sublane(shape)
    sign = jnp.where(row == 0, half, jnp.where(row == 7, -half, 0.0))
    jump = []
    for s, b, a in zip(state, before, after):
        planes = []
        for x in range(8):
            low = 0.0 if b is None else rolled(b, -x, 0)
            high = 0.0 if a is None else rolled(a, 7 - x, 0)
            planes.append(jnp.where(row[x] == 0, low, jnp.where(row[x] == 7, high, s[x])) - s[x])
        jump.append(jnp.stack(planes, axis=0))
    jump_flux = wave_flux(jump, mean, 1)
    for c in range(4):
        change = lift * jump[c] + sign * jump_flux[c]
        for b in range(8):
            change = change - deriv[:, b : b + 1][None] * flux[c][:, b : b + 1, :]
        total[c] = total[c] + change
    flux = wave_flux(state, mean, 2)
    before, after = halos[2]
    column = lane(shape)
    place = lax.rem(column, 8)
    sign = jnp.where(place == 0, half, jnp.where(place == 7, -half, 0.0))
    jump = [
        jnp.where(
            place == 0,
            shifted(s, 2, -1, b),
            jnp.where(place == 7, shifted(s, 2, 1, a), s),
        )
        - s
        for s, b, a in zip(state, before, after)
    ]
    jump_flux = wave_flux(jump, mean, 2)
    for c in range(4):
        slope = dot3(flux[c].reshape(64, 128), along_z).reshape(shape)
        total[c] = total[c] + (lift * jump[c] + sign * jump_flux[c] - slope)
    return total


def mean_layers(mean):
    return [
        [m[0] for m in mean],
        [m[7] for m in mean],
        [m[:, 0, :] for m in mean],
        [m[:, 7, :] for m in mean],
        [z_layer(m, jnp.int32(0)) for m in mean],
        [z_layer(m, jnp.int32(127)) for m in mean],
    ]


def acoustic_outer(mean_faces, halos):
    half, lift = 0.5 * face_lift, 0.5 * face_lift * upwind_speed
    layers = []
    for axis, halo in enumerate(halos):
        if halo is None:
            layers.append(None)
            continue
        before, after = halo
        low_flux = wave_flux(before, mean_faces[2 * axis], axis)
        high_flux = wave_flux(after, mean_faces[2 * axis + 1], axis)
        layers.append(
            (
                [half * f + lift * b for f, b in zip(low_flux, before)],
                [lift * a - half * f for f, a in zip(high_flux, after)],
            )
        )
    return layers


def tile_rows(matrix):
    spread = (lax.rem(lane((8, 128)), 8) == sublane((8, 128))).astype(f32)
    return jnp.dot(
        matrix, spread, precision=lax.Precision.HIGHEST, preferred_element_type=f32
    )


def pairings(count):
    sets = []
    for first in (0, 1):
        pairs = [(i, i + 1) for i in range(first, count - 1, 2)]
        if pairs:
            sets.append(pairs)
    return sets


def slots(counts):
    found = [(axis, n) for axis in range(3) for n in range(len(pairings(counts[axis])))]
    lower = ((2, 1), (2, 0), (0, 1), (1, 0), (1, 1), (0, 0))
    upper = ((2, 1), (0, 1), (2, 0), (0, 0), (1, 1), (1, 0))
    lower = [swap for swap in lower if swap in found]
    upper = [swap for swap in upper if swap in found] if counts[1] == 4 else lower
    return list(zip(lower, upper))


def in_upper_half(counts):
    return lax.axis_index("gy") >= counts[1] // 2


def routes(counts):
    places = [(x, y, z) for x in range(counts[0]) for y in range(counts[1]) for z in range(counts[2])]
    number = {place: n for n, place in enumerate(places)}

    def partner(place, axis, n):
        pairs = pairings(counts[axis])[n]
        swap = dict(pairs + [(j, i) for i, j in pairs])
        alone = [i for i in range(counts[axis]) if i not in swap]
        spare = 0 if axis else 2
        other = list(place)
        if place[axis] in swap:
            other[axis] = swap[place[axis]]
        elif axis == 0 and len(alone) == 2:
            other[axis] = sum(alone) - place[axis]
        elif counts[spare] % 2 == 0:
            other[spare] = place[spare] ^ 1
        return number[tuple(other)]

    return [
        [
            (number[place], partner(place, *(upper if place[1] >= counts[1] // 2 else lower)))
            for place in places
        ]
        for lower, upper in slots(counts)
    ]


def z_layer(field, at):
    packed = jnp.zeros((8, 128), f32)
    column = lane((8, 128))
    for x in range(8):
        turned = pltpu.roll(field[x], lax.rem(2 * x - at + 128, 128), 1)
        packed = jnp.where(column == 2 * x, turned, packed)
    return packed


def store_faces(fields, out_refs, counts):
    high_half = in_upper_half(counts)
    for c, field in enumerate(fields):
        faces = {}
        for axis in range(3):
            even = lax.rem(lax.axis_index(axes[axis]), 2) == 0
            if axis == 0:
                low, high = field[0], field[7]
            elif axis == 1:
                low, high = field[:, 0, :], field[:, 7, :]
            for n in range(len(pairings(counts[axis]))):
                last = even == (n == 0)
                if axis == 2:
                    faces[axis, n] = z_layer(field, jnp.where(last, 127, 0))
                else:
                    faces[axis, n] = jnp.where(last, high, low)
        for ref, (lower, upper) in zip(out_refs, slots(counts)):
            if lower == upper:
                ref[c] = faces[lower]
            else:
                ref[c] = jnp.where(high_half, faces[upper], faces[lower])


def load_faces(in_refs, counts, first, last, chosen=(0, 1, 2)):
    high_half = in_upper_half(counts)
    lower, upper = zip(*slots(counts))
    halos = []
    for axis in range(3):
        if axis not in chosen:
            halos.append(None)
            continue
        place = lax.axis_index(axes[axis])
        even = lax.rem(place, 2) == 0
        got = []
        for n in range(len(pairings(counts[axis]))):
            a, b = in_refs[lower.index((axis, n))], in_refs[upper.index((axis, n))]
            got.append(
                [a[c] if a is b else jnp.where(high_half, b[c], a[c]) for c in range(first, last)]
            )
        while len(got) < 2:
            got.append([jnp.zeros((8, 128), f32)] * (last - first))
        before = [jnp.where(place == 0, 0.0, jnp.where(even, b, a)) for a, b in zip(*got)]
        after = [
            jnp.where(place == counts[axis] - 1, 0.0, jnp.where(even, a, b))
            for a, b in zip(*got)
        ]
        halos.append((before, after))
    return halos


def face_shapes(counts, width):
    total = sum(len(pairings(count)) for count in counts)
    return [jax.ShapeDtypeStruct((width, 8, 128), f32)] * total


def exchange(faces, counts):
    return [lax.ppermute(face, axes, way) for face, way in zip(faces, routes(counts))]


def read_all(ref):
    return [ref[c] for c in range(ref.shape[0])]


def load_kernel(counts, *refs):
    sources, targets, out_refs, sems = refs[:5], refs[5:10], refs[10:-1], refs[-1]
    copies = [
        pltpu.make_async_copy(source, target, sems.at[n])
        for n, (source, target) in enumerate(zip(sources, targets))
    ]
    for copy in copies:
        copy.start()
    for copy, target, first in zip(copies, targets, (0, 5)):
        copy.wait()
        count = target.shape[0]
        store_faces(read_all(target), [ref.at[first : first + count] for ref in out_refs], counts)
    for copy in copies[2:]:
        copy.wait()


def partners(count):
    if count == window:
        return [[(i, i ^ mask) for i in range(count)] for mask in range(count)]
    turns = sorted({d % count for d in range(1 - window, window)})
    return [[(i, (i + turn) % count) for i in range(count)] for turn in turns]


def sending_sets(count):
    return [3, 2, 1, 0] if count == window else list(range(count))


def plan_kernel(
    counts, owner_ref, slot_ref, proj_ref, order_ref, marks_ref, along_x_ref, along_y_ref, tile_ref
):
    count = counts[0]
    n_sets = len(partners(count))
    own = lax.axis_index("gx")
    n_blocks = owner_ref.shape[-1]
    square = (n_blocks, n_blocks)
    block, other = sublane(square), lane(square)

    def spread(ref):
        by_lane = jnp.broadcast_to(ref[0], square)
        here = jnp.where(block == other, by_lane, 0).astype(f32)
        return by_lane, jnp.sum(here, axis=1, keepdims=True).astype(jnp.int32)

    def group_of(owner):
        if count == window:
            return lax.bitwise_xor(owner, own)
        turn = lax.rem(owner - own + count, count)
        if n_sets == count:
            return turn
        return jnp.where(turn < window, turn, turn - (count - n_sets))

    owner_by_lane, owner = spread(owner_ref)
    slot = spread(slot_ref)[1]
    group = group_of(owner)
    before = (group_of(owner_by_lane) == group) & (other < block)
    taken = jnp.sum(before.astype(f32), axis=1, keepdims=True).astype(jnp.int32)
    wide = (n_blocks, 128)
    place = jnp.broadcast_to(group * window + taken, wide)
    column = lane((8, 128))
    quarter = column // 32
    for s in range((n_sets + 3) // 4):
        here = place - 16 * s == lane(wide) // 8
        label = jnp.sum(jnp.where(here, (slot + 1).astype(f32), 0.0), axis=0, keepdims=True) - 1.0
        source = jnp.sum(
            jnp.where(here, (8 * sublane(wide)).astype(f32), 0.0), axis=0, keepdims=True
        )
        labels = jnp.broadcast_to(label, (8, 128))
        order = jnp.broadcast_to(source, (8, 128)).astype(jnp.int32) + lax.rem(column, 8)
        for t in range(4):
            order_ref[4 * s + t] = rolled(order, 32 * t, 1)
        for r in range(min(4, n_sets - 4 * s)):
            marks = labels
            for t in range(1, 4):
                marks = jnp.where(quarter == (r + t) % 4, rolled(labels, 32 * t, 1), marks)
            marks_ref[4 * s + r] = marks
    proj = proj_ref[...]
    for a in range(8):
        along_y = jnp.broadcast_to(proj[:, a : a + 1], (8, 128))
        along_y_ref[a] = along_y
        for i in range(8):
            along_x_ref[8 * i + a] = jnp.broadcast_to(along_y[i : i + 1], (8, 128))
    tile = tile_rows(proj)
    high = tile.astype(jnp.bfloat16).astype(f32)
    tile_ref[0] = high
    tile_ref[1] = tile - high


def speeds(state):
    inverse = 1.0 / (state[0] + 1.0)
    return [state[c] * inverse for c in (1, 2, 3)]


def vorticity_kernel(les_ref, velocity_ref, vort_ref):
    velocity = speeds([les_ref[c] for c in range(4)])

    def slope(c, axis):
        return shifted(velocity[c], axis, 1) - shifted(velocity[c], axis, -1)

    vort = [slope(2, 1) - slope(1, 2), slope(0, 2) - slope(2, 0), slope(1, 0) - slope(0, 1)]
    for c in range(3):
        velocity_ref[c] = velocity[c]
        vort_ref[c] = vort[c]


def vorticity_z_kernel(counts, present, vort_ref, *refs):
    refs = list(refs)
    face_refs = [refs.pop(0) if here else None for here in present]
    (out_ref,) = refs
    before, after = [speeds(layer) for layer in load_faces(face_refs, counts, 0, 4, (2,))[2]]
    for c, layer in ((0, (before[1], -after[1])), (1, (-before[0], after[0]))):
        for x, plane in enumerate(with_layers(vort_ref[c], (None, None, layer))):
            out_ref[c, x] = plane
    out_ref[2] = vort_ref[2]


def lamb_kernel(
    counts, n_faces, order_ref, marks_ref, along_x_ref, along_y_ref, velocity_ref, vort_ref, *refs
):
    face_refs, out_refs = refs[:n_faces], refs[n_faces:]
    outer = [
        halo and (speeds(halo[0]), speeds(halo[1]))
        for halo in load_faces(face_refs, counts, 0, 4, (0, 1))
    ]

    def rise(c, axis):
        return -outer[axis][0][c], outer[axis][1][c]

    def fall(c, axis):
        return outer[axis][0][c], -outer[axis][1][c]

    layers = [
        (None, rise(2, 1), None),
        (fall(2, 0), None, None),
        (rise(1, 0), fall(0, 1), None),
    ]
    vort = [0.5 * jnp.stack(with_layers(vort_ref[c], layers[c]), axis=0) for c in range(3)]
    velocity = read_all(velocity_ref)
    lamb = [
        vort[1] * velocity[2] - vort[2] * velocity[1],
        vort[2] * velocity[0] - vort[0] * velocity[2],
        vort[0] * velocity[1] - vort[1] * velocity[0],
    ]
    blocks = []
    for field in lamb:
        along_y = along_y_ref[0][None] * field[:, 0:1, :]
        for b in range(1, 8):
            along_y = along_y + along_y_ref[b][None] * field[:, b : b + 1, :]
        for i in range(8):
            plane = along_x_ref[8 * i] * along_y[0]
            for a in range(1, 8):
                plane = plane + along_x_ref[8 * i + a] * along_y[a]
            blocks.append(plane)

    quarter = lane((8, 128)) // 32
    for s in range((len(out_refs) + 3) // 4):
        ordered = [
            jnp.take_along_axis(block, order_ref[4 * s + k % 4], axis=1)
            for k, block in enumerate(blocks)
        ]
        for r in range(min(4, len(out_refs) - 4 * s)):
            out = out_refs[4 * s + r]
            for q in range(6):
                packed = ordered[4 * q]
                for t in range(1, 4):
                    packed = jnp.where(quarter == (r + t) % 4, ordered[4 * q + t], packed)
                out[q] = packed
            out[6] = marks_ref[4 * s + r]


def first_kernel(
    counts, n_faces, deriv_ref, high_ref, low_ref, les_ref, wave_ref, mean_ref, *refs
):
    face_refs, (section_ref, rate_ref, mean_faces_ref), out_refs = (
        refs[:n_faces], refs[n_faces : n_faces + 3], refs[n_faces + 3 :],
    )
    for n, face in enumerate(mean_layers(read_all(mean_ref))):
        for c in range(3):
            mean_faces_ref[n, c] = face[c]
    state = read_all(les_ref)
    rate = les_rate(state, load_faces(face_refs, counts, 0, 5))
    section = [s + r for s, r in zip(state, rate)]
    for c in range(5):
        section_ref[c] = section[c]
    store_faces(section, out_refs, counts)
    rate = acoustic_rate(
        read_all(wave_ref), read_all(mean_ref), load_faces(face_refs, counts, 5, 9),
        deriv_ref[...], (high_ref[...], low_ref[...]),
    )
    for c in range(4):
        rate_ref[c] = rate[c]


def source_kernel(counts, n_faces, tile_ref, wave_ref, rate_ref, *refs):
    n_pieces = len(partners(counts[0]))
    pieces = [None] * n_pieces
    for ref, k in zip(refs, sending_sets(n_pieces)):
        pieces[k] = ref
    refs = refs[n_pieces:]
    section_faces, (source_ref, middle_ref, carry_ref), face_refs = (
        refs[:n_faces], refs[n_faces : n_faces + 3], refs[n_faces + 3 :],
    )
    quarter = lane((8, 128)) // 32
    tile_high, tile_low = tile_ref[0], tile_ref[1]
    total = None
    for s in range((n_pieces + 3) // 4):
        count = min(4, n_pieces - 4 * s)

        def gathered(q, t):
            value = jnp.full((8, 128), -1.0 if q == 6 else 0.0, f32)
            for r in range(count):
                value = jnp.where(quarter == (r + t) % 4, pieces[4 * s + r][q], value)
            return value

        here = [gathered(6, 0).astype(jnp.int32) == slot for slot in range(16)]
        chosen_high, chosen_low = [
            jnp.concatenate([jnp.where(h, part, 0.0) for h in here], axis=0).astype(jnp.bfloat16)
            for part in (tile_high, tile_low)
        ]
        data = []
        for k in range(24):
            piece = gathered(k // 4, k % 4)
            data.append(pltpu.roll(piece, 128 - 32 * (k % 4), 1) if k % 4 else piece)
        data = jnp.concatenate(data, axis=0)
        high = data.astype(jnp.bfloat16)
        low = (data - high.astype(f32)).astype(jnp.bfloat16)
        dot = functools.partial(
            lax.dot_general,
            dimension_numbers=(((1,), (1,)), ((), ())),
            preferred_element_type=f32,
        )
        moved = dot(high, chosen_high) + (dot(low, chosen_high) + dot(high, chosen_low))
        total = moved if total is None else total + moved
    source = [total[64 * c : 64 * c + 64].reshape(8, 8, 128) for c in range(3)]
    middle = []
    for c in range(4):
        rate = rate_ref[c]
        if c:
            source_ref[c - 1] = source[c - 1]
            rate = rate + source[c - 1]
        middle.append(wave_ref[c] + acoustic_step * rate)
        middle_ref[c] = middle[c]
        carry = wave_ref[c] + middle[c]
        carry_ref[c] = carry + acoustic_step * source[c - 1] if c else carry
    for ready, face in zip(section_faces, face_refs):
        face[0:5] = ready[...]
    store_faces(middle, [face.at[5:9] for face in face_refs], counts)


def inner_kernel(
    deriv_ref, high_ref, low_ref, les_ref, section_ref, middle_ref, carry_ref, mean_ref, source_ref,
    les_base_ref, wave_base_ref, source_out, sem,
):
    copy = pltpu.make_async_copy(source_ref, source_out, sem)
    copy.start()
    section = read_all(section_ref)
    rate = les_rate(section, None)
    for c in range(5):
        les_base_ref[c] = 0.5 * ((les_ref[c] + section[c]) + rate[c])
    rate = acoustic_rate(
        read_all(middle_ref), read_all(mean_ref), None,
        deriv_ref[...], (high_ref[...], low_ref[...]),
    )
    for c in range(4):
        wave_base_ref[c] = 0.5 * (carry_ref[c] + acoustic_step * rate[c])
    copy.wait()


def add_layers(counts, chosen, face_refs, mean_faces_ref, les_base_ref, wave_base_ref, put):
    layers = les_outer(load_faces(face_refs, counts, 0, 5, chosen))
    for c in range(5):
        part = [layer and (0.5 * layer[0][c], 0.5 * layer[1][c]) for layer in layers]
        put(c, with_layers(les_base_ref[c], part))
    mean_faces = [[mean_faces_ref[n, c] for c in range(3)] for n in range(6)]
    layers = acoustic_outer(mean_faces, load_faces(face_refs, counts, 5, 9, chosen))
    step = 0.5 * acoustic_step
    for c in range(4):
        part = [layer and (step * layer[0][c], step * layer[1][c]) for layer in layers]
        put(5 + c, with_layers(wave_base_ref[c], part))


def z_faces(faces, counts):
    holds = [any(axis == 2 for axis, _ in pair) for pair in slots(counts)]
    return [face if hold else None for face, hold in zip(faces, holds)]


def z_kernel(counts, present, les_base_ref, wave_base_ref, mean_faces_ref, *refs):
    refs = list(refs)
    face_refs = [refs.pop(0) if here else None for here in present]
    les_ref, wave_ref = refs

    def put(c, planes):
        for x, plane in enumerate(planes):
            if c < 5:
                les_ref[c, x] = plane
            else:
                wave_ref[c - 5, x] = plane

    add_layers(counts, (2,), face_refs, mean_faces_ref, les_base_ref, wave_base_ref, put)


def last_kernel(counts, n_faces, les_base_ref, wave_base_ref, mean_faces_ref, *refs):
    face_refs, (les_out, wave_out, les_ref, wave_ref, sems) = (
        refs[:n_faces], refs[n_faces:],
    )
    copies = []

    def put(c, planes):
        kept, target = (les_ref.at[c], les_out.at[c]) if c < 5 else (
            wave_ref.at[c - 5], wave_out.at[c - 5]
        )
        for x, plane in enumerate(planes):
            kept[x] = plane
        copies.append(pltpu.make_async_copy(kept, target, sems.at[c]))
        copies[-1].start()

    add_layers(counts, (0, 1), face_refs, mean_faces_ref, les_base_ref, wave_base_ref, put)
    for copy in copies:
        copy.wait()


VMEM = pl.BlockSpec(memory_space=pltpu.VMEM)


HBM = pl.BlockSpec(memory_space=pltpu.HBM)


def call(kernel, in_specs, out_shapes, name, cost, scratch=(), out_spec=None):
    return pl.pallas_call(
        kernel,
        in_specs=in_specs,
        out_specs=out_spec or [VMEM] * len(out_shapes),
        out_shape=out_shapes,
        scratch_shapes=list(scratch),
        name=name,
        cost_estimate=pl.CostEstimate(flops=cost, bytes_accessed=800000, transcendentals=0),
        compiler_params=pltpu.CompilerParams(vmem_limit_bytes=24 * 1024 * 1024),
    )


def local(counts, les, wave, mean, projection, owner, slot):
    shape = les.shape[1:]
    faces = face_shapes(counts, 9)
    n_faces = len(faces)
    like = lambda n: jax.ShapeDtypeStruct((n,) + shape, f32)

    table = derivative_matrix()
    deriv = jnp.asarray(table, f32)
    along_z = np.kron(np.eye(16), table.T).astype(np.float32)
    high = along_z.astype(jnp.bfloat16)
    low = (along_z - high.astype(np.float32)).astype(jnp.bfloat16)
    tables = (deriv, jnp.asarray(high), jnp.asarray(low))

    arguments = (les, wave, owner, slot, projection)
    les, wave, owner, slot, projection, *sent = call(
        functools.partial(load_kernel, counts),
        [HBM] * 5,
        [jax.ShapeDtypeStruct(a.shape, a.dtype) for a in arguments] + faces,
        "load_and_faces",
        100000,
        [pltpu.SemaphoreType.DMA((5,))],
    )(*(pltpu.with_memory_space_constraint(a, pltpu.HBM) for a in arguments))
    got = exchange(sent, counts)

    sets = partners(counts[0])
    n_plans = 4 * ((len(sets) + 3) // 4)
    order, marks, along_x, along_y, tile = call(
        functools.partial(plan_kernel, counts),
        [VMEM] * 3,
        [
            jax.ShapeDtypeStruct((n_plans, 8, 128), jnp.int32),
            jax.ShapeDtypeStruct((len(sets), 8, 128), f32),
            jax.ShapeDtypeStruct((64, 8, 128), f32),
            jax.ShapeDtypeStruct((8, 8, 128), f32),
            jax.ShapeDtypeStruct((2, 8, 128), f32),
        ],
        "plan",
        1000000,
    )(owner, slot, projection)
    turning = list(call(vorticity_kernel, [VMEM], [like(3)] * 2, "vorticity", 1000000)(les))
    z_got = z_faces(got, counts)
    present = [face is not None for face in z_got]
    turning[1] = call(
        functools.partial(vorticity_z_kernel, counts, present),
        [VMEM] * (1 + sum(present)),
        [like(3)],
        "vorticity_z",
        1000000,
    )(turning[1], *(face for face in z_got if face is not None))[0]
    pieces = call(
        functools.partial(lamb_kernel, counts, n_faces),
        [VMEM] * (6 + n_faces),
        [jax.ShapeDtypeStruct((7, 8, 128), f32)] * len(sets),
        "lamb_blocks",
        10000000,
    )(order, marks, along_x, along_y, *turning, *got)
    moved = []
    for k in sending_sets(len(sets)):
        still = all(i == j for i, j in sets[k])
        moved.append(pieces[k] if still else lax.ppermute(pieces[k], "gx", sets[k]))
    section, rate, mean_faces, *section_faces = call(
        functools.partial(first_kernel, counts, n_faces),
        [VMEM] * (6 + n_faces),
        [like(5), like(4), jax.ShapeDtypeStruct((6, 3, 8, 128), f32)] + face_shapes(counts, 5),
        "first_rates",
        40000000,
    )(*tables, les, wave, mean, *got)

    source, middle, carry, *sent = call(
        functools.partial(source_kernel, counts, n_faces),
        [VMEM] * (3 + len(moved) + n_faces),
        [like(3), like(4), like(4)] + faces,
        "source_and_faces",
        10000000,
    )(tile, wave, rate, *moved, *section_faces)
    got = exchange(sent, counts)
    les_base, wave_base, source_out = call(
        inner_kernel,
        [VMEM] * 9,
        [like(5), like(4), like(3)],
        "second_rates_inner",
        40000000,
        [pltpu.SemaphoreType.DMA],
        out_spec=[VMEM, VMEM, HBM],
    )(*tables, les, section, middle, carry, mean, source)
    z_got = z_faces(got, counts)
    present = [face is not None for face in z_got]
    les_base, wave_base = call(
        functools.partial(z_kernel, counts, present),
        [VMEM] * (3 + sum(present)),
        [like(5), like(4)],
        "second_rates_z",
        1000000,
    )(les_base, wave_base, mean_faces, *(face for face in z_got if face is not None))
    les_next, wave_next = call(
        functools.partial(last_kernel, counts, n_faces),
        [VMEM] * (3 + n_faces),
        [like(5), like(4)],
        "second_rates_outer",
        4000000,
        [
            pltpu.VMEM(les.shape, f32),
            pltpu.VMEM(wave.shape, f32),
            pltpu.SemaphoreType.DMA((9,)),
        ],
        out_spec=[HBM, HBM],
    )(les_base, wave_base, mean_faces, *got)
    return les_next, source_out, wave_next


def solution(mesh):
    counts = tuple(mesh.shape[axis] for axis in axes)
    field = P(None, *axes)
    return jax.shard_map(
        functools.partial(local, counts),
        mesh=mesh,
        in_specs=(field, field, field, P(), P(*axes), P(*axes)),
        out_specs=(field, field, field),
        check_vma=False,
    )
```

profile of v0, /device:TPU:0, one launch (start us, length us, event | category | flops | bytes accessed | tf_op | source)
XLA Modules:
  0.0 20.2 jit_solution(3198973877078351462)
XLA Ops:
  0.6 1.2 %load_and_faces.1 = (f32[5,8,8,128]{3,2,1,0:T(8,128)S(1)}, f32[4,8,8,128]{3,2,1,0:T(8,128)S(1)}, s32[1,1,16]{2,1,0:T(1,128)S(1)}, s32[1,1,16]{2,1,0:T(1,128)S(1)...) custom-call(f32[5,8,8,128]{3,2,1,0:T(8,128)} %refs_0_.1, ...), custom_call_target="tpu_custom_call" | custom-call | flops 100000 | bytes 800000 | tf_op jit(solution)/shard_map/load_and_faces/pallas_call | solution.py:744
  1.8 3.0 %collective-permute-start = (f32[9,8,128]{2,1,0:T(8,128)S(1)}, f32[9,8,128]{2,1,0:T(8,128)S(1)}, u32[]{:S(2)}, u32[]{:S(2)}) collective-permute-start(f32[9,8,128]{2,1,0:T(8,128)S(1)} %get-tuple-element.49), channel_id=1, source_target_pairs={{0,1},{1,0},{2,3},{3,2},{4,28},{5,29},{6,30},{7,31},{8,9},{9,8},{1... | collective-permute-start | bytes 110600 | tf_op jit(solution)/shard_map/ppermute | solution.py:385
  4.8 0.7 %collective-permute-start.1 = (f32[9,8,128]{2,1,0:T(8,128)S(1)}, f32[9,8,128]{2,1,0:T(8,128)S(1)}, u32[]{:S(2)}, u32[]{:S(2)}) collective-permute-start(f32[9,8,128]{2,1,0:T(8,128)S(1)} %get-tuple-element.50), channel_id=1, source_target_pairs={{0,24},{1,25},{2,26},{3,27},{4,5},{5,4},{6,7},{7,6},{8,16},{9,17},... | collective-permute-start | bytes 110600 | tf_op jit(solution)/shard_map/ppermute | solution.py:385
  5.5 1.6 %collective-permute-start.2 = (f32[9,8,128]{2,1,0:T(8,128)S(1)}, f32[9,8,128]{2,1,0:T(8,128)S(1)}, u32[]{:S(2)}, u32[]{:S(2)}) collective-permute-start(f32[9,8,128]{2,1,0:T(8,128)S(1)} %get-tuple-element.51), channel_id=1, source_target_pairs={{0,2},{1,3},{2,0},{3,1},{4,12},{5,13},{6,14},{7,15},{8,10},{9,11},... | collective-permute-start | bytes 110600 | tf_op jit(solution)/shard_map/ppermute | solution.py:385
  7.1 0.7 %collective-permute-start.3 = (f32[9,8,128]{2,1,0:T(8,128)S(1)}, f32[9,8,128]{2,1,0:T(8,128)S(1)}, u32[]{:S(2)}, u32[]{:S(2)}) collective-permute-start(f32[9,8,128]{2,1,0:T(8,128)S(1)} %get-tuple-element.52), channel_id=1, source_target_pairs={{0,8},{1,9},{2,4},{3,5},{4,2},{5,3},{6,14},{7,15},{8,0},{9,1},{10,... | collective-permute-start | bytes 110600 | tf_op jit(solution)/shard_map/ppermute | solution.py:385
  7.8 0.1 vorticity.1
  7.9 0.3 %plan.1 = (s32[4,8,128]{2,1,0:T(8,128)S(1)}, f32[4,8,128]{2,1,0:T(8,128)S(1)}, f32[64,8,128]{2,1,0:T(8,128)S(1)}, f32[8,8,128]{2,1,0:T(8,128)S(1)}, f32[2,8,128]{2,1,0:T(8,128)S(1)}) custom-call(s32[1,1,16]{2,1,0:T(1,128)S(1)} %get-tuple-element.55.owner_ref, s32[1,1,16]{2,1,0:T(1,128)S(1)} %get-tuple-element.56.slot_ref, f32[8,8]{1,0:T(8,128)S(1)} %get-tuple-element.57.proj_ref), custom_call_target="tpu_custom_call" | custom-call | flops 1000000 | bytes 800000 | tf_op jit(solution)/shard_map/plan/pallas_call | solution.py:756
  8.2 0.0 collective-permute-done.refs_0_
  8.2 0.3 %collective-permute-done.1.refs_1_ = f32[9,8,128]{2,1,0:T(8,128)S(1)} collective-permute-done((f32[9,8,128]{2,1,0:T(8,128)S(1)}, f32[9,8,128]{2,1,0:T(8,128)S(1)}, u32[]{:S(2)}, u32[]{:S(2)}) %collective-permute-start.1) | collective-permute-done | bytes 36896 | tf_op jit(solution)/shard_map/ppermute | solution.py:385
  8.5 0.2 vorticity_z.1.vort_ref
  8.7 1.1 %collective-permute-done.2.refs_2_ = f32[9,8,128]{2,1,0:T(8,128)S(1)} collective-permute-done((f32[9,8,128]{2,1,0:T(8,128)S(1)}, f32[9,8,128]{2,1,0:T(8,128)S(1)}, u32[]{:S(2)}, u32[]{:S(2)}) %collective-permute-start.2) | collective-permute-done | bytes 36896 | tf_op jit(solution)/shard_map/ppermute | solution.py:385
  9.9 0.0 collective-permute-done.4.refs_4_
  9.9 0.0 copy-start.1
  9.9 0.0 copy-start.2
  9.9 0.3 %lamb_blocks.1 = (f32[7,8,128]{2,1,0:T(8,128)S(1)}, f32[7,8,128]{2,1,0:T(8,128)S(1)}, f32[7,8,128]{2,1,0:T(8,128)S(1)}, f32[7,8,128]{2,1,0:T(8,128)S(1)}) custom-call(s32[4,8,128]{2,1,0:T(8,128)S(1)} %get-tuple-element.60.order_ref, f32[4,8,128]{2,1,0:T(8,128)S(1)} %get-tuple-element.61.marks_ref, f32[64,8,128]{2,1,0:T(8,128)S(1)} %get-tuple-element.62.along_x_ref, ...), custom_call_target="tpu_custom_call" | custom-call | flops 10000000 | bytes 800000 | tf_op jit(solution)/shard_map/lamb_blocks/pallas_call | solution.py:779
  10.1 0.0 copy-start.3
  10.2 0.1 collective-permute-start.5
  10.2 1.7 %collective-permute-start.6 = (f32[7,8,128]{2,1,0:T(8,128)S(1)}, f32[7,8,128]{2,1,0:T(8,128)S(1)}, u32[]{:S(2)}, u32[]{:S(2)}) collective-permute-start(f32[7,8,128]{2,1,0:T(8,128)S(1)} %get-tuple-element.67), channel_id=1, source_target_pairs={{0,16},{8,24},{16,0},{24,8},{1,17},{9,25},{17,1},{25,9},{2,18},{10... | collective-permute-start | bytes 86024 | tf_op jit(solution)/shard_map/ppermute | solution.py:789
  12.0 0.1 collective-permute-start.7
  12.1 0.7 %first_rates.1 = (f32[5,8,8,128]{3,2,1,0:T(8,128)S(1)}, f32[4,8,8,128]{3,2,1,0:T(8,128)S(1)}, f32[6,3,8,128]{3,2,1,0:T(8,128)S(1)}, f32[5,8,128]{2,1,0:T(8,128)S...) custom-call(f32[8,8]{1,0:T(8,128)S(1)} %copy-done.3, ...), custom_call_target="tpu_custom_call" | custom-call | flops 40000000 | bytes 800000 | tf_op jit(solution)/shard_map/first_rates/pallas_call | solution.py:790
  12.8 0.7 %collective-permute-done.5.refs_0_ = f32[7,8,128]{2,1,0:T(8,128)S(1)} collective-permute-done((f32[7,8,128]{2,1,0:T(8,128)S(1)}, f32[7,8,128]{2,1,0:T(8,128)S(1)}, u32[]{:S(2)}, u32[]{:S(2)}) %collective-permute-start.5) | collective-permute-done | bytes 28704 | tf_op jit(solution)/shard_map/ppermute | solution.py:789
  13.5 0.9 %collective-permute-done.6.refs_1_ = f32[7,8,128]{2,1,0:T(8,128)S(1)} collective-permute-done((f32[7,8,128]{2,1,0:T(8,128)S(1)}, f32[7,8,128]{2,1,0:T(8,128)S(1)}, u32[]{:S(2)}, u32[]{:S(2)}) %collective-permute-start.6) | collective-permute-done | bytes 28704 | tf_op jit(solution)/shard_map/ppermute | solution.py:789
  14.4 0.4 %source_and_faces.1 = (f32[3,8,8,128]{3,2,1,0:T(8,128)S(1)}, f32[4,8,8,128]{3,2,1,0:T(8,128)S(1)}, f32[4,8,8,128]{3,2,1,0:T(8,128)S(1)}, f32[9,8,128]{2,1,0:T(8,...) custom-call(f32[2,8,128]{2,1,0:T(8,128)S(1)} %get-tuple-element.58.t, ...), custom_call_target="tpu_custom_call" | custom-call | flops 10000000 | bytes 800000 | tf_op jit(solution)/shard_map/source_and_faces/pallas_call | solution.py:798
  14.8 0.6 %collective-permute-start.8 = (f32[9,8,128]{2,1,0:T(8,128)S(1)}, f32[9,8,128]{2,1,0:T(8,128)S(1)}, u32[]{:S(2)}, u32[]{:S(2)}) collective-permute-start(f32[9,8,128]{2,1,0:T(8,128)S(1)} %get-tuple-element.81), channel_id=1, source_target_pairs={{0,1},{1,0},{2,3},{3,2},{4,28},{5,29},{6,30},{7,31},{8,9},{9,8},{1... | collective-permute-start | bytes 110600 | tf_op jit(solution)/shard_map/ppermute | solution.py:385
  15.4 1.7 %collective-permute-start.10 = (f32[9,8,128]{2,1,0:T(8,128)S(1)}, f32[9,8,128]{2,1,0:T(8,128)S(1)}, u32[]{:S(2)}, u32[]{:S(2)}) collective-permute-start(f32[9,8,128]{2,1,0:T(8,128)S(1)} %get-tuple-element.85), channel_id=1, source_target_pairs={{0,2},{1,3},{2,0},{3,1},{4,12},{5,13},{6,14},{7,15},{8,10},{9,11},... | collective-permute-start | bytes 110600 | tf_op jit(solution)/shard_map/ppermute | solution.py:385
  17.1 1.1 %collective-permute-start.11 = (f32[9,8,128]{2,1,0:T(8,128)S(1)}, f32[9,8,128]{2,1,0:T(8,128)S(1)}, u32[]{:S(2)}, u32[]{:S(2)}) collective-permute-start(f32[9,8,128]{2,1,0:T(8,128)S(1)} %get-tuple-element.86), channel_id=1, source_target_pairs={{0,8},{1,9},{2,4},{3,5},{4,2},{5,3},{6,14},{7,15},{8,0},{9,1},{10,... | collective-permute-start | bytes 110600 | tf_op jit(solution)/shard_map/ppermute | solution.py:385
  18.2 0.6 %second_rates_inner.1 = (f32[5,8,8,128]{3,2,1,0:T(8,128)S(1)}, f32[4,8,8,128]{3,2,1,0:T(8,128)S(1)}, f32[3,8,8,128]{3,2,1,0:T(8,128)}) custom-call(f32[8,8]{1,0:T(8,128)S(1)} %copy-done.3, bf16[128,128]{1,0:T(8,128)(2,1)S(1)} %copy-done.2, bf16[128,128]{1,0:T(8,128)(2,1)S(1)} %copy-done.1, f32[5,8,8,128]{3,2,1,0:T(8,128)S(1)} %get-tuple-element.47.les_ref, ...), custom_call_target="tpu_custom_call" | custom-call | flops 40000000 | bytes 800000 | tf_op jit(solution)/shard_map/second_rates_inner/pallas_call | solution.py:806
  18.9 0.2 %collective-permute-done.9.refs_1_ = f32[9,8,128]{2,1,0:T(8,128)S(1)} collective-permute-done((f32[9,8,128]{2,1,0:T(8,128)S(1)}, f32[9,8,128]{2,1,0:T(8,128)S(1)}, u32[]{:S(2)}, u32[]{:S(2)}) %collective-permute-start.9) | collective-permute-done | bytes 36896 | tf_op jit(solution)/shard_map/ppermute | solution.py:385
  19.1 0.2 %second_rates_z.1 = (f32[5,8,8,128]{3,2,1,0:T(8,128)S(1)}, f32[4,8,8,128]{3,2,1,0:T(8,128)S(1)}) custom-call(f32[5,8,8,128]{3,2,1,0:T(8,128)S(1)} %get-tuple-element.78.les_base_ref, f32[4,8,8,128]{3,2,1,0:T(8,128)S(1)} %get-tuple-element.79.wave_base_ref, f32[6,3,8,128]{3,2,1,0:T(8,128)S(1)} %get-tuple-element.80.mean_faces_ref, ...), custom_call_target="tpu_custom_call" | custom-call | flops 1000000 | bytes 800000 | tf_op jit(solution)/shard_map/second_rates_z/pallas_call | solution.py:817
  19.3 0.0 collective-permute-done.10.refs_2_
  19.4 0.0 collective-permute-done.12.refs_4_
  19.4 0.8 %second_rates_outer.1 = (f32[5,8,8,128]{3,2,1,0:T(8,128)}, f32[4,8,8,128]{3,2,1,0:T(8,128)}) custom-call(f32[5,8,8,128]{3,2,1,0:T(8,128)S(1)} %get-tuple-element.83.les_base_ref, f32[4,8,8,128]{3,2,1,0:T(8,128)S(1)} %get-tuple-element.84.wave_base_ref, f32[6,3,8,128]{3,2,1,0:T(8,128)S(1)} %get-tuple-element.80.mean_faces_ref, ...), custom_call_target="tpu_custom_call" | custom-call | flops 4000000 | bytes 800000 | tf_op jit(solution)/shard_map/second_rates_outer/pallas_call | solution.py:824
  (12 shorter events, 0.0 us)
Async XLA Ops:
  1.8 6.4 %collective-permute-start = (f32[9,8,128]{2,1,0:T(8,128)S(1)}, f32[9,8,128]{2,1,0:T(8,128)S(1)}, u32[]{:S(2)}, u32[]{:S(2)}) collective-permute-start(f32[9,8,128]{2,1,0:T(8,128)S(1)} %get-tuple-element.49), channel_id=1, source_target_pairs={{0,1},{1,0},{2,3},{3,2},{4,28},{5,29},{6,30},{7,31},{8,9},{9,8},{1... | collective-permute-start | bytes 110600 | tf_op jit(solution)/shard_map/ppermute | solution.py:385
  4.8 3.7 %collective-permute-start.1 = (f32[9,8,128]{2,1,0:T(8,128)S(1)}, f32[9,8,128]{2,1,0:T(8,128)S(1)}, u32[]{:S(2)}, u32[]{:S(2)}) collective-permute-start(f32[9,8,128]{2,1,0:T(8,128)S(1)} %get-tuple-element.50), channel_id=1, source_target_pairs={{0,24},{1,25},{2,26},{3,27},{4,5},{5,4},{6,7},{7,6},{8,16},{9,17},... | collective-permute-start | bytes 110600 | tf_op jit(solution)/shard_map/ppermute | solution.py:385
  5.5 4.3 %collective-permute-start.2 = (f32[9,8,128]{2,1,0:T(8,128)S(1)}, f32[9,8,128]{2,1,0:T(8,128)S(1)}, u32[]{:S(2)}, u32[]{:S(2)}) collective-permute-start(f32[9,8,128]{2,1,0:T(8,128)S(1)} %get-tuple-element.51), channel_id=1, source_target_pairs={{0,2},{1,3},{2,0},{3,1},{4,12},{5,13},{6,14},{7,15},{8,10},{9,11},... | collective-permute-start | bytes 110600 | tf_op jit(solution)/shard_map/ppermute | solution.py:385
  7.1 2.8 %collective-permute-start.3 = (f32[9,8,128]{2,1,0:T(8,128)S(1)}, f32[9,8,128]{2,1,0:T(8,128)S(1)}, u32[]{:S(2)}, u32[]{:S(2)}) collective-permute-start(f32[9,8,128]{2,1,0:T(8,128)S(1)} %get-tuple-element.52), channel_id=1, source_target_pairs={{0,8},{1,9},{2,4},{3,5},{4,2},{5,3},{6,14},{7,15},{8,0},{9,1},{10,... | collective-permute-start | bytes 110600 | tf_op jit(solution)/shard_map/ppermute | solution.py:385
  7.8 2.1 %collective-permute-start.4 = (f32[9,8,128]{2,1,0:T(8,128)S(1)}, f32[9,8,128]{2,1,0:T(8,128)S(1)}, u32[]{:S(2)}, u32[]{:S(2)}) collective-permute-start(f32[9,8,128]{2,1,0:T(8,128)S(1)} %get-tuple-element.53), channel_id=1, source_target_pairs={{0,8},{1,9},{2,10},{3,11},{4,6},{5,7},{6,4},{7,5},{8,0},{9,1},{10,... | collective-permute-start | bytes 110600 | tf_op jit(solution)/shard_map/ppermute | solution.py:385
  9.9 2.2 %copy-start = (f32[3,8,8,128]{3,2,1,0:T(8,128)S(1)}, f32[3,8,8,128]{3,2,1,0:T(8,128)}, u32[]{:S(2)}) copy-start(f32[3,8,8,128]{3,2,1,0:T(8,128)} %mean_ref.3) | copy-start | bytes 294916
  9.9 2.2 %copy-start.1 = (bf16[128,128]{1,0:T(8,128)(2,1)S(1)}, bf16[128,128]{1,0:T(8,128)(2,1)}, u32[]{:S(2)}) copy-start(bf16[128,128]{1,0:T(8,128)(2,1)} %constant.8.clone.low_ref) | copy-start | bytes 98308
  9.9 2.2 %copy-start.2 = (bf16[128,128]{1,0:T(8,128)(2,1)S(1)}, bf16[128,128]{1,0:T(8,128)(2,1)}, u32[]{:S(2)}) copy-start(bf16[128,128]{1,0:T(8,128)(2,1)} %constant.7.clone.high_ref) | copy-start | bytes 98308
  10.1 2.0 %copy-start.3 = (f32[8,8]{1,0:T(8,128)S(1)}, f32[8,8]{1,0:T(8,128)}, u32[]{:S(2)}) copy-start(f32[8,8]{1,0:T(8,128)} %constant.6.clone.deriv_ref) | copy-start | bytes 772
  10.2 3.4 %collective-permute-start.5 = (f32[7,8,128]{2,1,0:T(8,128)S(1)}, f32[7,8,128]{2,1,0:T(8,128)S(1)}, u32[]{:S(2)}, u32[]{:S(2)}) collective-permute-start(f32[7,8,128]{2,1,0:T(8,128)S(1)} %get-tuple-element.66), channel_id=1, source_target_pairs={{0,24},{8,16},{16,8},{24,0},{1,25},{9,17},{17,9},{25,1},{2,26},{10... | collective-permute-start | bytes 86024 | tf_op jit(solution)/shard_map/ppermute | solution.py:789
  10.2 4.2 %collective-permute-start.6 = (f32[7,8,128]{2,1,0:T(8,128)S(1)}, f32[7,8,128]{2,1,0:T(8,128)S(1)}, u32[]{:S(2)}, u32[]{:S(2)}) collective-permute-start(f32[7,8,128]{2,1,0:T(8,128)S(1)} %get-tuple-element.67), channel_id=1, source_target_pairs={{0,16},{8,24},{16,0},{24,8},{1,17},{9,25},{17,1},{25,9},{2,18},{10... | collective-permute-start | bytes 86024 | tf_op jit(solution)/shard_map/ppermute | solution.py:789
  12.0 2.5 %collective-permute-start.7 = (f32[7,8,128]{2,1,0:T(8,128)S(1)}, f32[7,8,128]{2,1,0:T(8,128)S(1)}, u32[]{:S(2)}, u32[]{:S(2)}) collective-permute-start(f32[7,8,128]{2,1,0:T(8,128)S(1)} %get-tuple-element.68), channel_id=1, source_target_pairs={{0,8},{8,0},{16,24},{24,16},{1,9},{9,1},{17,25},{25,17},{2,10},{10... | collective-permute-start | bytes 86024 | tf_op jit(solution)/shard_map/ppermute | solution.py:789
  14.8 4.1 %collective-permute-start.8 = (f32[9,8,128]{2,1,0:T(8,128)S(1)}, f32[9,8,128]{2,1,0:T(8,128)S(1)}, u32[]{:S(2)}, u32[]{:S(2)}) collective-permute-start(f32[9,8,128]{2,1,0:T(8,128)S(1)} %get-tuple-element.81), channel_id=1, source_target_pairs={{0,1},{1,0},{2,3},{3,2},{4,28},{5,29},{6,30},{7,31},{8,9},{9,8},{1... | collective-permute-start | bytes 110600 | tf_op jit(solution)/shard_map/ppermute | solution.py:385
  15.4 3.7 %collective-permute-start.9 = (f32[9,8,128]{2,1,0:T(8,128)S(1)}, f32[9,8,128]{2,1,0:T(8,128)S(1)}, u32[]{:S(2)}, u32[]{:S(2)}) collective-permute-start(f32[9,8,128]{2,1,0:T(8,128)S(1)} %get-tuple-element.82), channel_id=1, source_target_pairs={{0,24},{1,25},{2,26},{3,27},{4,5},{5,4},{6,7},{7,6},{8,16},{9,17},... | collective-permute-start | bytes 110600 | tf_op jit(solution)/shard_map/ppermute | solution.py:385
  15.4 4.0 %collective-permute-start.10 = (f32[9,8,128]{2,1,0:T(8,128)S(1)}, f32[9,8,128]{2,1,0:T(8,128)S(1)}, u32[]{:S(2)}, u32[]{:S(2)}) collective-permute-start(f32[9,8,128]{2,1,0:T(8,128)S(1)} %get-tuple-element.85), channel_id=1, source_target_pairs={{0,2},{1,3},{2,0},{3,1},{4,12},{5,13},{6,14},{7,15},{8,10},{9,11},... | collective-permute-start | bytes 110600 | tf_op jit(solution)/shard_map/ppermute | solution.py:385
  17.1 2.2 %collective-permute-start.11 = (f32[9,8,128]{2,1,0:T(8,128)S(1)}, f32[9,8,128]{2,1,0:T(8,128)S(1)}, u32[]{:S(2)}, u32[]{:S(2)}) collective-permute-start(f32[9,8,128]{2,1,0:T(8,128)S(1)} %get-tuple-element.86), channel_id=1, source_target_pairs={{0,8},{1,9},{2,4},{3,5},{4,2},{5,3},{6,14},{7,15},{8,0},{9,1},{10,... | collective-permute-start | bytes 110600 | tf_op jit(solution)/shard_map/ppermute | solution.py:385
  18.2 1.2 %collective-permute-start.12 = (f32[9,8,128]{2,1,0:T(8,128)S(1)}, f32[9,8,128]{2,1,0:T(8,128)S(1)}, u32[]{:S(2)}, u32[]{:S(2)}) collective-permute-start(f32[9,8,128]{2,1,0:T(8,128)S(1)} %get-tuple-element.87), channel_id=1, source_target_pairs={{0,8},{1,9},{2,10},{3,11},{4,6},{5,7},{6,4},{7,5},{8,0},{9,1},{10,... | collective-permute-start | bytes 110600 | tf_op jit(solution)/shard_map/ppermute | solution.py:385
where the time goes:
time: 20.4 us; the launch traced here: 20.2 us
  starting transfers between devices  11.3 us (55%)
  Pallas kernels  4.77 us (23%)
  waiting for transfers between devices  3.43 us (17%)
  between operations  0.75 us (4%)
    ppermute x10, starting transfers between devices, exchange(): lax.ppermute(face, axes, way)  9.34 us
    ppermute x3, starting transfers between devices, local(): moved.append(pieces[k] if still else lax.ppermute(pieces[k], 'gx', sets[k]))  1.94 us
    ppermute x10, waiting for transfers between devices, exchange(): lax.ppermute(face, axes, way)  1.81 us
    ppermute x3, waiting for transfers between devices, local(): moved.append(pieces[k] if still else lax.ppermute(pieces[k], 'gx', sets[k]))  1.62 us
    pallas_call x1, Pallas kernels, local(): call(functools.partial(load_kernel, counts), [HBM] * 5, [jax.ShapeDtypeSt...  1.19 us
    pallas_call x1, Pallas kernels, local(): call(functools.partial(last_kernel, counts, n_faces), [VMEM] * (3 + n_fac...  0.82 us
    pallas_call x1, Pallas kernels, local(): call(functools.partial(first_kernel, counts, n_faces), [VMEM] * (6 + n_fa...  0.7 us
    pallas_call x1, Pallas kernels, local(): call(inner_kernel, [VMEM] * 9, [like(5), like(4), like(3)], 'second_rates...  0.65 us
  transfers between devices with their start and end apart: 13, of which 5 were waited for; matrix products, arithmetic and copies ran while one was open for 0% of the time, Pallas kernels for 11%

commit v1 on v0

--- a/solution.py
+++ b/solution.py
@@ -571,13 +571,13 @@
     section = [s + r for s, r in zip(state, rate)]
     for c in range(5):
         section_ref[c] = section[c]
-    store_faces(section, out_refs, counts)
     rate = acoustic_rate(
         read_all(wave_ref), read_all(mean_ref), load_faces(face_refs, counts, 5, 9),
         deriv_ref[...], (high_ref[...], low_ref[...]),
     )
     for c in range(4):
         rate_ref[c] = rate[c]
+    store_faces(section + [wave_ref[0] + acoustic_step * rate[0]], out_refs, counts)
 
 
 def source_kernel(counts, n_faces, tile_ref, wave_ref, rate_ref, *refs):
@@ -586,9 +586,7 @@
     for ref, k in zip(refs, sending_sets(n_pieces)):
         pieces[k] = ref
     refs = refs[n_pieces:]
-    section_faces, (source_ref, middle_ref, carry_ref), face_refs = (
-        refs[:n_faces], refs[n_faces : n_faces + 3], refs[n_faces + 3 :],
-    )
+    ready_faces, source_ref, face_refs = refs[:n_faces], refs[n_faces], refs[n_faces + 1 :]
     quarter = lane((8, 128)) // 32
     tile_high, tile_low = tile_ref[0], tile_ref[1]
     total = None
@@ -622,22 +620,16 @@
         total = moved if total is None else total + moved
     source = [total[64 * c : 64 * c + 64].reshape(8, 8, 128) for c in range(3)]
     middle = []
-    for c in range(4):
-        rate = rate_ref[c]
-        if c:
-            source_ref[c - 1] = source[c - 1]
-            rate = rate + source[c - 1]
-        middle.append(wave_ref[c] + acoustic_step * rate)
-        middle_ref[c] = middle[c]
-        carry = wave_ref[c] + middle[c]
-        carry_ref[c] = carry + acoustic_step * source[c - 1] if c else carry
-    for ready, face in zip(section_faces, face_refs):
-        face[0:5] = ready[...]
-    store_faces(middle, [face.at[5:9] for face in face_refs], counts)
+    for c in range(3):
+        source_ref[c] = source[c]
+        middle.append(wave_ref[1 + c] + acoustic_step * (rate_ref[1 + c] + source[c]))
+    for ready, face in zip(ready_faces, face_refs):
+        face[0:6] = ready[...]
+    store_faces(middle, [face.at[6:9] for face in face_refs], counts)
 
 
 def inner_kernel(
-    deriv_ref, high_ref, low_ref, les_ref, section_ref, middle_ref, carry_ref, mean_ref, source_ref,
+    deriv_ref, high_ref, low_ref, les_ref, section_ref, wave_ref, rate_ref, mean_ref, source_ref,
     les_base_ref, wave_base_ref, source_out, sem,
 ):
     copy = pltpu.make_async_copy(source_ref, source_out, sem)
@@ -646,12 +638,16 @@
     rate = les_rate(section, None)
     for c in range(5):
         les_base_ref[c] = 0.5 * ((les_ref[c] + section[c]) + rate[c])
+    first = read_all(rate_ref)
+    middle = [wave_ref[0] + acoustic_step * first[0]]
+    for c in range(1, 4):
+        middle.append(wave_ref[c] + acoustic_step * (first[c] + source_ref[c - 1]))
     rate = acoustic_rate(
-        read_all(middle_ref), read_all(mean_ref), None,
-        deriv_ref[...], (high_ref[...], low_ref[...]),
+        middle, read_all(mean_ref), None, deriv_ref[...], (high_ref[...], low_ref[...])
     )
     for c in range(4):
-        wave_base_ref[c] = 0.5 * (carry_ref[c] + acoustic_step * rate[c])
+        total = rate[c] + source_ref[c - 1] if c else rate[c]
+        wave_base_ref[c] = 0.5 * (wave_ref[c] + middle[c] + acoustic_step * total)
     copy.wait()
 
 
@@ -787,21 +783,21 @@
     for k in sending_sets(len(sets)):
         still = all(i == j for i, j in sets[k])
         moved.append(pieces[k] if still else lax.ppermute(pieces[k], "gx", sets[k]))
-    section, rate, mean_faces, *section_faces = call(
+    section, rate, mean_faces, *ready_faces = call(
         functools.partial(first_kernel, counts, n_faces),
         [VMEM] * (6 + n_faces),
-        [like(5), like(4), jax.ShapeDtypeStruct((6, 3, 8, 128), f32)] + face_shapes(counts, 5),
+        [like(5), like(4), jax.ShapeDtypeStruct((6, 3, 8, 128), f32)] + face_shapes(counts, 6),
         "first_rates",
         40000000,
     )(*tables, les, wave, mean, *got)
 
-    source, middle, carry, *sent = call(
+    source, *sent = call(
         functools.partial(source_kernel, counts, n_faces),
         [VMEM] * (3 + len(moved) + n_faces),
-        [like(3), like(4), like(4)] + faces,
+        [like(3)] + faces,
         "source_and_faces",
         10000000,
-    )(tile, wave, rate, *moved, *section_faces)
+    )(tile, wave, rate, *moved, *ready_faces)
     got = exchange(sent, counts)
     les_base, wave_base, source_out = call(
         inner_kernel,
@@ -811,7 +807,7 @@
         40000000,
         [pltpu.SemaphoreType.DMA],
         out_spec=[VMEM, VMEM, HBM],
-    )(*tables, les, section, middle, carry, mean, source)
+    )(*tables, les, section, wave, rate, mean, source)
     z_got = z_faces(got, counts)
     present = [face is not None for face in z_got]
     les_base, wave_base = call(

time: 20.4 us -> 20.4 us (level)
  no operation moved by 1% of the time
where the time goes in v1:
time: 20.4 us; the launch traced here: 20.2 us
  starting transfers between devices  11.3 us (55%)
  Pallas kernels  4.82 us (24%)
  waiting for transfers between devices  3.36 us (16%)
  between operations  0.75 us (4%)
    ppermute x10, starting transfers between devices, exchange(): lax.ppermute(face, axes, way)  9.33 us
    ppermute x3, starting transfers between devices, local(): moved.append(pieces[k] if still else lax.ppermute(pieces[k], 'gx', sets[k]))  1.94 us
    ppermute x10, waiting for transfers between devices, exchange(): lax.ppermute(face, axes, way)  1.81 us
    ppermute x3, waiting for transfers between devices, local(): moved.append(pieces[k] if still else lax.ppermute(pieces[k], 'gx', sets[k]))  1.55 us
    pallas_call x1, Pallas kernels, local(): call(functools.partial(load_kernel, counts), [HBM] * 5, [jax.ShapeDtypeSt...  1.19 us
    pallas_call x1, Pallas kernels, local(): call(functools.partial(last_kernel, counts, n_faces), [VMEM] * (3 + n_fac...  0.82 us
    pallas_call x1, Pallas kernels, local(): call(functools.partial(first_kernel, counts, n_faces), [VMEM] * (6 + n_fa...  0.77 us
    pallas_call x1, Pallas kernels, local(): call(inner_kernel, [VMEM] * 9, [like(5), like(4), like(3)], 'second_rates...  0.65 us
  transfers between devices with their start and end apart: 13, of which 5 were waited for; matrix products, arithmetic and copies ran while one was open for 0% of the time, Pallas kernels for 11%

profile of v1, /device:TPU:0, one launch (start us, length us, event | category | flops | bytes accessed | tf_op | source)
XLA Modules:
  0.0 20.2 jit_solution(2388679419235408287)
XLA Ops:
  0.6 1.2 %load_and_faces.1 = (f32[5,8,8,128]{3,2,1,0:T(8,128)S(1)}, f32[4,8,8,128]{3,2,1,0:T(8,128)S(1)}, s32[1,1,16]{2,1,0:T(1,128)S(1)}, s32[1,1,16]{2,1,0:T(1,128)S(1)...) custom-call(f32[5,8,8,128]{3,2,1,0:T(8,128)} %refs_0_.1, ...), custom_call_target="tpu_custom_call" | custom-call | flops 100000 | bytes 800000 | tf_op jit(solution)/shard_map/load_and_faces/pallas_call | solution.py:740
  1.8 3.0 %collective-permute-start = (f32[9,8,128]{2,1,0:T(8,128)S(1)}, f32[9,8,128]{2,1,0:T(8,128)S(1)}, u32[]{:S(2)}, u32[]{:S(2)}) collective-permute-start(f32[9,8,128]{2,1,0:T(8,128)S(1)} %get-tuple-element.47), channel_id=1, source_target_pairs={{0,1},{1,0},{2,3},{3,2},{4,28},{5,29},{6,30},{7,31},{8,9},{9,8},{1... | collective-permute-start | bytes 110600 | tf_op jit(solution)/shard_map/ppermute | solution.py:385
  4.8 0.7 %collective-permute-start.1 = (f32[9,8,128]{2,1,0:T(8,128)S(1)}, f32[9,8,128]{2,1,0:T(8,128)S(1)}, u32[]{:S(2)}, u32[]{:S(2)}) collective-permute-start(f32[9,8,128]{2,1,0:T(8,128)S(1)} %get-tuple-element.48), channel_id=1, source_target_pairs={{0,24},{1,25},{2,26},{3,27},{4,5},{5,4},{6,7},{7,6},{8,16},{9,17},... | collective-permute-start | bytes 110600 | tf_op jit(solution)/shard_map/ppermute | solution.py:385
  5.5 1.6 %collective-permute-start.2 = (f32[9,8,128]{2,1,0:T(8,128)S(1)}, f32[9,8,128]{2,1,0:T(8,128)S(1)}, u32[]{:S(2)}, u32[]{:S(2)}) collective-permute-start(f32[9,8,128]{2,1,0:T(8,128)S(1)} %get-tuple-element.49), channel_id=1, source_target_pairs={{0,2},{1,3},{2,0},{3,1},{4,12},{5,13},{6,14},{7,15},{8,10},{9,11},... | collective-permute-start | bytes 110600 | tf_op jit(solution)/shard_map/ppermute | solution.py:385
  7.1 0.7 %collective-permute-start.3 = (f32[9,8,128]{2,1,0:T(8,128)S(1)}, f32[9,8,128]{2,1,0:T(8,128)S(1)}, u32[]{:S(2)}, u32[]{:S(2)}) collective-permute-start(f32[9,8,128]{2,1,0:T(8,128)S(1)} %get-tuple-element.50), channel_id=1, source_target_pairs={{0,8},{1,9},{2,4},{3,5},{4,2},{5,3},{6,14},{7,15},{8,0},{9,1},{10,... | collective-permute-start | bytes 110600 | tf_op jit(solution)/shard_map/ppermute | solution.py:385
  7.8 0.0 collective-permute-start.4
  7.8 0.1 vorticity.1
  7.9 0.3 %plan.1 = (s32[4,8,128]{2,1,0:T(8,128)S(1)}, f32[4,8,128]{2,1,0:T(8,128)S(1)}, f32[64,8,128]{2,1,0:T(8,128)S(1)}, f32[8,8,128]{2,1,0:T(8,128)S(1)}, f32[2,8,128]{2,1,0:T(8,128)S(1)}) custom-call(s32[1,1,16]{2,1,0:T(1,128)S(1)} %get-tuple-element.54.owner_ref, s32[1,1,16]{2,1,0:T(1,128)S(1)} %get-tuple-element.55.slot_ref, f32[8,8]{1,0:T(8,128)S(1)} %get-tuple-element.56.proj_ref), custom_call_target="tpu_custom_call" | custom-call | flops 1000000 | bytes 800000 | tf_op jit(solution)/shard_map/plan/pallas_call | solution.py:752
  8.2 0.0 collective-permute-done.refs_0_
  8.2 0.3 %collective-permute-done.1.refs_1_ = f32[9,8,128]{2,1,0:T(8,128)S(1)} collective-permute-done((f32[9,8,128]{2,1,0:T(8,128)S(1)}, f32[9,8,128]{2,1,0:T(8,128)S(1)}, u32[]{:S(2)}, u32[]{:S(2)}) %collective-permute-start.1) | collective-permute-done | bytes 36896 | tf_op jit(solution)/shard_map/ppermute | solution.py:385
  8.5 0.2 vorticity_z.1.vort_ref
  8.7 1.1 %collective-permute-done.2.refs_2_ = f32[9,8,128]{2,1,0:T(8,128)S(1)} collective-permute-done((f32[9,8,128]{2,1,0:T(8,128)S(1)}, f32[9,8,128]{2,1,0:T(8,128)S(1)}, u32[]{:S(2)}, u32[]{:S(2)}) %collective-permute-start.2) | collective-permute-done | bytes 36896 | tf_op jit(solution)/shard_map/ppermute | solution.py:385
  9.9 0.0 copy-start.1
  9.9 0.0 copy-start.2
  9.9 0.3 %lamb_blocks.1 = (f32[7,8,128]{2,1,0:T(8,128)S(1)}, f32[7,8,128]{2,1,0:T(8,128)S(1)}, f32[7,8,128]{2,1,0:T(8,128)S(1)}, f32[7,8,128]{2,1,0:T(8,128)S(1)}) custom-call(s32[4,8,128]{2,1,0:T(8,128)S(1)} %get-tuple-element.58.order_ref, f32[4,8,128]{2,1,0:T(8,128)S(1)} %get-tuple-element.59.marks_ref, f32[64,8,128]{2,1,0:T(8,128)S(1)} %get-tuple-element.60.along_x_ref, ...), custom_call_target="tpu_custom_call" | custom-call | flops 10000000 | bytes 800000 | tf_op jit(solution)/shard_map/lamb_blocks/pallas_call | solution.py:775
  10.1 0.0 copy-start.3
  10.2 0.1 collective-permute-start.5
  10.2 1.7 %collective-permute-start.6 = (f32[7,8,128]{2,1,0:T(8,128)S(1)}, f32[7,8,128]{2,1,0:T(8,128)S(1)}, u32[]{:S(2)}, u32[]{:S(2)}) collective-permute-start(f32[7,8,128]{2,1,0:T(8,128)S(1)} %get-tuple-element.65), channel_id=1, source_target_pairs={{0,16},{8,24},{16,0},{24,8},{1,17},{9,25},{17,1},{25,9},{2,18},{10... | collective-permute-start | bytes 86024 | tf_op jit(solution)/shard_map/ppermute | solution.py:785
  12.0 0.1 collective-permute-start.7
  12.1 0.8 %first_rates.1 = (f32[5,8,8,128]{3,2,1,0:T(8,128)S(1)}, f32[4,8,8,128]{3,2,1,0:T(8,128)S(1)}, f32[6,3,8,128]{3,2,1,0:T(8,128)S(1)}, f32[6,8,128]{2,1,0:T(8,128)S...) custom-call(f32[8,8]{1,0:T(8,128)S(1)} %copy-done.3, ...), custom_call_target="tpu_custom_call" | custom-call | flops 40000000 | bytes 800000 | tf_op jit(solution)/shard_map/first_rates/pallas_call | solution.py:786
  12.9 0.7 %collective-permute-done.5.refs_0_ = f32[7,8,128]{2,1,0:T(8,128)S(1)} collective-permute-done((f32[7,8,128]{2,1,0:T(8,128)S(1)}, f32[7,8,128]{2,1,0:T(8,128)S(1)}, u32[]{:S(2)}, u32[]{:S(2)}) %collective-permute-start.5) | collective-permute-done | bytes 28704 | tf_op jit(solution)/shard_map/ppermute | solution.py:785
  13.5 0.9 %collective-permute-done.6.refs_1_ = f32[7,8,128]{2,1,0:T(8,128)S(1)} collective-permute-done((f32[7,8,128]{2,1,0:T(8,128)S(1)}, f32[7,8,128]{2,1,0:T(8,128)S(1)}, u32[]{:S(2)}, u32[]{:S(2)}) %collective-permute-start.6) | collective-permute-done | bytes 28704 | tf_op jit(solution)/shard_map/ppermute | solution.py:785
  14.4 0.3 %source_and_faces.1 = (f32[3,8,8,128]{3,2,1,0:T(8,128)S(1)}, f32[9,8,128]{2,1,0:T(8,128)S(1)}, f32[9,8,128]{2,1,0:T(8,128)S(1)}, f32[9,8,128]{2,1,0:T(8,128)S(1)...) custom-call(f32[2,8,128]{2,1,0:T(8,128)S(1)} %get-tuple-element.57.tile_ref, ...), custom_call_target="tpu_custom_call" | custom-call | flops 10000000 | bytes 800000 | tf_op jit(solution)/shard_map/source_and_faces/pallas_call | solution.py:794
  14.8 0.6 %collective-permute-start.8 = (f32[9,8,128]{2,1,0:T(8,128)S(1)}, f32[9,8,128]{2,1,0:T(8,128)S(1)}, u32[]{:S(2)}, u32[]{:S(2)}) collective-permute-start(f32[9,8,128]{2,1,0:T(8,128)S(1)} %get-tuple-element.77), channel_id=1, source_target_pairs={{0,1},{1,0},{2,3},{3,2},{4,28},{5,29},{6,30},{7,31},{8,9},{9,8},{1... | collective-permute-start | bytes 110600 | tf_op jit(solution)/shard_map/ppermute | solution.py:385
  15.4 1.7 %collective-permute-start.10 = (f32[9,8,128]{2,1,0:T(8,128)S(1)}, f32[9,8,128]{2,1,0:T(8,128)S(1)}, u32[]{:S(2)}, u32[]{:S(2)}) collective-permute-start(f32[9,8,128]{2,1,0:T(8,128)S(1)} %get-tuple-element.81), channel_id=1, source_target_pairs={{0,2},{1,3},{2,0},{3,1},{4,12},{5,13},{6,14},{7,15},{8,10},{9,11},... | collective-permute-start | bytes 110600 | tf_op jit(solution)/shard_map/ppermute | solution.py:385
  17.1 1.1 %collective-permute-start.11 = (f32[9,8,128]{2,1,0:T(8,128)S(1)}, f32[9,8,128]{2,1,0:T(8,128)S(1)}, u32[]{:S(2)}, u32[]{:S(2)}) collective-permute-start(f32[9,8,128]{2,1,0:T(8,128)S(1)} %get-tuple-element.82), channel_id=1, source_target_pairs={{0,8},{1,9},{2,4},{3,5},{4,2},{5,3},{6,14},{7,15},{8,0},{9,1},{10,... | collective-permute-start | bytes 110600 | tf_op jit(solution)/shard_map/ppermute | solution.py:385
  18.2 0.6 %second_rates_inner.1 = (f32[5,8,8,128]{3,2,1,0:T(8,128)S(1)}, f32[4,8,8,128]{3,2,1,0:T(8,128)S(1)}, f32[3,8,8,128]{3,2,1,0:T(8,128)}) custom-call(f32[8,8]{1,0:T(8,128)S(1)} %copy-done.3, bf16[128,128]{1,0:T(8,128)(2,1)S(1)} %copy-done.2, bf16[128,128]{1,0:T(8,128)(2,1)S(1)} %copy-done.1, f32[5,8,8,128]{3,2,1,0:T(8,128)S(1)} %get-tuple-element.45.les_ref, ...), custom_call_target="tpu_custom_call" | custom-call | flops 40000000 | bytes 800000 | tf_op jit(solution)/shard_map/second_rates_inner/pallas_call | solution.py:802
  18.9 0.2 %collective-permute-done.9.refs_1_ = f32[9,8,128]{2,1,0:T(8,128)S(1)} collective-permute-done((f32[9,8,128]{2,1,0:T(8,128)S(1)}, f32[9,8,128]{2,1,0:T(8,128)S(1)}, u32[]{:S(2)}, u32[]{:S(2)}) %collective-permute-start.9) | collective-permute-done | bytes 36896 | tf_op jit(solution)/shard_map/ppermute | solution.py:385
  19.1 0.2 %second_rates_z.1 = (f32[5,8,8,128]{3,2,1,0:T(8,128)S(1)}, f32[4,8,8,128]{3,2,1,0:T(8,128)S(1)}) custom-call(f32[5,8,8,128]{3,2,1,0:T(8,128)S(1)} %get-tuple-element.74.les_base_ref, f32[4,8,8,128]{3,2,1,0:T(8,128)S(1)} %get-tuple-element.75.wave_base_ref, f32[6,3,8,128]{3,2,1,0:T(8,128)S(1)} %get-tuple-element.76.mean_faces_ref, ...), custom_call_target="tpu_custom_call" | custom-call | flops 1000000 | bytes 800000 | tf_op jit(solution)/shard_map/second_rates_z/pallas_call | solution.py:813
  19.3 0.0 collective-permute-done.10.refs_2_
  19.4 0.0 collective-permute-done.12.refs_4_
  19.4 0.8 %second_rates_outer.1 = (f32[5,8,8,128]{3,2,1,0:T(8,128)}, f32[4,8,8,128]{3,2,1,0:T(8,128)}) custom-call(f32[5,8,8,128]{3,2,1,0:T(8,128)S(1)} %get-tuple-element.79.les_base_ref, f32[4,8,8,128]{3,2,1,0:T(8,128)S(1)} %get-tuple-element.80.wave_base_ref, f32[6,3,8,128]{3,2,1,0:T(8,128)S(1)} %get-tuple-element.76.mean_faces_ref, ...), custom_call_target="tpu_custom_call" | custom-call | flops 4000000 | bytes 800000 | tf_op jit(solution)/shard_map/second_rates_outer/pallas_call | solution.py:820
  (12 shorter events, 0.0 us)
Async XLA Ops:
  1.8 6.4 %collective-permute-start = (f32[9,8,128]{2,1,0:T(8,128)S(1)}, f32[9,8,128]{2,1,0:T(8,128)S(1)}, u32[]{:S(2)}, u32[]{:S(2)}) collective-permute-start(f32[9,8,128]{2,1,0:T(8,128)S(1)} %get-tuple-element.47), channel_id=1, source_target_pairs={{0,1},{1,0},{2,3},{3,2},{4,28},{5,29},{6,30},{7,31},{8,9},{9,8},{1... | collective-permute-start | bytes 110600 | tf_op jit(solution)/shard_map/ppermute | solution.py:385
  4.8 3.7 %collective-permute-start.1 = (f32[9,8,128]{2,1,0:T(8,128)S(1)}, f32[9,8,128]{2,1,0:T(8,128)S(1)}, u32[]{:S(2)}, u32[]{:S(2)}) collective-permute-start(f32[9,8,128]{2,1,0:T(8,128)S(1)} %get-tuple-element.48), channel_id=1, source_target_pairs={{0,24},{1,25},{2,26},{3,27},{4,5},{5,4},{6,7},{7,6},{8,16},{9,17},... | collective-permute-start | bytes 110600 | tf_op jit(solution)/shard_map/ppermute | solution.py:385
  5.5 4.3 %collective-permute-start.2 = (f32[9,8,128]{2,1,0:T(8,128)S(1)}, f32[9,8,128]{2,1,0:T(8,128)S(1)}, u32[]{:S(2)}, u32[]{:S(2)}) collective-permute-start(f32[9,8,128]{2,1,0:T(8,128)S(1)} %get-tuple-element.49), channel_id=1, source_target_pairs={{0,2},{1,3},{2,0},{3,1},{4,12},{5,13},{6,14},{7,15},{8,10},{9,11},... | collective-permute-start | bytes 110600 | tf_op jit(solution)/shard_map/ppermute | solution.py:385
  7.1 2.8 %collective-permute-start.3 = (f32[9,8,128]{2,1,0:T(8,128)S(1)}, f32[9,8,128]{2,1,0:T(8,128)S(1)}, u32[]{:S(2)}, u32[]{:S(2)}) collective-permute-start(f32[9,8,128]{2,1,0:T(8,128)S(1)} %get-tuple-element.50), channel_id=1, source_target_pairs={{0,8},{1,9},{2,4},{3,5},{4,2},{5,3},{6,14},{7,15},{8,0},{9,1},{10,... | collective-permute-start | bytes 110600 | tf_op jit(solution)/shard_map/ppermute | solution.py:385
  7.8 2.1 %collective-permute-start.4 = (f32[9,8,128]{2,1,0:T(8,128)S(1)}, f32[9,8,128]{2,1,0:T(8,128)S(1)}, u32[]{:S(2)}, u32[]{:S(2)}) collective-permute-start(f32[9,8,128]{2,1,0:T(8,128)S(1)} %get-tuple-element.51), channel_id=1, source_target_pairs={{0,8},{1,9},{2,10},{3,11},{4,6},{5,7},{6,4},{7,5},{8,0},{9,1},{10,... | collective-permute-start | bytes 110600 | tf_op jit(solution)/shard_map/ppermute | solution.py:385
  9.9 2.2 %copy-start = (f32[3,8,8,128]{3,2,1,0:T(8,128)S(1)}, f32[3,8,8,128]{3,2,1,0:T(8,128)}, u32[]{:S(2)}) copy-start(f32[3,8,8,128]{3,2,1,0:T(8,128)} %mean_ref.3) | copy-start | bytes 294916
  9.9 2.2 %copy-start.1 = (bf16[128,128]{1,0:T(8,128)(2,1)S(1)}, bf16[128,128]{1,0:T(8,128)(2,1)}, u32[]{:S(2)}) copy-start(bf16[128,128]{1,0:T(8,128)(2,1)} %constant.8.clone.low_ref) | copy-start | bytes 98308
  9.9 2.2 %copy-start.2 = (bf16[128,128]{1,0:T(8,128)(2,1)S(1)}, bf16[128,128]{1,0:T(8,128)(2,1)}, u32[]{:S(2)}) copy-start(bf16[128,128]{1,0:T(8,128)(2,1)} %constant.7.clone.high_ref) | copy-start | bytes 98308
  10.1 2.0 %copy-start.3 = (f32[8,8]{1,0:T(8,128)S(1)}, f32[8,8]{1,0:T(8,128)}, u32[]{:S(2)}) copy-start(f32[8,8]{1,0:T(8,128)} %constant.6.clone.deriv_ref) | copy-start | bytes 772
  10.2 3.4 %collective-permute-start.5 = (f32[7,8,128]{2,1,0:T(8,128)S(1)}, f32[7,8,128]{2,1,0:T(8,128)S(1)}, u32[]{:S(2)}, u32[]{:S(2)}) collective-permute-start(f32[7,8,128]{2,1,0:T(8,128)S(1)} %get-tuple-element.64), channel_id=1, source_target_pairs={{0,24},{8,16},{16,8},{24,0},{1,25},{9,17},{17,9},{25,1},{2,26},{10... | collective-permute-start | bytes 86024 | tf_op jit(solution)/shard_map/ppermute | solution.py:785
  10.2 4.2 %collective-permute-start.6 = (f32[7,8,128]{2,1,0:T(8,128)S(1)}, f32[7,8,128]{2,1,0:T(8,128)S(1)}, u32[]{:S(2)}, u32[]{:S(2)}) collective-permute-start(f32[7,8,128]{2,1,0:T(8,128)S(1)} %get-tuple-element.65), channel_id=1, source_target_pairs={{0,16},{8,24},{16,0},{24,8},{1,17},{9,25},{17,1},{25,9},{2,18},{10... | collective-permute-start | bytes 86024 | tf_op jit(solution)/shard_map/ppermute | solution.py:785
  12.0 2.5 %collective-permute-start.7 = (f32[7,8,128]{2,1,0:T(8,128)S(1)}, f32[7,8,128]{2,1,0:T(8,128)S(1)}, u32[]{:S(2)}, u32[]{:S(2)}) collective-permute-start(f32[7,8,128]{2,1,0:T(8,128)S(1)} %get-tuple-element.66), channel_id=1, source_target_pairs={{0,8},{8,0},{16,24},{24,16},{1,9},{9,1},{17,25},{25,17},{2,10},{10... | collective-permute-start | bytes 86024 | tf_op jit(solution)/shard_map/ppermute | solution.py:785
  14.8 4.1 %collective-permute-start.8 = (f32[9,8,128]{2,1,0:T(8,128)S(1)}, f32[9,8,128]{2,1,0:T(8,128)S(1)}, u32[]{:S(2)}, u32[]{:S(2)}) collective-permute-start(f32[9,8,128]{2,1,0:T(8,128)S(1)} %get-tuple-element.77), channel_id=1, source_target_pairs={{0,1},{1,0},{2,3},{3,2},{4,28},{5,29},{6,30},{7,31},{8,9},{9,8},{1... | collective-permute-start | bytes 110600 | tf_op jit(solution)/shard_map/ppermute | solution.py:385
  15.4 3.7 %collective-permute-start.9 = (f32[9,8,128]{2,1,0:T(8,128)S(1)}, f32[9,8,128]{2,1,0:T(8,128)S(1)}, u32[]{:S(2)}, u32[]{:S(2)}) collective-permute-start(f32[9,8,128]{2,1,0:T(8,128)S(1)} %get-tuple-element.78), channel_id=1, source_target_pairs={{0,24},{1,25},{2,26},{3,27},{4,5},{5,4},{6,7},{7,6},{8,16},{9,17},... | collective-permute-start | bytes 110600 | tf_op jit(solution)/shard_map/ppermute | solution.py:385
  15.4 4.0 %collective-permute-start.10 = (f32[9,8,128]{2,1,0:T(8,128)S(1)}, f32[9,8,128]{2,1,0:T(8,128)S(1)}, u32[]{:S(2)}, u32[]{:S(2)}) collective-permute-start(f32[9,8,128]{2,1,0:T(8,128)S(1)} %get-tuple-element.81), channel_id=1, source_target_pairs={{0,2},{1,3},{2,0},{3,1},{4,12},{5,13},{6,14},{7,15},{8,10},{9,11},... | collective-permute-start | bytes 110600 | tf_op jit(solution)/shard_map/ppermute | solution.py:385
  17.1 2.2 %collective-permute-start.11 = (f32[9,8,128]{2,1,0:T(8,128)S(1)}, f32[9,8,128]{2,1,0:T(8,128)S(1)}, u32[]{:S(2)}, u32[]{:S(2)}) collective-permute-start(f32[9,8,128]{2,1,0:T(8,128)S(1)} %get-tuple-element.82), channel_id=1, source_target_pairs={{0,8},{1,9},{2,4},{3,5},{4,2},{5,3},{6,14},{7,15},{8,0},{9,1},{10,... | collective-permute-start | bytes 110600 | tf_op jit(solution)/shard_map/ppermute | solution.py:385
  18.2 1.2 %collective-permute-start.12 = (f32[9,8,128]{2,1,0:T(8,128)S(1)}, f32[9,8,128]{2,1,0:T(8,128)S(1)}, u32[]{:S(2)}, u32[]{:S(2)}) collective-permute-start(f32[9,8,128]{2,1,0:T(8,128)S(1)} %get-tuple-element.83), channel_id=1, source_target_pairs={{0,8},{1,9},{2,10},{3,11},{4,6},{5,7},{6,4},{7,5},{8,0},{9,1},{10,... | collective-permute-start | bytes 110600 | tf_op jit(solution)/shard_map/ppermute | solution.py:385

commit v2 on v1

--- a/solution.py
+++ b/solution.py
@@ -544,7 +544,9 @@
     quarter = lane((8, 128)) // 32
     for s in range((len(out_refs) + 3) // 4):
         ordered = [
-            jnp.take_along_axis(block, order_ref[4 * s + k % 4], axis=1)
+            jnp.take_along_axis(
+                block, order_ref[4 * s + k % 4], axis=1, mode="promise_in_bounds"
+            )
             for k, block in enumerate(blocks)
         ]
         for r in range(min(4, len(out_refs) - 4 * s)):
@@ -652,16 +654,16 @@
 
 
 def add_layers(counts, chosen, face_refs, mean_faces_ref, les_base_ref, wave_base_ref, put):
-    layers = les_outer(load_faces(face_refs, counts, 0, 5, chosen))
-    for c in range(5):
-        part = [layer and (0.5 * layer[0][c], 0.5 * layer[1][c]) for layer in layers]
-        put(c, with_layers(les_base_ref[c], part))
     mean_faces = [[mean_faces_ref[n, c] for c in range(3)] for n in range(6)]
     layers = acoustic_outer(mean_faces, load_faces(face_refs, counts, 5, 9, chosen))
     step = 0.5 * acoustic_step
     for c in range(4):
         part = [layer and (step * layer[0][c], step * layer[1][c]) for layer in layers]
         put(5 + c, with_layers(wave_base_ref[c], part))
+    layers = les_outer(load_faces(face_refs, counts, 0, 5, chosen))
+    for c in range(5):
+        part = [layer and (0.5 * layer[0][c], 0.5 * layer[1][c]) for layer in layers]
+        put(c, with_layers(les_base_ref[c], part))
 
 
 def z_faces(faces, counts):

time: 20.4 us -> 20.4 us (level)
  no operation moved by 1% of the time
where the time goes in v2:
time: 20.4 us; the launch traced here: 20.2 us
  starting transfers between devices  11.3 us (55%)
  Pallas kernels  4.82 us (24%)
  waiting for transfers between devices  3.36 us (16%)
  between operations  0.75 us (4%)
    ppermute x10, starting transfers between devices, exchange(): lax.ppermute(face, axes, way)  9.33 us
    ppermute x3, starting transfers between devices, local(): moved.append(pieces[k] if still else lax.ppermute(pieces[k], 'gx', sets[k]))  1.94 us
    ppermute x10, waiting for transfers between devices, exchange(): lax.ppermute(face, axes, way)  1.81 us
    ppermute x3, waiting for transfers between devices, local(): moved.append(pieces[k] if still else lax.ppermute(pieces[k], 'gx', sets[k]))  1.55 us
    pallas_call x1, Pallas kernels, local(): call(functools.partial(load_kernel, counts), [HBM] * 5, [jax.ShapeDtypeSt...  1.19 us
    pallas_call x1, Pallas kernels, local(): call(functools.partial(last_kernel, counts, n_faces), [VMEM] * (3 + n_fac...  0.83 us
    pallas_call x1, Pallas kernels, local(): call(functools.partial(first_kernel, counts, n_faces), [VMEM] * (6 + n_fa...  0.77 us
    pallas_call x1, Pallas kernels, local(): call(inner_kernel, [VMEM] * 9, [like(5), like(4), like(3)], 'second_rates...  0.65 us
  transfers between devices with their start and end apart: 13, of which 5 were waited for; matrix products, arithmetic and copies ran while one was open for 0% of the time, Pallas kernels for 11%

profile of v2, /device:TPU:0, one launch (start us, length us, event | category | flops | bytes accessed | tf_op | source)
XLA Modules:
  0.0 20.2 jit_solution(12437774412595628909)
XLA Ops:
  0.6 1.2 %load_and_faces.1 = (f32[5,8,8,128]{3,2,1,0:T(8,128)S(1)}, f32[4,8,8,128]{3,2,1,0:T(8,128)S(1)}, s32[1,1,16]{2,1,0:T(1,128)S(1)}, s32[1,1,16]{2,1,0:T(1,128)S(1)...) custom-call(f32[5,8,8,128]{3,2,1,0:T(8,128)} %refs_0_.1, ...), custom_call_target="tpu_custom_call" | custom-call | flops 100000 | bytes 800000 | tf_op jit(solution)/shard_map/load_and_faces/pallas_call | solution.py:742
  1.8 3.0 %collective-permute-start = (f32[9,8,128]{2,1,0:T(8,128)S(1)}, f32[9,8,128]{2,1,0:T(8,128)S(1)}, u32[]{:S(2)}, u32[]{:S(2)}) collective-permute-start(f32[9,8,128]{2,1,0:T(8,128)S(1)} %get-tuple-element.47), channel_id=1, source_target_pairs={{0,1},{1,0},{2,3},{3,2},{4,28},{5,29},{6,30},{7,31},{8,9},{9,8},{1... | collective-permute-start | bytes 110600 | tf_op jit(solution)/shard_map/ppermute | solution.py:385
  4.8 0.7 %collective-permute-start.1 = (f32[9,8,128]{2,1,0:T(8,128)S(1)}, f32[9,8,128]{2,1,0:T(8,128)S(1)}, u32[]{:S(2)}, u32[]{:S(2)}) collective-permute-start(f32[9,8,128]{2,1,0:T(8,128)S(1)} %get-tuple-element.48), channel_id=1, source_target_pairs={{0,24},{1,25},{2,26},{3,27},{4,5},{5,4},{6,7},{7,6},{8,16},{9,17},... | collective-permute-start | bytes 110600 | tf_op jit(solution)/shard_map/ppermute | solution.py:385
  5.5 1.6 %collective-permute-start.2 = (f32[9,8,128]{2,1,0:T(8,128)S(1)}, f32[9,8,128]{2,1,0:T(8,128)S(1)}, u32[]{:S(2)}, u32[]{:S(2)}) collective-permute-start(f32[9,8,128]{2,1,0:T(8,128)S(1)} %get-tuple-element.49), channel_id=1, source_target_pairs={{0,2},{1,3},{2,0},{3,1},{4,12},{5,13},{6,14},{7,15},{8,10},{9,11},... | collective-permute-start | bytes 110600 | tf_op jit(solution)/shard_map/ppermute | solution.py:385
  7.1 0.7 %collective-permute-start.3 = (f32[9,8,128]{2,1,0:T(8,128)S(1)}, f32[9,8,128]{2,1,0:T(8,128)S(1)}, u32[]{:S(2)}, u32[]{:S(2)}) collective-permute-start(f32[9,8,128]{2,1,0:T(8,128)S(1)} %get-tuple-element.50), channel_id=1, source_target_pairs={{0,8},{1,9},{2,4},{3,5},{4,2},{5,3},{6,14},{7,15},{8,0},{9,1},{10,... | collective-permute-start | bytes 110600 | tf_op jit(solution)/shard_map/ppermute | solution.py:385
  7.8 0.0 collective-permute-start.4
  7.8 0.1 vorticity.1
  7.9 0.3 %plan.1 = (s32[4,8,128]{2,1,0:T(8,128)S(1)}, f32[4,8,128]{2,1,0:T(8,128)S(1)}, f32[64,8,128]{2,1,0:T(8,128)S(1)}, f32[8,8,128]{2,1,0:T(8,128)S(1)}, f32[2,8,128]{2,1,0:T(8,128)S(1)}) custom-call(s32[1,1,16]{2,1,0:T(1,128)S(1)} %get-tuple-element.54.owner_ref, s32[1,1,16]{2,1,0:T(1,128)S(1)} %get-tuple-element.55.slot_ref, f32[8,8]{1,0:T(8,128)S(1)} %get-tuple-element.56.proj_ref), custom_call_target="tpu_custom_call" | custom-call | flops 1000000 | bytes 800000 | tf_op jit(solution)/shard_map/plan/pallas_call | solution.py:754
  8.2 0.0 collective-permute-done.refs_0_
  8.2 0.3 %collective-permute-done.1.refs_1_ = f32[9,8,128]{2,1,0:T(8,128)S(1)} collective-permute-done((f32[9,8,128]{2,1,0:T(8,128)S(1)}, f32[9,8,128]{2,1,0:T(8,128)S(1)}, u32[]{:S(2)}, u32[]{:S(2)}) %collective-permute-start.1) | collective-permute-done | bytes 36896 | tf_op jit(solution)/shard_map/ppermute | solution.py:385
  8.5 0.2 vorticity_z.1.vort_ref
  8.7 1.1 %collective-permute-done.2.refs_2_ = f32[9,8,128]{2,1,0:T(8,128)S(1)} collective-permute-done((f32[9,8,128]{2,1,0:T(8,128)S(1)}, f32[9,8,128]{2,1,0:T(8,128)S(1)}, u32[]{:S(2)}, u32[]{:S(2)}) %collective-permute-start.2) | collective-permute-done | bytes 36896 | tf_op jit(solution)/shard_map/ppermute | solution.py:385
  9.9 0.0 copy-start.1
  9.9 0.0 copy-start.2
  9.9 0.3 %lamb_blocks.1 = (f32[7,8,128]{2,1,0:T(8,128)S(1)}, f32[7,8,128]{2,1,0:T(8,128)S(1)}, f32[7,8,128]{2,1,0:T(8,128)S(1)}, f32[7,8,128]{2,1,0:T(8,128)S(1)}) custom-call(s32[4,8,128]{2,1,0:T(8,128)S(1)} %get-tuple-element.58.order_ref, f32[4,8,128]{2,1,0:T(8,128)S(1)} %get-tuple-element.59.marks_ref, f32[64,8,128]{2,1,0:T(8,128)S(1)} %get-tuple-element.60.along_x_ref, ...), custom_call_target="tpu_custom_call" | custom-call | flops 10000000 | bytes 800000 | tf_op jit(solution)/shard_map/lamb_blocks/pallas_call | solution.py:777
  10.1 0.0 copy-start.3
  10.2 0.1 collective-permute-start.5
  10.2 1.7 %collective-permute-start.6 = (f32[7,8,128]{2,1,0:T(8,128)S(1)}, f32[7,8,128]{2,1,0:T(8,128)S(1)}, u32[]{:S(2)}, u32[]{:S(2)}) collective-permute-start(f32[7,8,128]{2,1,0:T(8,128)S(1)} %get-tuple-element.65), channel_id=1, source_target_pairs={{0,16},{8,24},{16,0},{24,8},{1,17},{9,25},{17,1},{25,9},{2,18},{10... | collective-permute-start | bytes 86024 | tf_op jit(solution)/shard_map/ppermute | solution.py:787
  12.0 0.1 collective-permute-start.7
  12.1 0.8 %first_rates.1 = (f32[5,8,8,128]{3,2,1,0:T(8,128)S(1)}, f32[4,8,8,128]{3,2,1,0:T(8,128)S(1)}, f32[6,3,8,128]{3,2,1,0:T(8,128)S(1)}, f32[6,8,128]{2,1,0:T(8,128)S...) custom-call(f32[8,8]{1,0:T(8,128)S(1)} %copy-done.3, ...), custom_call_target="tpu_custom_call" | custom-call | flops 40000000 | bytes 800000 | tf_op jit(solution)/shard_map/first_rates/pallas_call | solution.py:788
  12.9 0.7 %collective-permute-done.5.refs_0_ = f32[7,8,128]{2,1,0:T(8,128)S(1)} collective-permute-done((f32[7,8,128]{2,1,0:T(8,128)S(1)}, f32[7,8,128]{2,1,0:T(8,128)S(1)}, u32[]{:S(2)}, u32[]{:S(2)}) %collective-permute-start.5) | collective-permute-done | bytes 28704 | tf_op jit(solution)/shard_map/ppermute | solution.py:787
  13.5 0.9 %collective-permute-done.6.refs_1_ = f32[7,8,128]{2,1,0:T(8,128)S(1)} collective-permute-done((f32[7,8,128]{2,1,0:T(8,128)S(1)}, f32[7,8,128]{2,1,0:T(8,128)S(1)}, u32[]{:S(2)}, u32[]{:S(2)}) %collective-permute-start.6) | collective-permute-done | bytes 28704 | tf_op jit(solution)/shard_map/ppermute | solution.py:787
  14.4 0.3 %source_and_faces.1 = (f32[3,8,8,128]{3,2,1,0:T(8,128)S(1)}, f32[9,8,128]{2,1,0:T(8,128)S(1)}, f32[9,8,128]{2,1,0:T(8,128)S(1)}, f32[9,8,128]{2,1,0:T(8,128)S(1)...) custom-call(f32[2,8,128]{2,1,0:T(8,128)S(1)} %get-tuple-element.57.tile_ref, ...), custom_call_target="tpu_custom_call" | custom-call | flops 10000000 | bytes 800000 | tf_op jit(solution)/shard_map/source_and_faces/pallas_call | solution.py:796
  14.8 0.6 %collective-permute-start.8 = (f32[9,8,128]{2,1,0:T(8,128)S(1)}, f32[9,8,128]{2,1,0:T(8,128)S(1)}, u32[]{:S(2)}, u32[]{:S(2)}) collective-permute-start(f32[9,8,128]{2,1,0:T(8,128)S(1)} %get-tuple-element.77), channel_id=1, source_target_pairs={{0,1},{1,0},{2,3},{3,2},{4,28},{5,29},{6,30},{7,31},{8,9},{9,8},{1... | collective-permute-start | bytes 110600 | tf_op jit(solution)/shard_map/ppermute | solution.py:385
  15.4 1.7 %collective-permute-start.10 = (f32[9,8,128]{2,1,0:T(8,128)S(1)}, f32[9,8,128]{2,1,0:T(8,128)S(1)}, u32[]{:S(2)}, u32[]{:S(2)}) collective-permute-start(f32[9,8,128]{2,1,0:T(8,128)S(1)} %get-tuple-element.81), channel_id=1, source_target_pairs={{0,2},{1,3},{2,0},{3,1},{4,12},{5,13},{6,14},{7,15},{8,10},{9,11},... | collective-permute-start | bytes 110600 | tf_op jit(solution)/shard_map/ppermute | solution.py:385
  17.1 1.1 %collective-permute-start.11 = (f32[9,8,128]{2,1,0:T(8,128)S(1)}, f32[9,8,128]{2,1,0:T(8,128)S(1)}, u32[]{:S(2)}, u32[]{:S(2)}) collective-permute-start(f32[9,8,128]{2,1,0:T(8,128)S(1)} %get-tuple-element.82), channel_id=1, source_target_pairs={{0,8},{1,9},{2,4},{3,5},{4,2},{5,3},{6,14},{7,15},{8,0},{9,1},{10,... | collective-permute-start | bytes 110600 | tf_op jit(solution)/shard_map/ppermute | solution.py:385
  18.2 0.6 %second_rates_inner.1 = (f32[5,8,8,128]{3,2,1,0:T(8,128)S(1)}, f32[4,8,8,128]{3,2,1,0:T(8,128)S(1)}, f32[3,8,8,128]{3,2,1,0:T(8,128)}) custom-call(f32[8,8]{1,0:T(8,128)S(1)} %copy-done.3, bf16[128,128]{1,0:T(8,128)(2,1)S(1)} %copy-done.2, bf16[128,128]{1,0:T(8,128)(2,1)S(1)} %copy-done.1, f32[5,8,8,128]{3,2,1,0:T(8,128)S(1)} %get-tuple-element.45.les_ref, ...), custom_call_target="tpu_custom_call" | custom-call | flops 40000000 | bytes 800000 | tf_op jit(solution)/shard_map/second_rates_inner/pallas_call | solution.py:804
  18.9 0.2 %collective-permute-done.9.refs_1_ = f32[9,8,128]{2,1,0:T(8,128)S(1)} collective-permute-done((f32[9,8,128]{2,1,0:T(8,128)S(1)}, f32[9,8,128]{2,1,0:T(8,128)S(1)}, u32[]{:S(2)}, u32[]{:S(2)}) %collective-permute-start.9) | collective-permute-done | bytes 36896 | tf_op jit(solution)/shard_map/ppermute | solution.py:385
  19.1 0.2 %second_rates_z.1 = (f32[5,8,8,128]{3,2,1,0:T(8,128)S(1)}, f32[4,8,8,128]{3,2,1,0:T(8,128)S(1)}) custom-call(f32[5,8,8,128]{3,2,1,0:T(8,128)S(1)} %get-tuple-element.74.les_base_ref, f32[4,8,8,128]{3,2,1,0:T(8,128)S(1)} %get-tuple-element.75.wave_base_ref, f32[6,3,8,128]{3,2,1,0:T(8,128)S(1)} %get-tuple-element.76.mean_faces_ref, ...), custom_call_target="tpu_custom_call" | custom-call | flops 1000000 | bytes 800000 | tf_op jit(solution)/shard_map/second_rates_z/pallas_call | solution.py:815
  19.3 0.0 collective-permute-done.10.refs_2_
  19.4 0.0 collective-permute-done.12.refs_4_
  19.4 0.8 %second_rates_outer.1 = (f32[5,8,8,128]{3,2,1,0:T(8,128)}, f32[4,8,8,128]{3,2,1,0:T(8,128)}) custom-call(f32[5,8,8,128]{3,2,1,0:T(8,128)S(1)} %get-tuple-element.79.les_base_ref, f32[4,8,8,128]{3,2,1,0:T(8,128)S(1)} %get-tuple-element.80.wave_base_ref, f32[6,3,8,128]{3,2,1,0:T(8,128)S(1)} %get-tuple-element.76.mean_faces_ref, ...), custom_call_target="tpu_custom_call" | custom-call | flops 4000000 | bytes 800000 | tf_op jit(solution)/shard_map/second_rates_outer/pallas_call | solution.py:822
  (12 shorter events, 0.0 us)
Async XLA Ops:
  1.8 6.4 %collective-permute-start = (f32[9,8,128]{2,1,0:T(8,128)S(1)}, f32[9,8,128]{2,1,0:T(8,128)S(1)}, u32[]{:S(2)}, u32[]{:S(2)}) collective-permute-start(f32[9,8,128]{2,1,0:T(8,128)S(1)} %get-tuple-element.47), channel_id=1, source_target_pairs={{0,1},{1,0},{2,3},{3,2},{4,28},{5,29},{6,30},{7,31},{8,9},{9,8},{1... | collective-permute-start | bytes 110600 | tf_op jit(solution)/shard_map/ppermute | solution.py:385
  4.8 3.7 %collective-permute-start.1 = (f32[9,8,128]{2,1,0:T(8,128)S(1)}, f32[9,8,128]{2,1,0:T(8,128)S(1)}, u32[]{:S(2)}, u32[]{:S(2)}) collective-permute-start(f32[9,8,128]{2,1,0:T(8,128)S(1)} %get-tuple-element.48), channel_id=1, source_target_pairs={{0,24},{1,25},{2,26},{3,27},{4,5},{5,4},{6,7},{7,6},{8,16},{9,17},... | collective-permute-start | bytes 110600 | tf_op jit(solution)/shard_map/ppermute | solution.py:385
  5.5 4.3 %collective-permute-start.2 = (f32[9,8,128]{2,1,0:T(8,128)S(1)}, f32[9,8,128]{2,1,0:T(8,128)S(1)}, u32[]{:S(2)}, u32[]{:S(2)}) collective-permute-start(f32[9,8,128]{2,1,0:T(8,128)S(1)} %get-tuple-element.49), channel_id=1, source_target_pairs={{0,2},{1,3},{2,0},{3,1},{4,12},{5,13},{6,14},{7,15},{8,10},{9,11},... | collective-permute-start | bytes 110600 | tf_op jit(solution)/shard_map/ppermute | solution.py:385
  7.1 2.8 %collective-permute-start.3 = (f32[9,8,128]{2,1,0:T(8,128)S(1)}, f32[9,8,128]{2,1,0:T(8,128)S(1)}, u32[]{:S(2)}, u32[]{:S(2)}) collective-permute-start(f32[9,8,128]{2,1,0:T(8,128)S(1)} %get-tuple-element.50), channel_id=1, source_target_pairs={{0,8},{1,9},{2,4},{3,5},{4,2},{5,3},{6,14},{7,15},{8,0},{9,1},{10,... | collective-permute-start | bytes 110600 | tf_op jit(solution)/shard_map/ppermute | solution.py:385
  7.8 2.1 %collective-permute-start.4 = (f32[9,8,128]{2,1,0:T(8,128)S(1)}, f32[9,8,128]{2,1,0:T(8,128)S(1)}, u32[]{:S(2)}, u32[]{:S(2)}) collective-permute-start(f32[9,8,128]{2,1,0:T(8,128)S(1)} %get-tuple-element.51), channel_id=1, source_target_pairs={{0,8},{1,9},{2,10},{3,11},{4,6},{5,7},{6,4},{7,5},{8,0},{9,1},{10,... | collective-permute-start | bytes 110600 | tf_op jit(solution)/shard_map/ppermute | solution.py:385
  9.9 2.2 %copy-start = (f32[3,8,8,128]{3,2,1,0:T(8,128)S(1)}, f32[3,8,8,128]{3,2,1,0:T(8,128)}, u32[]{:S(2)}) copy-start(f32[3,8,8,128]{3,2,1,0:T(8,128)} %mean_ref.3) | copy-start | bytes 294916
  9.9 2.2 %copy-start.1 = (bf16[128,128]{1,0:T(8,128)(2,1)S(1)}, bf16[128,128]{1,0:T(8,128)(2,1)}, u32[]{:S(2)}) copy-start(bf16[128,128]{1,0:T(8,128)(2,1)} %constant.8.clone.low_ref) | copy-start | bytes 98308
  9.9 2.2 %copy-start.2 = (bf16[128,128]{1,0:T(8,128)(2,1)S(1)}, bf16[128,128]{1,0:T(8,128)(2,1)}, u32[]{:S(2)}) copy-start(bf16[128,128]{1,0:T(8,128)(2,1)} %constant.7.clone.high_ref) | copy-start | bytes 98308
  10.1 2.0 %copy-start.3 = (f32[8,8]{1,0:T(8,128)S(1)}, f32[8,8]{1,0:T(8,128)}, u32[]{:S(2)}) copy-start(f32[8,8]{1,0:T(8,128)} %constant.6.clone.deriv_ref) | copy-start | bytes 772
  10.2 3.4 %collective-permute-start.5 = (f32[7,8,128]{2,1,0:T(8,128)S(1)}, f32[7,8,128]{2,1,0:T(8,128)S(1)}, u32[]{:S(2)}, u32[]{:S(2)}) collective-permute-start(f32[7,8,128]{2,1,0:T(8,128)S(1)} %get-tuple-element.64), channel_id=1, source_target_pairs={{0,24},{8,16},{16,8},{24,0},{1,25},{9,17},{17,9},{25,1},{2,26},{10... | collective-permute-start | bytes 86024 | tf_op jit(solution)/shard_map/ppermute | solution.py:787
  10.2 4.2 %collective-permute-start.6 = (f32[7,8,128]{2,1,0:T(8,128)S(1)}, f32[7,8,128]{2,1,0:T(8,128)S(1)}, u32[]{:S(2)}, u32[]{:S(2)}) collective-permute-start(f32[7,8,128]{2,1,0:T(8,128)S(1)} %get-tuple-element.65), channel_id=1, source_target_pairs={{0,16},{8,24},{16,0},{24,8},{1,17},{9,25},{17,1},{25,9},{2,18},{10... | collective-permute-start | bytes 86024 | tf_op jit(solution)/shard_map/ppermute | solution.py:787
  12.0 2.5 %collective-permute-start.7 = (f32[7,8,128]{2,1,0:T(8,128)S(1)}, f32[7,8,128]{2,1,0:T(8,128)S(1)}, u32[]{:S(2)}, u32[]{:S(2)}) collective-permute-start(f32[7,8,128]{2,1,0:T(8,128)S(1)} %get-tuple-element.66), channel_id=1, source_target_pairs={{0,8},{8,0},{16,24},{24,16},{1,9},{9,1},{17,25},{25,17},{2,10},{10... | collective-permute-start | bytes 86024 | tf_op jit(solution)/shard_map/ppermute | solution.py:787
  14.8 4.1 %collective-permute-start.8 = (f32[9,8,128]{2,1,0:T(8,128)S(1)}, f32[9,8,128]{2,1,0:T(8,128)S(1)}, u32[]{:S(2)}, u32[]{:S(2)}) collective-permute-start(f32[9,8,128]{2,1,0:T(8,128)S(1)} %get-tuple-element.77), channel_id=1, source_target_pairs={{0,1},{1,0},{2,3},{3,2},{4,28},{5,29},{6,30},{7,31},{8,9},{9,8},{1... | collective-permute-start | bytes 110600 | tf_op jit(solution)/shard_map/ppermute | solution.py:385
  15.4 3.7 %collective-permute-start.9 = (f32[9,8,128]{2,1,0:T(8,128)S(1)}, f32[9,8,128]{2,1,0:T(8,128)S(1)}, u32[]{:S(2)}, u32[]{:S(2)}) collective-permute-start(f32[9,8,128]{2,1,0:T(8,128)S(1)} %get-tuple-element.78), channel_id=1, source_target_pairs={{0,24},{1,25},{2,26},{3,27},{4,5},{5,4},{6,7},{7,6},{8,16},{9,17},... | collective-permute-start | bytes 110600 | tf_op jit(solution)/shard_map/ppermute | solution.py:385
  15.4 4.0 %collective-permute-start.10 = (f32[9,8,128]{2,1,0:T(8,128)S(1)}, f32[9,8,128]{2,1,0:T(8,128)S(1)}, u32[]{:S(2)}, u32[]{:S(2)}) collective-permute-start(f32[9,8,128]{2,1,0:T(8,128)S(1)} %get-tuple-element.81), channel_id=1, source_target_pairs={{0,2},{1,3},{2,0},{3,1},{4,12},{5,13},{6,14},{7,15},{8,10},{9,11},... | collective-permute-start | bytes 110600 | tf_op jit(solution)/shard_map/ppermute | solution.py:385
  17.1 2.2 %collective-permute-start.11 = (f32[9,8,128]{2,1,0:T(8,128)S(1)}, f32[9,8,128]{2,1,0:T(8,128)S(1)}, u32[]{:S(2)}, u32[]{:S(2)}) collective-permute-start(f32[9,8,128]{2,1,0:T(8,128)S(1)} %get-tuple-element.82), channel_id=1, source_target_pairs={{0,8},{1,9},{2,4},{3,5},{4,2},{5,3},{6,14},{7,15},{8,0},{9,1},{10,... | collective-permute-start | bytes 110600 | tf_op jit(solution)/shard_map/ppermute | solution.py:385
  18.2 1.2 %collective-permute-start.12 = (f32[9,8,128]{2,1,0:T(8,128)S(1)}, f32[9,8,128]{2,1,0:T(8,128)S(1)}, u32[]{:S(2)}, u32[]{:S(2)}) collective-permute-start(f32[9,8,128]{2,1,0:T(8,128)S(1)} %get-tuple-element.83), channel_id=1, source_target_pairs={{0,8},{1,9},{2,10},{3,11},{4,6},{5,7},{6,4},{7,5},{8,0},{9,1},{10,... | collective-permute-start | bytes 110600 | tf_op jit(solution)/shard_map/ppermute | solution.py:385

commit v3 on v1

--- a/solution.py
+++ b/solution.py
@@ -389,20 +389,27 @@
     return [ref[c] for c in range(ref.shape[0])]
 
 
-def load_kernel(counts, *refs):
-    sources, targets, out_refs, sems = refs[:5], refs[5:10], refs[10:-1], refs[-1]
+def load_kernel(counts, les_hbm, wave_hbm, les_ref, wave_ref, *refs):
+    out_refs, sems = refs[:-1], refs[-1]
+    parts = [
+        (source.at[low:high], target.at[low:high], first + low, high - low)
+        for source, target, low, high, first in (
+            (les_hbm, les_ref, 0, 3, 0),
+            (les_hbm, les_ref, 3, 5, 0),
+            (wave_hbm, wave_ref, 0, 2, 5),
+            (wave_hbm, wave_ref, 2, 4, 5),
+        )
+    ]
     copies = [
         pltpu.make_async_copy(source, target, sems.at[n])
-        for n, (source, target) in enumerate(zip(sources, targets))
+        for n, (source, target, _, _) in enumerate(parts)
     ]
     for copy in copies:
         copy.start()
-    for copy, target, first in zip(copies, targets, (0, 5)):
+    for copy, (_, target, first, count) in zip(copies, parts):
         copy.wait()
-        count = target.shape[0]
-        store_faces(read_all(target), [ref.at[first : first + count] for ref in out_refs], counts)
-    for copy in copies[2:]:
-        copy.wait()
+        fields = [target[c] for c in range(count)]
+        store_faces(fields, [ref.at[first : first + count] for ref in out_refs], counts)
 
 
 def partners(count):
@@ -412,13 +419,42 @@
     return [[(i, (i + turn) % count) for i in range(count)] for turn in turns]
 
 
+def speeds(state):
+    inverse = 1.0 / (state[0] + 1.0)
+    return [state[c] * inverse for c in (1, 2, 3)]
+
+
+def vorticity(les_ref, velocity_ref, vort_ref):
+    velocity = speeds([les_ref[c] for c in range(4)])
+
+    def slope(c, axis):
+        return shifted(velocity[c], axis, 1) - shifted(velocity[c], axis, -1)
+
+    vort = [slope(2, 1) - slope(1, 2), slope(0, 2) - slope(2, 0), slope(1, 0) - slope(0, 1)]
+    for c in range(3):
+        velocity_ref[c] = velocity[c]
+        vort_ref[c] = vort[c]
+
+
 def sending_sets(count):
     return [3, 2, 1, 0] if count == window else list(range(count))
 
 
 def plan_kernel(
-    counts, owner_ref, slot_ref, proj_ref, order_ref, marks_ref, along_x_ref, along_y_ref, tile_ref
+    counts, owner_hbm, slot_hbm, proj_hbm, les_ref, order_ref, marks_ref, along_x_ref, along_y_ref,
+    tile_ref, velocity_ref, vort_ref, owner_ref, slot_ref, proj_ref, sems,
 ):
+    copies = [
+        pltpu.make_async_copy(source, target, sems.at[n])
+        for n, (source, target) in enumerate(
+            ((owner_hbm, owner_ref), (slot_hbm, slot_ref), (proj_hbm, proj_ref))
+        )
+    ]
+    for copy in copies:
+        copy.start()
+    vorticity(les_ref, velocity_ref, vort_ref)
+    for copy in copies:
+        copy.wait()
     count = counts[0]
     n_sets = len(partners(count))
     own = lax.axis_index("gx")
@@ -475,23 +511,6 @@
     tile_ref[1] = tile - high
 
 
-def speeds(state):
-    inverse = 1.0 / (state[0] + 1.0)
-    return [state[c] * inverse for c in (1, 2, 3)]
-
-
-def vorticity_kernel(les_ref, velocity_ref, vort_ref):
-    velocity = speeds([les_ref[c] for c in range(4)])
-
-    def slope(c, axis):
-        return shifted(velocity[c], axis, 1) - shifted(velocity[c], axis, -1)
-
-    vort = [slope(2, 1) - slope(1, 2), slope(0, 2) - slope(2, 0), slope(1, 0) - slope(0, 1)]
-    for c in range(3):
-        velocity_ref[c] = velocity[c]
-        vort_ref[c] = vort[c]
-
-
 def vorticity_z_kernel(counts, present, vort_ref, *refs):
     refs = list(refs)
     face_refs = [refs.pop(0) if here else None for here in present]
@@ -736,33 +755,36 @@
     low = (along_z - high.astype(np.float32)).astype(jnp.bfloat16)
     tables = (deriv, jnp.asarray(high), jnp.asarray(low))
 
-    arguments = (les, wave, owner, slot, projection)
-    les, wave, owner, slot, projection, *sent = call(
+    in_hbm = lambda *arrays: [pltpu.with_memory_space_constraint(a, pltpu.HBM) for a in arrays]
+    les, wave, *sent = call(
         functools.partial(load_kernel, counts),
-        [HBM] * 5,
-        [jax.ShapeDtypeStruct(a.shape, a.dtype) for a in arguments] + faces,
+        [HBM] * 2,
+        [like(5), like(4)] + faces,
         "load_and_faces",
         100000,
-        [pltpu.SemaphoreType.DMA((5,))],
-    )(*(pltpu.with_memory_space_constraint(a, pltpu.HBM) for a in arguments))
+        [pltpu.SemaphoreType.DMA((4,))],
+    )(*in_hbm(les, wave))
     got = exchange(sent, counts)
 
     sets = partners(counts[0])
     n_plans = 4 * ((len(sets) + 3) // 4)
-    order, marks, along_x, along_y, tile = call(
+    small = (owner, slot, projection)
+    order, marks, along_x, along_y, tile, *turning = call(
         functools.partial(plan_kernel, counts),
-        [VMEM] * 3,
+        [HBM] * 3 + [VMEM],
         [
             jax.ShapeDtypeStruct((n_plans, 8, 128), jnp.int32),
             jax.ShapeDtypeStruct((len(sets), 8, 128), f32),
             jax.ShapeDtypeStruct((64, 8, 128), f32),
             jax.ShapeDtypeStruct((8, 8, 128), f32),
             jax.ShapeDtypeStruct((2, 8, 128), f32),
+            like(3),
+            like(3),
         ],
-        "plan",
+        "plan_and_vorticity",
         1000000,
-    )(owner, slot, projection)
-    turning = list(call(vorticity_kernel, [VMEM], [like(3)] * 2, "vorticity", 1000000)(les))
+        [pltpu.VMEM(a.shape, a.dtype) for a in small] + [pltpu.SemaphoreType.DMA((3,))],
+    )(*in_hbm(*small), les)
     z_got = z_faces(got, counts)
     present = [face is not None for face in z_got]
     turning[1] = call(

time: 20.4 us -> 20.5 us (level)
  Pallas kernels: 4.82 us -> 5.56 us
  waiting for transfers between devices: 3.36 us -> 2.71 us
    pallas_call x3 -> x2, Pallas kernels: 1.62 us -> 2.35 us  [the longest x1 1.29 us: local(): call(functools.partial(load_kernel, counts), [HBM] * 2, [like(5), like(4)...]
    ppermute x10, waiting for transfers between devices: 1.81 us -> 1.15 us  [exchange(): lax.ppermute(face, axes, way)]
  transfers between devices with their start and end apart: 13 -> 13, of which waited for: 5 -> 4; matrix products, arithmetic and copies ran while one was open for 0% -> 0% of each run, Pallas kernels for 11% -> 14%
where the time goes in v3:
time: 20.5 us; the launch traced here: 20.3 us
  starting transfers between devices  11.3 us (55%)
  Pallas kernels  5.56 us (27%)
  waiting for transfers between devices  2.71 us (13%)
  between operations  0.76 us (4%)
    ppermute x10, starting transfers between devices, exchange(): lax.ppermute(face, axes, way)  9.34 us
    ppermute x3, starting transfers between devices, local(): moved.append(pieces[k] if still else lax.ppermute(pieces[k], 'gx', sets[k]))  1.94 us
    ppermute x3, waiting for transfers between devices, local(): moved.append(pieces[k] if still else lax.ppermute(pieces[k], 'gx', sets[k]))  1.55 us
    pallas_call x1, Pallas kernels, local(): call(functools.partial(load_kernel, counts), [HBM] * 2, [like(5), like(4)...  1.29 us
    ppermute x10, waiting for transfers between devices, exchange(): lax.ppermute(face, axes, way)  1.15 us
    pallas_call x1, Pallas kernels, local(): call(functools.partial(plan_kernel, counts), [HBM] * 3 + [VMEM], [jax.Sha...  1.06 us
    pallas_call x1, Pallas kernels, local(): call(functools.partial(last_kernel, counts, n_faces), [VMEM] * (3 + n_fac...  0.83 us
    pallas_call x1, Pallas kernels, local(): call(functools.partial(first_kernel, counts, n_faces), [VMEM] * (6 + n_fa...  0.77 us
  transfers between devices with their start and end apart: 13, of which 4 were waited for; matrix products, arithmetic and copies ran while one was open for 0% of the time, Pallas kernels for 14%

profile of v3, /device:TPU:0, one launch (start us, length us, event | category | flops | bytes accessed | tf_op | source)
XLA Modules:
  0.0 20.3 jit_solution(17155386976330977749)
XLA Ops:
  0.6 1.3 %load_and_faces.1 = (f32[5,8,8,128]{3,2,1,0:T(8,128)S(1)}, f32[4,8,8,128]{3,2,1,0:T(8,128)S(1)}, f32[9,8,128]{2,1,0:T(8,128)S(1)}, f32[9,8,128]{2,1,0:T(8,128)S(...) custom-call(f32[5,8,8,128]{3,2,1,0:T(8,128)} %les_hbm.1, f32[4,8,8,128]{3,2,1,0:T(8,128)} %wave_hbm.1), custom_call_target="tpu_custom_call" | custom-call | flops 100000 | bytes 800000 | tf_op jit(solution)/shard_map/load_and_faces/pallas_call | solution.py:759
  1.9 3.0 %collective-permute-start = (f32[9,8,128]{2,1,0:T(8,128)S(1)}, f32[9,8,128]{2,1,0:T(8,128)S(1)}, u32[]{:S(2)}, u32[]{:S(2)}) collective-permute-start(f32[9,8,128]{2,1,0:T(8,128)S(1)} %get-tuple-element.44), channel_id=1, source_target_pairs={{0,1},{1,0},{2,3},{3,2},{4,28},{5,29},{6,30},{7,31},{8,9},{9,8},{1... | collective-permute-start | bytes 110600 | tf_op jit(solution)/shard_map/ppermute | solution.py:385
  4.9 0.7 %collective-permute-start.1 = (f32[9,8,128]{2,1,0:T(8,128)S(1)}, f32[9,8,128]{2,1,0:T(8,128)S(1)}, u32[]{:S(2)}, u32[]{:S(2)}) collective-permute-start(f32[9,8,128]{2,1,0:T(8,128)S(1)} %get-tuple-element.45), channel_id=1, source_target_pairs={{0,24},{1,25},{2,26},{3,27},{4,5},{5,4},{6,7},{7,6},{8,16},{9,17},... | collective-permute-start | bytes 110600 | tf_op jit(solution)/shard_map/ppermute | solution.py:385
  5.6 1.6 %collective-permute-start.2 = (f32[9,8,128]{2,1,0:T(8,128)S(1)}, f32[9,8,128]{2,1,0:T(8,128)S(1)}, u32[]{:S(2)}, u32[]{:S(2)}) collective-permute-start(f32[9,8,128]{2,1,0:T(8,128)S(1)} %get-tuple-element.46), channel_id=1, source_target_pairs={{0,2},{1,3},{2,0},{3,1},{4,12},{5,13},{6,14},{7,15},{8,10},{9,11},... | collective-permute-start | bytes 110600 | tf_op jit(solution)/shard_map/ppermute | solution.py:385
  7.2 0.7 %collective-permute-start.3 = (f32[9,8,128]{2,1,0:T(8,128)S(1)}, f32[9,8,128]{2,1,0:T(8,128)S(1)}, u32[]{:S(2)}, u32[]{:S(2)}) collective-permute-start(f32[9,8,128]{2,1,0:T(8,128)S(1)} %get-tuple-element.47), channel_id=1, source_target_pairs={{0,8},{1,9},{2,4},{3,5},{4,2},{5,3},{6,14},{7,15},{8,0},{9,1},{10,... | collective-permute-start | bytes 110600 | tf_op jit(solution)/shard_map/ppermute | solution.py:385
  7.9 0.0 collective-permute-start.4
  7.9 1.1 %plan_and_vorticity.1 = (s32[4,8,128]{2,1,0:T(8,128)S(1)}, f32[4,8,128]{2,1,0:T(8,128)S(1)}, f32[64,8,128]{2,1,0:T(8,128)S(1)}, f32[8,8,128]{2,1,0:T(8,128)S(1)}...) custom-call(s32[1,1,16]{2,1,0:T(1,128)} %owner_hbm.1, ...), custom_call_target="tpu_custom_call" | custom-call | flops 1000000 | bytes 800000 | tf_op jit(solution)/shard_map/plan_and_vorticity/pallas_call | solution.py:772
  8.9 0.0 collective-permute-done.1.refs_1_
  9.0 0.2 vorticity_z.1.vort_ref
  9.1 0.8 %collective-permute-done.2.refs_2_ = f32[9,8,128]{2,1,0:T(8,128)S(1)} collective-permute-done((f32[9,8,128]{2,1,0:T(8,128)S(1)}, f32[9,8,128]{2,1,0:T(8,128)S(1)}, u32[]{:S(2)}, u32[]{:S(2)}) %collective-permute-start.2) | collective-permute-done | bytes 36896 | tf_op jit(solution)/shard_map/ppermute | solution.py:385
  9.9 0.0 collective-permute-done.3.refs_3_
  10.0 0.0 collective-permute-done.4.refs_4_
  10.0 0.0 copy-start.1
  10.0 0.0 copy-start.2
  10.0 0.3 %lamb_blocks.1 = (f32[7,8,128]{2,1,0:T(8,128)S(1)}, f32[7,8,128]{2,1,0:T(8,128)S(1)}, f32[7,8,128]{2,1,0:T(8,128)S(1)}, f32[7,8,128]{2,1,0:T(8,128)S(1)}) custom-call(s32[4,8,128]{2,1,0:T(8,128)S(1)} %get-tuple-element.52.order_ref, f32[4,8,128]{2,1,0:T(8,128)S(1)} %get-tuple-element.53.marks_ref, f32[64,8,128]{2,1,0:T(8,128)S(1)} %get-tuple-element.54.along_x_ref, ...), custom_call_target="tpu_custom_call" | custom-call | flops 10000000 | bytes 800000 | tf_op jit(solution)/shard_map/lamb_blocks/pallas_call | solution.py:797
  10.2 0.0 copy-start.3
  10.3 0.1 collective-permute-start.5
  10.3 1.7 %collective-permute-start.6 = (f32[7,8,128]{2,1,0:T(8,128)S(1)}, f32[7,8,128]{2,1,0:T(8,128)S(1)}, u32[]{:S(2)}, u32[]{:S(2)}) collective-permute-start(f32[7,8,128]{2,1,0:T(8,128)S(1)} %get-tuple-element.59), channel_id=1, source_target_pairs={{0,16},{8,24},{16,0},{24,8},{1,17},{9,25},{17,1},{25,9},{2,18},{10... | collective-permute-start | bytes 86024 | tf_op jit(solution)/shard_map/ppermute | solution.py:807
  12.1 0.1 collective-permute-start.7
  12.2 0.8 %first_rates.1 = (f32[5,8,8,128]{3,2,1,0:T(8,128)S(1)}, f32[4,8,8,128]{3,2,1,0:T(8,128)S(1)}, f32[6,3,8,128]{3,2,1,0:T(8,128)S(1)}, f32[6,8,128]{2,1,0:T(8,128)S...) custom-call(f32[8,8]{1,0:T(8,128)S(1)} %copy-done.3, ...), custom_call_target="tpu_custom_call" | custom-call | flops 40000000 | bytes 800000 | tf_op jit(solution)/shard_map/first_rates/pallas_call | solution.py:808
  13.0 0.7 %collective-permute-done.5.refs_0_ = f32[7,8,128]{2,1,0:T(8,128)S(1)} collective-permute-done((f32[7,8,128]{2,1,0:T(8,128)S(1)}, f32[7,8,128]{2,1,0:T(8,128)S(1)}, u32[]{:S(2)}, u32[]{:S(2)}) %collective-permute-start.5) | collective-permute-done | bytes 28704 | tf_op jit(solution)/shard_map/ppermute | solution.py:807
  13.6 0.9 %collective-permute-done.6.refs_1_ = f32[7,8,128]{2,1,0:T(8,128)S(1)} collective-permute-done((f32[7,8,128]{2,1,0:T(8,128)S(1)}, f32[7,8,128]{2,1,0:T(8,128)S(1)}, u32[]{:S(2)}, u32[]{:S(2)}) %collective-permute-start.6) | collective-permute-done | bytes 28704 | tf_op jit(solution)/shard_map/ppermute | solution.py:807
  14.5 0.3 %source_and_faces.1 = (f32[3,8,8,128]{3,2,1,0:T(8,128)S(1)}, f32[9,8,128]{2,1,0:T(8,128)S(1)}, f32[9,8,128]{2,1,0:T(8,128)S(1)}, f32[9,8,128]{2,1,0:T(8,128)S(1)...) custom-call(f32[2,8,128]{2,1,0:T(8,128)S(1)} %get-tuple-element.51.tile_ref, ...), custom_call_target="tpu_custom_call" | custom-call | flops 10000000 | bytes 800000 | tf_op jit(solution)/shard_map/source_and_faces/pallas_call | solution.py:816
  14.9 0.6 %collective-permute-start.8 = (f32[9,8,128]{2,1,0:T(8,128)S(1)}, f32[9,8,128]{2,1,0:T(8,128)S(1)}, u32[]{:S(2)}, u32[]{:S(2)}) collective-permute-start(f32[9,8,128]{2,1,0:T(8,128)S(1)} %get-tuple-element.71), channel_id=1, source_target_pairs={{0,1},{1,0},{2,3},{3,2},{4,28},{5,29},{6,30},{7,31},{8,9},{9,8},{1... | collective-permute-start | bytes 110600 | tf_op jit(solution)/shard_map/ppermute | solution.py:385
  15.5 1.7 %collective-permute-start.10 = (f32[9,8,128]{2,1,0:T(8,128)S(1)}, f32[9,8,128]{2,1,0:T(8,128)S(1)}, u32[]{:S(2)}, u32[]{:S(2)}) collective-permute-start(f32[9,8,128]{2,1,0:T(8,128)S(1)} %get-tuple-element.75), channel_id=1, source_target_pairs={{0,2},{1,3},{2,0},{3,1},{4,12},{5,13},{6,14},{7,15},{8,10},{9,11},... | collective-permute-start | bytes 110600 | tf_op jit(solution)/shard_map/ppermute | solution.py:385
  17.2 1.1 %collective-permute-start.11 = (f32[9,8,128]{2,1,0:T(8,128)S(1)}, f32[9,8,128]{2,1,0:T(8,128)S(1)}, u32[]{:S(2)}, u32[]{:S(2)}) collective-permute-start(f32[9,8,128]{2,1,0:T(8,128)S(1)} %get-tuple-element.76), channel_id=1, source_target_pairs={{0,8},{1,9},{2,4},{3,5},{4,2},{5,3},{6,14},{7,15},{8,0},{9,1},{10,... | collective-permute-start | bytes 110600 | tf_op jit(solution)/shard_map/ppermute | solution.py:385
  18.3 0.6 %second_rates_inner.1 = (f32[5,8,8,128]{3,2,1,0:T(8,128)S(1)}, f32[4,8,8,128]{3,2,1,0:T(8,128)S(1)}, f32[3,8,8,128]{3,2,1,0:T(8,128)}) custom-call(f32[8,8]{1,0:T(8,128)S(1)} %copy-done.3, bf16[128,128]{1,0:T(8,128)(2,1)S(1)} %copy-done.1, bf16[128,128]{1,0:T(8,128)(2,1)S(1)} %copy-done.2, f32[5,8,8,128]{3,2,1,0:T(8,128)S(1)} %get-tuple-element.42.les_ref, ...), custom_call_target="tpu_custom_call" | custom-call | flops 40000000 | bytes 800000 | tf_op jit(solution)/shard_map/second_rates_inner/pallas_call | solution.py:824
  19.0 0.2 %collective-permute-done.9.refs_1_ = f32[9,8,128]{2,1,0:T(8,128)S(1)} collective-permute-done((f32[9,8,128]{2,1,0:T(8,128)S(1)}, f32[9,8,128]{2,1,0:T(8,128)S(1)}, u32[]{:S(2)}, u32[]{:S(2)}) %collective-permute-start.9) | collective-permute-done | bytes 36896 | tf_op jit(solution)/shard_map/ppermute | solution.py:385
  19.2 0.2 %second_rates_z.1 = (f32[5,8,8,128]{3,2,1,0:T(8,128)S(1)}, f32[4,8,8,128]{3,2,1,0:T(8,128)S(1)}) custom-call(f32[5,8,8,128]{3,2,1,0:T(8,128)S(1)} %get-tuple-element.68.les_base_ref, f32[4,8,8,128]{3,2,1,0:T(8,128)S(1)} %get-tuple-element.69.wave_base_ref, f32[6,3,8,128]{3,2,1,0:T(8,128)S(1)} %get-tuple-element.70.mean_faces_ref, ...), custom_call_target="tpu_custom_call" | custom-call | flops 1000000 | bytes 800000 | tf_op jit(solution)/shard_map/second_rates_z/pallas_call | solution.py:835
  19.4 0.0 collective-permute-done.10.refs_2_
  19.5 0.0 collective-permute-done.12.refs_4_
  19.5 0.8 %second_rates_outer.1 = (f32[5,8,8,128]{3,2,1,0:T(8,128)}, f32[4,8,8,128]{3,2,1,0:T(8,128)}) custom-call(f32[5,8,8,128]{3,2,1,0:T(8,128)S(1)} %get-tuple-element.73.les_base_ref, f32[4,8,8,128]{3,2,1,0:T(8,128)S(1)} %get-tuple-element.74.wave_base_ref, f32[6,3,8,128]{3,2,1,0:T(8,128)S(1)} %get-tuple-element.70.mean_faces_ref, ...), custom_call_target="tpu_custom_call" | custom-call | flops 4000000 | bytes 800000 | tf_op jit(solution)/shard_map/second_rates_outer/pallas_call | solution.py:842
  (11 shorter events, 0.0 us)
Async XLA Ops:
  1.9 7.0 %collective-permute-start = (f32[9,8,128]{2,1,0:T(8,128)S(1)}, f32[9,8,128]{2,1,0:T(8,128)S(1)}, u32[]{:S(2)}, u32[]{:S(2)}) collective-permute-start(f32[9,8,128]{2,1,0:T(8,128)S(1)} %get-tuple-element.44), channel_id=1, source_target_pairs={{0,1},{1,0},{2,3},{3,2},{4,28},{5,29},{6,30},{7,31},{8,9},{9,8},{1... | collective-permute-start | bytes 110600 | tf_op jit(solution)/shard_map/ppermute | solution.py:385
  4.9 4.0 %collective-permute-start.1 = (f32[9,8,128]{2,1,0:T(8,128)S(1)}, f32[9,8,128]{2,1,0:T(8,128)S(1)}, u32[]{:S(2)}, u32[]{:S(2)}) collective-permute-start(f32[9,8,128]{2,1,0:T(8,128)S(1)} %get-tuple-element.45), channel_id=1, source_target_pairs={{0,24},{1,25},{2,26},{3,27},{4,5},{5,4},{6,7},{7,6},{8,16},{9,17},... | collective-permute-start | bytes 110600 | tf_op jit(solution)/shard_map/ppermute | solution.py:385
  5.6 4.3 %collective-permute-start.2 = (f32[9,8,128]{2,1,0:T(8,128)S(1)}, f32[9,8,128]{2,1,0:T(8,128)S(1)}, u32[]{:S(2)}, u32[]{:S(2)}) collective-permute-start(f32[9,8,128]{2,1,0:T(8,128)S(1)} %get-tuple-element.46), channel_id=1, source_target_pairs={{0,2},{1,3},{2,0},{3,1},{4,12},{5,13},{6,14},{7,15},{8,10},{9,11},... | collective-permute-start | bytes 110600 | tf_op jit(solution)/shard_map/ppermute | solution.py:385
  7.2 2.8 %collective-permute-start.3 = (f32[9,8,128]{2,1,0:T(8,128)S(1)}, f32[9,8,128]{2,1,0:T(8,128)S(1)}, u32[]{:S(2)}, u32[]{:S(2)}) collective-permute-start(f32[9,8,128]{2,1,0:T(8,128)S(1)} %get-tuple-element.47), channel_id=1, source_target_pairs={{0,8},{1,9},{2,4},{3,5},{4,2},{5,3},{6,14},{7,15},{8,0},{9,1},{10,... | collective-permute-start | bytes 110600 | tf_op jit(solution)/shard_map/ppermute | solution.py:385
  7.9 2.1 %collective-permute-start.4 = (f32[9,8,128]{2,1,0:T(8,128)S(1)}, f32[9,8,128]{2,1,0:T(8,128)S(1)}, u32[]{:S(2)}, u32[]{:S(2)}) collective-permute-start(f32[9,8,128]{2,1,0:T(8,128)S(1)} %get-tuple-element.48), channel_id=1, source_target_pairs={{0,8},{1,9},{2,10},{3,11},{4,6},{5,7},{6,4},{7,5},{8,0},{9,1},{10,... | collective-permute-start | bytes 110600 | tf_op jit(solution)/shard_map/ppermute | solution.py:385
  10.0 2.2 %copy-start = (f32[3,8,8,128]{3,2,1,0:T(8,128)S(1)}, f32[3,8,8,128]{3,2,1,0:T(8,128)}, u32[]{:S(2)}) copy-start(f32[3,8,8,128]{3,2,1,0:T(8,128)} %mean_ref.3) | copy-start | bytes 294916
  10.0 2.2 %copy-start.1 = (bf16[128,128]{1,0:T(8,128)(2,1)S(1)}, bf16[128,128]{1,0:T(8,128)(2,1)}, u32[]{:S(2)}) copy-start(bf16[128,128]{1,0:T(8,128)(2,1)} %constant.7.clone.high_ref) | copy-start | bytes 98308
  10.0 2.2 %copy-start.2 = (bf16[128,128]{1,0:T(8,128)(2,1)S(1)}, bf16[128,128]{1,0:T(8,128)(2,1)}, u32[]{:S(2)}) copy-start(bf16[128,128]{1,0:T(8,128)(2,1)} %constant.8.clone.low_ref) | copy-start | bytes 98308
  10.2 2.0 %copy-start.3 = (f32[8,8]{1,0:T(8,128)S(1)}, f32[8,8]{1,0:T(8,128)}, u32[]{:S(2)}) copy-start(f32[8,8]{1,0:T(8,128)} %constant.6.clone.deriv_ref) | copy-start | bytes 772
  10.3 3.4 %collective-permute-start.5 = (f32[7,8,128]{2,1,0:T(8,128)S(1)}, f32[7,8,128]{2,1,0:T(8,128)S(1)}, u32[]{:S(2)}, u32[]{:S(2)}) collective-permute-start(f32[7,8,128]{2,1,0:T(8,128)S(1)} %get-tuple-element.58), channel_id=1, source_target_pairs={{0,24},{8,16},{16,8},{24,0},{1,25},{9,17},{17,9},{25,1},{2,26},{10... | collective-permute-start | bytes 86024 | tf_op jit(solution)/shard_map/ppermute | solution.py:807
  10.3 4.2 %collective-permute-start.6 = (f32[7,8,128]{2,1,0:T(8,128)S(1)}, f32[7,8,128]{2,1,0:T(8,128)S(1)}, u32[]{:S(2)}, u32[]{:S(2)}) collective-permute-start(f32[7,8,128]{2,1,0:T(8,128)S(1)} %get-tuple-element.59), channel_id=1, source_target_pairs={{0,16},{8,24},{16,0},{24,8},{1,17},{9,25},{17,1},{25,9},{2,18},{10... | collective-permute-start | bytes 86024 | tf_op jit(solution)/shard_map/ppermute | solution.py:807
  12.1 2.5 %collective-permute-start.7 = (f32[7,8,128]{2,1,0:T(8,128)S(1)}, f32[7,8,128]{2,1,0:T(8,128)S(1)}, u32[]{:S(2)}, u32[]{:S(2)}) collective-permute-start(f32[7,8,128]{2,1,0:T(8,128)S(1)} %get-tuple-element.60), channel_id=1, source_target_pairs={{0,8},{8,0},{16,24},{24,16},{1,9},{9,1},{17,25},{25,17},{2,10},{10... | collective-permute-start | bytes 86024 | tf_op jit(solution)/shard_map/ppermute | solution.py:807
  14.9 4.1 %collective-permute-start.8 = (f32[9,8,128]{2,1,0:T(8,128)S(1)}, f32[9,8,128]{2,1,0:T(8,128)S(1)}, u32[]{:S(2)}, u32[]{:S(2)}) collective-permute-start(f32[9,8,128]{2,1,0:T(8,128)S(1)} %get-tuple-element.71), channel_id=1, source_target_pairs={{0,1},{1,0},{2,3},{3,2},{4,28},{5,29},{6,30},{7,31},{8,9},{9,8},{1... | collective-permute-start | bytes 110600 | tf_op jit(solution)/shard_map/ppermute | solution.py:385
  15.5 3.7 %collective-permute-start.9 = (f32[9,8,128]{2,1,0:T(8,128)S(1)}, f32[9,8,128]{2,1,0:T(8,128)S(1)}, u32[]{:S(2)}, u32[]{:S(2)}) collective-permute-start(f32[9,8,128]{2,1,0:T(8,128)S(1)} %get-tuple-element.72), channel_id=1, source_target_pairs={{0,24},{1,25},{2,26},{3,27},{4,5},{5,4},{6,7},{7,6},{8,16},{9,17},... | collective-permute-start | bytes 110600 | tf_op jit(solution)/shard_map/ppermute | solution.py:385
  15.5 4.0 %collective-permute-start.10 = (f32[9,8,128]{2,1,0:T(8,128)S(1)}, f32[9,8,128]{2,1,0:T(8,128)S(1)}, u32[]{:S(2)}, u32[]{:S(2)}) collective-permute-start(f32[9,8,128]{2,1,0:T(8,128)S(1)} %get-tuple-element.75), channel_id=1, source_target_pairs={{0,2},{1,3},{2,0},{3,1},{4,12},{5,13},{6,14},{7,15},{8,10},{9,11},... | collective-permute-start | bytes 110600 | tf_op jit(solution)/shard_map/ppermute | solution.py:385
  17.2 2.2 %collective-permute-start.11 = (f32[9,8,128]{2,1,0:T(8,128)S(1)}, f32[9,8,128]{2,1,0:T(8,128)S(1)}, u32[]{:S(2)}, u32[]{:S(2)}) collective-permute-start(f32[9,8,128]{2,1,0:T(8,128)S(1)} %get-tuple-element.76), channel_id=1, source_target_pairs={{0,8},{1,9},{2,4},{3,5},{4,2},{5,3},{6,14},{7,15},{8,0},{9,1},{10,... | collective-permute-start | bytes 110600 | tf_op jit(solution)/shard_map/ppermute | solution.py:385
  18.3 1.2 %collective-permute-start.12 = (f32[9,8,128]{2,1,0:T(8,128)S(1)}, f32[9,8,128]{2,1,0:T(8,128)S(1)}, u32[]{:S(2)}, u32[]{:S(2)}) collective-permute-start(f32[9,8,128]{2,1,0:T(8,128)S(1)} %get-tuple-element.77), channel_id=1, source_target_pairs={{0,8},{1,9},{2,10},{3,11},{4,6},{5,7},{6,4},{7,5},{8,0},{9,1},{10,... | collective-permute-start | bytes 110600 | tf_op jit(solution)/shard_map/ppermute | solution.py:385

commit v4 on v1

--- a/solution.py
+++ b/solution.py
@@ -397,12 +397,9 @@
     ]
     for copy in copies:
         copy.start()
-    for copy, target, first in zip(copies, targets, (0, 5)):
+    for copy in copies:
         copy.wait()
-        count = target.shape[0]
-        store_faces(read_all(target), [ref.at[first : first + count] for ref in out_refs], counts)
-    for copy in copies[2:]:
-        copy.wait()
+    store_faces(read_all(targets[0]) + read_all(targets[1]), out_refs, counts)
 
 
 def partners(count):
@@ -688,16 +685,19 @@
     face_refs, (les_out, wave_out, les_ref, wave_ref, sems) = (
         refs[:n_faces], refs[n_faces:],
     )
-    copies = []
+    copies = [
+        pltpu.make_async_copy(les_ref, les_out, sems.at[0]),
+        pltpu.make_async_copy(wave_ref, wave_out, sems.at[1]),
+    ]
 
     def put(c, planes):
-        kept, target = (les_ref.at[c], les_out.at[c]) if c < 5 else (
-            wave_ref.at[c - 5], wave_out.at[c - 5]
-        )
         for x, plane in enumerate(planes):
-            kept[x] = plane
-        copies.append(pltpu.make_async_copy(kept, target, sems.at[c]))
-        copies[-1].start()
+            if c < 5:
+                les_ref[c, x] = plane
+            else:
+                wave_ref[c - 5, x] = plane
+        if c in (4, 8):
+            copies[c // 8].start()
 
     add_layers(counts, (0, 1), face_refs, mean_faces_ref, les_base_ref, wave_base_ref, put)
     for copy in copies:
@@ -826,7 +826,7 @@
         [
             pltpu.VMEM(les.shape, f32),
             pltpu.VMEM(wave.shape, f32),
-            pltpu.SemaphoreType.DMA((9,)),
+            pltpu.SemaphoreType.DMA((2,)),
         ],
         out_spec=[HBM, HBM],
     )(les_base, wave_base, mean_faces, *got)

time: 20.4 us -> 20.4 us (level)
  no operation moved by 1% of the time
where the time goes in v4:
time: 20.4 us; the launch traced here: 20.2 us
  starting transfers between devices  11.3 us (55%)
  Pallas kernels  4.81 us (24%)
  waiting for transfers between devices  3.36 us (16%)
  between operations  0.75 us (4%)
    ppermute x10, starting transfers between devices, exchange(): lax.ppermute(face, axes, way)  9.33 us
    ppermute x3, starting transfers between devices, local(): moved.append(pieces[k] if still else lax.ppermute(pieces[k], 'gx', sets[k]))  1.94 us
    ppermute x10, waiting for transfers between devices, exchange(): lax.ppermute(face, axes, way)  1.81 us
    ppermute x3, waiting for transfers between devices, local(): moved.append(pieces[k] if still else lax.ppermute(pieces[k], 'gx', sets[k]))  1.55 us
    pallas_call x1, Pallas kernels, local(): call(functools.partial(load_kernel, counts), [HBM] * 5, [jax.ShapeDtypeSt...  1.21 us
    pallas_call x1, Pallas kernels, local(): call(functools.partial(last_kernel, counts, n_faces), [VMEM] * (3 + n_fac...  0.8 us
    pallas_call x1, Pallas kernels, local(): call(functools.partial(first_kernel, counts, n_faces), [VMEM] * (6 + n_fa...  0.77 us
    pallas_call x1, Pallas kernels, local(): call(inner_kernel, [VMEM] * 9, [like(5), like(4), like(3)], 'second_rates...  0.65 us
  transfers between devices with their start and end apart: 13, of which 5 were waited for; matrix products, arithmetic and copies ran while one was open for 0% of the time, Pallas kernels for 11%

profile of v4, /device:TPU:0, one launch (start us, length us, event | category | flops | bytes accessed | tf_op | source)
XLA Modules:
  0.0 20.2 jit_solution(6591783255426171317)
XLA Ops:
  0.6 1.2 %load_and_faces.1 = (f32[5,8,8,128]{3,2,1,0:T(8,128)S(1)}, f32[4,8,8,128]{3,2,1,0:T(8,128)S(1)}, s32[1,1,16]{2,1,0:T(1,128)S(1)}, s32[1,1,16]{2,1,0:T(1,128)S(1)...) custom-call(f32[5,8,8,128]{3,2,1,0:T(8,128)} %refs_0_.1, ...), custom_call_target="tpu_custom_call" | custom-call | flops 100000 | bytes 800000 | tf_op jit(solution)/shard_map/load_and_faces/pallas_call | solution.py:740
  1.8 3.0 %collective-permute-start = (f32[9,8,128]{2,1,0:T(8,128)S(1)}, f32[9,8,128]{2,1,0:T(8,128)S(1)}, u32[]{:S(2)}, u32[]{:S(2)}) collective-permute-start(f32[9,8,128]{2,1,0:T(8,128)S(1)} %get-tuple-element.47), channel_id=1, source_target_pairs={{0,1},{1,0},{2,3},{3,2},{4,28},{5,29},{6,30},{7,31},{8,9},{9,8},{1... | collective-permute-start | bytes 110600 | tf_op jit(solution)/shard_map/ppermute | solution.py:385
  4.9 0.7 %collective-permute-start.1 = (f32[9,8,128]{2,1,0:T(8,128)S(1)}, f32[9,8,128]{2,1,0:T(8,128)S(1)}, u32[]{:S(2)}, u32[]{:S(2)}) collective-permute-start(f32[9,8,128]{2,1,0:T(8,128)S(1)} %get-tuple-element.48), channel_id=1, source_target_pairs={{0,24},{1,25},{2,26},{3,27},{4,5},{5,4},{6,7},{7,6},{8,16},{9,17},... | collective-permute-start | bytes 110600 | tf_op jit(solution)/shard_map/ppermute | solution.py:385
  5.5 1.6 %collective-permute-start.2 = (f32[9,8,128]{2,1,0:T(8,128)S(1)}, f32[9,8,128]{2,1,0:T(8,128)S(1)}, u32[]{:S(2)}, u32[]{:S(2)}) collective-permute-start(f32[9,8,128]{2,1,0:T(8,128)S(1)} %get-tuple-element.49), channel_id=1, source_target_pairs={{0,2},{1,3},{2,0},{3,1},{4,12},{5,13},{6,14},{7,15},{8,10},{9,11},... | collective-permute-start | bytes 110600 | tf_op jit(solution)/shard_map/ppermute | solution.py:385
  7.1 0.7 %collective-permute-start.3 = (f32[9,8,128]{2,1,0:T(8,128)S(1)}, f32[9,8,128]{2,1,0:T(8,128)S(1)}, u32[]{:S(2)}, u32[]{:S(2)}) collective-permute-start(f32[9,8,128]{2,1,0:T(8,128)S(1)} %get-tuple-element.50), channel_id=1, source_target_pairs={{0,8},{1,9},{2,4},{3,5},{4,2},{5,3},{6,14},{7,15},{8,0},{9,1},{10,... | collective-permute-start | bytes 110600 | tf_op jit(solution)/shard_map/ppermute | solution.py:385
  7.8 0.1 vorticity.1
  7.9 0.3 %plan.1 = (s32[4,8,128]{2,1,0:T(8,128)S(1)}, f32[4,8,128]{2,1,0:T(8,128)S(1)}, f32[64,8,128]{2,1,0:T(8,128)S(1)}, f32[8,8,128]{2,1,0:T(8,128)S(1)}, f32[2,8,128]{2,1,0:T(8,128)S(1)}) custom-call(s32[1,1,16]{2,1,0:T(1,128)S(1)} %get-tuple-element.54.owner_ref, s32[1,1,16]{2,1,0:T(1,128)S(1)} %get-tuple-element.55.slot_ref, f32[8,8]{1,0:T(8,128)S(1)} %get-tuple-element.56.proj_ref), custom_call_target="tpu_custom_call" | custom-call | flops 1000000 | bytes 800000 | tf_op jit(solution)/shard_map/plan/pallas_call | solution.py:752
  8.2 0.0 collective-permute-done.refs_0_
  8.2 0.3 %collective-permute-done.1.refs_1_ = f32[9,8,128]{2,1,0:T(8,128)S(1)} collective-permute-done((f32[9,8,128]{2,1,0:T(8,128)S(1)}, f32[9,8,128]{2,1,0:T(8,128)S(1)}, u32[]{:S(2)}, u32[]{:S(2)}) %collective-permute-start.1) | collective-permute-done | bytes 36896 | tf_op jit(solution)/shard_map/ppermute | solution.py:385
  8.6 0.2 vorticity_z.1.vort_ref
  8.7 1.1 %collective-permute-done.2.refs_2_ = f32[9,8,128]{2,1,0:T(8,128)S(1)} collective-permute-done((f32[9,8,128]{2,1,0:T(8,128)S(1)}, f32[9,8,128]{2,1,0:T(8,128)S(1)}, u32[]{:S(2)}, u32[]{:S(2)}) %collective-permute-start.2) | collective-permute-done | bytes 36896 | tf_op jit(solution)/shard_map/ppermute | solution.py:385
  9.9 0.0 collective-permute-done.4.refs_4_
  9.9 0.0 copy-start.1
  9.9 0.0 copy-start.2
  9.9 0.3 %lamb_blocks.1 = (f32[7,8,128]{2,1,0:T(8,128)S(1)}, f32[7,8,128]{2,1,0:T(8,128)S(1)}, f32[7,8,128]{2,1,0:T(8,128)S(1)}, f32[7,8,128]{2,1,0:T(8,128)S(1)}) custom-call(s32[4,8,128]{2,1,0:T(8,128)S(1)} %get-tuple-element.58.order_ref, f32[4,8,128]{2,1,0:T(8,128)S(1)} %get-tuple-element.59.marks_ref, f32[64,8,128]{2,1,0:T(8,128)S(1)} %get-tuple-element.60.along_x_ref, ...), custom_call_target="tpu_custom_call" | custom-call | flops 10000000 | bytes 800000 | tf_op jit(solution)/shard_map/lamb_blocks/pallas_call | solution.py:775
  10.2 0.0 copy-start.3
  10.2 0.1 collective-permute-start.5
  10.3 1.7 %collective-permute-start.6 = (f32[7,8,128]{2,1,0:T(8,128)S(1)}, f32[7,8,128]{2,1,0:T(8,128)S(1)}, u32[]{:S(2)}, u32[]{:S(2)}) collective-permute-start(f32[7,8,128]{2,1,0:T(8,128)S(1)} %get-tuple-element.65), channel_id=1, source_target_pairs={{0,16},{8,24},{16,0},{24,8},{1,17},{9,25},{17,1},{25,9},{2,18},{10... | collective-permute-start | bytes 86024 | tf_op jit(solution)/shard_map/ppermute | solution.py:785
  12.0 0.1 collective-permute-start.7
  12.1 0.8 %first_rates.1 = (f32[5,8,8,128]{3,2,1,0:T(8,128)S(1)}, f32[4,8,8,128]{3,2,1,0:T(8,128)S(1)}, f32[6,3,8,128]{3,2,1,0:T(8,128)S(1)}, f32[6,8,128]{2,1,0:T(8,128)S...) custom-call(f32[8,8]{1,0:T(8,128)S(1)} %copy-done.3, ...), custom_call_target="tpu_custom_call" | custom-call | flops 40000000 | bytes 800000 | tf_op jit(solution)/shard_map/first_rates/pallas_call | solution.py:786
  12.9 0.7 %collective-permute-done.5.refs_0_ = f32[7,8,128]{2,1,0:T(8,128)S(1)} collective-permute-done((f32[7,8,128]{2,1,0:T(8,128)S(1)}, f32[7,8,128]{2,1,0:T(8,128)S(1)}, u32[]{:S(2)}, u32[]{:S(2)}) %collective-permute-start.5) | collective-permute-done | bytes 28704 | tf_op jit(solution)/shard_map/ppermute | solution.py:785
  13.6 0.9 %collective-permute-done.6.refs_1_ = f32[7,8,128]{2,1,0:T(8,128)S(1)} collective-permute-done((f32[7,8,128]{2,1,0:T(8,128)S(1)}, f32[7,8,128]{2,1,0:T(8,128)S(1)}, u32[]{:S(2)}, u32[]{:S(2)}) %collective-permute-start.6) | collective-permute-done | bytes 28704 | tf_op jit(solution)/shard_map/ppermute | solution.py:785
  14.5 0.3 %source_and_faces.1 = (f32[3,8,8,128]{3,2,1,0:T(8,128)S(1)}, f32[9,8,128]{2,1,0:T(8,128)S(1)}, f32[9,8,128]{2,1,0:T(8,128)S(1)}, f32[9,8,128]{2,1,0:T(8,128)S(1)...) custom-call(f32[2,8,128]{2,1,0:T(8,128)S(1)} %get-tuple-element.57.tile_ref, ...), custom_call_target="tpu_custom_call" | custom-call | flops 10000000 | bytes 800000 | tf_op jit(solution)/shard_map/source_and_faces/pallas_call | solution.py:794
  14.8 0.6 %collective-permute-start.8 = (f32[9,8,128]{2,1,0:T(8,128)S(1)}, f32[9,8,128]{2,1,0:T(8,128)S(1)}, u32[]{:S(2)}, u32[]{:S(2)}) collective-permute-start(f32[9,8,128]{2,1,0:T(8,128)S(1)} %get-tuple-element.77), channel_id=1, source_target_pairs={{0,1},{1,0},{2,3},{3,2},{4,28},{5,29},{6,30},{7,31},{8,9},{9,8},{1... | collective-permute-start | bytes 110600 | tf_op jit(solution)/shard_map/ppermute | solution.py:385
  15.4 1.7 %collective-permute-start.10 = (f32[9,8,128]{2,1,0:T(8,128)S(1)}, f32[9,8,128]{2,1,0:T(8,128)S(1)}, u32[]{:S(2)}, u32[]{:S(2)}) collective-permute-start(f32[9,8,128]{2,1,0:T(8,128)S(1)} %get-tuple-element.81), channel_id=1, source_target_pairs={{0,2},{1,3},{2,0},{3,1},{4,12},{5,13},{6,14},{7,15},{8,10},{9,11},... | collective-permute-start | bytes 110600 | tf_op jit(solution)/shard_map/ppermute | solution.py:385
  17.1 1.1 %collective-permute-start.11 = (f32[9,8,128]{2,1,0:T(8,128)S(1)}, f32[9,8,128]{2,1,0:T(8,128)S(1)}, u32[]{:S(2)}, u32[]{:S(2)}) collective-permute-start(f32[9,8,128]{2,1,0:T(8,128)S(1)} %get-tuple-element.82), channel_id=1, source_target_pairs={{0,8},{1,9},{2,4},{3,5},{4,2},{5,3},{6,14},{7,15},{8,0},{9,1},{10,... | collective-permute-start | bytes 110600 | tf_op jit(solution)/shard_map/ppermute | solution.py:385
  18.2 0.6 %second_rates_inner.1 = (f32[5,8,8,128]{3,2,1,0:T(8,128)S(1)}, f32[4,8,8,128]{3,2,1,0:T(8,128)S(1)}, f32[3,8,8,128]{3,2,1,0:T(8,128)}) custom-call(f32[8,8]{1,0:T(8,128)S(1)} %copy-done.3, bf16[128,128]{1,0:T(8,128)(2,1)S(1)} %copy-done.2, bf16[128,128]{1,0:T(8,128)(2,1)S(1)} %copy-done.1, f32[5,8,8,128]{3,2,1,0:T(8,128)S(1)} %get-tuple-element.45.les_ref, ...), custom_call_target="tpu_custom_call" | custom-call | flops 40000000 | bytes 800000 | tf_op jit(solution)/shard_map/second_rates_inner/pallas_call | solution.py:802
  18.9 0.2 %collective-permute-done.9.refs_1_ = f32[9,8,128]{2,1,0:T(8,128)S(1)} collective-permute-done((f32[9,8,128]{2,1,0:T(8,128)S(1)}, f32[9,8,128]{2,1,0:T(8,128)S(1)}, u32[]{:S(2)}, u32[]{:S(2)}) %collective-permute-start.9) | collective-permute-done | bytes 36896 | tf_op jit(solution)/shard_map/ppermute | solution.py:385
  19.1 0.2 %second_rates_z.1 = (f32[5,8,8,128]{3,2,1,0:T(8,128)S(1)}, f32[4,8,8,128]{3,2,1,0:T(8,128)S(1)}) custom-call(f32[5,8,8,128]{3,2,1,0:T(8,128)S(1)} %get-tuple-element.74.les_base_ref, f32[4,8,8,128]{3,2,1,0:T(8,128)S(1)} %get-tuple-element.75.wave_base_ref, f32[6,3,8,128]{3,2,1,0:T(8,128)S(1)} %get-tuple-element.76.mean_faces_ref, ...), custom_call_target="tpu_custom_call" | custom-call | flops 1000000 | bytes 800000 | tf_op jit(solution)/shard_map/second_rates_z/pallas_call | solution.py:813
  19.3 0.0 collective-permute-done.10.refs_2_
  19.4 0.0 collective-permute-done.12.refs_4_
  19.4 0.8 %second_rates_outer.1 = (f32[5,8,8,128]{3,2,1,0:T(8,128)}, f32[4,8,8,128]{3,2,1,0:T(8,128)}) custom-call(f32[5,8,8,128]{3,2,1,0:T(8,128)S(1)} %get-tuple-element.79.les_base_ref, f32[4,8,8,128]{3,2,1,0:T(8,128)S(1)} %get-tuple-element.80.wave_base_ref, f32[6,3,8,128]{3,2,1,0:T(8,128)S(1)} %get-tuple-element.76.mean_faces_ref, ...), custom_call_target="tpu_custom_call" | custom-call | flops 4000000 | bytes 800000 | tf_op jit(solution)/shard_map/second_rates_outer/pallas_call | solution.py:820
  (12 shorter events, 0.0 us)
Async XLA Ops:
  1.8 6.4 %collective-permute-start = (f32[9,8,128]{2,1,0:T(8,128)S(1)}, f32[9,8,128]{2,1,0:T(8,128)S(1)}, u32[]{:S(2)}, u32[]{:S(2)}) collective-permute-start(f32[9,8,128]{2,1,0:T(8,128)S(1)} %get-tuple-element.47), channel_id=1, source_target_pairs={{0,1},{1,0},{2,3},{3,2},{4,28},{5,29},{6,30},{7,31},{8,9},{9,8},{1... | collective-permute-start | bytes 110600 | tf_op jit(solution)/shard_map/ppermute | solution.py:385
  4.9 3.7 %collective-permute-start.1 = (f32[9,8,128]{2,1,0:T(8,128)S(1)}, f32[9,8,128]{2,1,0:T(8,128)S(1)}, u32[]{:S(2)}, u32[]{:S(2)}) collective-permute-start(f32[9,8,128]{2,1,0:T(8,128)S(1)} %get-tuple-element.48), channel_id=1, source_target_pairs={{0,24},{1,25},{2,26},{3,27},{4,5},{5,4},{6,7},{7,6},{8,16},{9,17},... | collective-permute-start | bytes 110600 | tf_op jit(solution)/shard_map/ppermute | solution.py:385
  5.5 4.3 %collective-permute-start.2 = (f32[9,8,128]{2,1,0:T(8,128)S(1)}, f32[9,8,128]{2,1,0:T(8,128)S(1)}, u32[]{:S(2)}, u32[]{:S(2)}) collective-permute-start(f32[9,8,128]{2,1,0:T(8,128)S(1)} %get-tuple-element.49), channel_id=1, source_target_pairs={{0,2},{1,3},{2,0},{3,1},{4,12},{5,13},{6,14},{7,15},{8,10},{9,11},... | collective-permute-start | bytes 110600 | tf_op jit(solution)/shard_map/ppermute | solution.py:385
  7.1 2.8 %collective-permute-start.3 = (f32[9,8,128]{2,1,0:T(8,128)S(1)}, f32[9,8,128]{2,1,0:T(8,128)S(1)}, u32[]{:S(2)}, u32[]{:S(2)}) collective-permute-start(f32[9,8,128]{2,1,0:T(8,128)S(1)} %get-tuple-element.50), channel_id=1, source_target_pairs={{0,8},{1,9},{2,4},{3,5},{4,2},{5,3},{6,14},{7,15},{8,0},{9,1},{10,... | collective-permute-start | bytes 110600 | tf_op jit(solution)/shard_map/ppermute | solution.py:385
  7.8 2.1 %collective-permute-start.4 = (f32[9,8,128]{2,1,0:T(8,128)S(1)}, f32[9,8,128]{2,1,0:T(8,128)S(1)}, u32[]{:S(2)}, u32[]{:S(2)}) collective-permute-start(f32[9,8,128]{2,1,0:T(8,128)S(1)} %get-tuple-element.51), channel_id=1, source_target_pairs={{0,8},{1,9},{2,10},{3,11},{4,6},{5,7},{6,4},{7,5},{8,0},{9,1},{10,... | collective-permute-start | bytes 110600 | tf_op jit(solution)/shard_map/ppermute | solution.py:385
  9.9 2.2 %copy-start = (f32[3,8,8,128]{3,2,1,0:T(8,128)S(1)}, f32[3,8,8,128]{3,2,1,0:T(8,128)}, u32[]{:S(2)}) copy-start(f32[3,8,8,128]{3,2,1,0:T(8,128)} %mean_ref.3) | copy-start | bytes 294916
  9.9 2.2 %copy-start.1 = (bf16[128,128]{1,0:T(8,128)(2,1)S(1)}, bf16[128,128]{1,0:T(8,128)(2,1)}, u32[]{:S(2)}) copy-start(bf16[128,128]{1,0:T(8,128)(2,1)} %constant.8.clone.low_ref) | copy-start | bytes 98308
  9.9 2.2 %copy-start.2 = (bf16[128,128]{1,0:T(8,128)(2,1)S(1)}, bf16[128,128]{1,0:T(8,128)(2,1)}, u32[]{:S(2)}) copy-start(bf16[128,128]{1,0:T(8,128)(2,1)} %constant.7.clone.high_ref) | copy-start | bytes 98308
  10.2 2.0 %copy-start.3 = (f32[8,8]{1,0:T(8,128)S(1)}, f32[8,8]{1,0:T(8,128)}, u32[]{:S(2)}) copy-start(f32[8,8]{1,0:T(8,128)} %constant.6.clone.deriv_ref) | copy-start | bytes 772
  10.2 3.4 %collective-permute-start.5 = (f32[7,8,128]{2,1,0:T(8,128)S(1)}, f32[7,8,128]{2,1,0:T(8,128)S(1)}, u32[]{:S(2)}, u32[]{:S(2)}) collective-permute-start(f32[7,8,128]{2,1,0:T(8,128)S(1)} %get-tuple-element.64), channel_id=1, source_target_pairs={{0,24},{8,16},{16,8},{24,0},{1,25},{9,17},{17,9},{25,1},{2,26},{10... | collective-permute-start | bytes 86024 | tf_op jit(solution)/shard_map/ppermute | solution.py:785
  10.3 4.2 %collective-permute-start.6 = (f32[7,8,128]{2,1,0:T(8,128)S(1)}, f32[7,8,128]{2,1,0:T(8,128)S(1)}, u32[]{:S(2)}, u32[]{:S(2)}) collective-permute-start(f32[7,8,128]{2,1,0:T(8,128)S(1)} %get-tuple-element.65), channel_id=1, source_target_pairs={{0,16},{8,24},{16,0},{24,8},{1,17},{9,25},{17,1},{25,9},{2,18},{10... | collective-permute-start | bytes 86024 | tf_op jit(solution)/shard_map/ppermute | solution.py:785
  12.0 2.5 %collective-permute-start.7 = (f32[7,8,128]{2,1,0:T(8,128)S(1)}, f32[7,8,128]{2,1,0:T(8,128)S(1)}, u32[]{:S(2)}, u32[]{:S(2)}) collective-permute-start(f32[7,8,128]{2,1,0:T(8,128)S(1)} %get-tuple-element.66), channel_id=1, source_target_pairs={{0,8},{8,0},{16,24},{24,16},{1,9},{9,1},{17,25},{25,17},{2,10},{10... | collective-permute-start | bytes 86024 | tf_op jit(solution)/shard_map/ppermute | solution.py:785
  14.8 4.1 %collective-permute-start.8 = (f32[9,8,128]{2,1,0:T(8,128)S(1)}, f32[9,8,128]{2,1,0:T(8,128)S(1)}, u32[]{:S(2)}, u32[]{:S(2)}) collective-permute-start(f32[9,8,128]{2,1,0:T(8,128)S(1)} %get-tuple-element.77), channel_id=1, source_target_pairs={{0,1},{1,0},{2,3},{3,2},{4,28},{5,29},{6,30},{7,31},{8,9},{9,8},{1... | collective-permute-start | bytes 110600 | tf_op jit(solution)/shard_map/ppermute | solution.py:385
  15.4 3.7 %collective-permute-start.9 = (f32[9,8,128]{2,1,0:T(8,128)S(1)}, f32[9,8,128]{2,1,0:T(8,128)S(1)}, u32[]{:S(2)}, u32[]{:S(2)}) collective-permute-start(f32[9,8,128]{2,1,0:T(8,128)S(1)} %get-tuple-element.78), channel_id=1, source_target_pairs={{0,24},{1,25},{2,26},{3,27},{4,5},{5,4},{6,7},{7,6},{8,16},{9,17},... | collective-permute-start | bytes 110600 | tf_op jit(solution)/shard_map/ppermute | solution.py:385
  15.4 4.0 %collective-permute-start.10 = (f32[9,8,128]{2,1,0:T(8,128)S(1)}, f32[9,8,128]{2,1,0:T(8,128)S(1)}, u32[]{:S(2)}, u32[]{:S(2)}) collective-permute-start(f32[9,8,128]{2,1,0:T(8,128)S(1)} %get-tuple-element.81), channel_id=1, source_target_pairs={{0,2},{1,3},{2,0},{3,1},{4,12},{5,13},{6,14},{7,15},{8,10},{9,11},... | collective-permute-start | bytes 110600 | tf_op jit(solution)/shard_map/ppermute | solution.py:385
  17.1 2.2 %collective-permute-start.11 = (f32[9,8,128]{2,1,0:T(8,128)S(1)}, f32[9,8,128]{2,1,0:T(8,128)S(1)}, u32[]{:S(2)}, u32[]{:S(2)}) collective-permute-start(f32[9,8,128]{2,1,0:T(8,128)S(1)} %get-tuple-element.82), channel_id=1, source_target_pairs={{0,8},{1,9},{2,4},{3,5},{4,2},{5,3},{6,14},{7,15},{8,0},{9,1},{10,... | collective-permute-start | bytes 110600 | tf_op jit(solution)/shard_map/ppermute | solution.py:385
  18.2 1.2 %collective-permute-start.12 = (f32[9,8,128]{2,1,0:T(8,128)S(1)}, f32[9,8,128]{2,1,0:T(8,128)S(1)}, u32[]{:S(2)}, u32[]{:S(2)}) collective-permute-start(f32[9,8,128]{2,1,0:T(8,128)S(1)} %get-tuple-element.83), channel_id=1, source_target_pairs={{0,8},{1,9},{2,10},{3,11},{4,6},{5,7},{6,4},{7,5},{8,0},{9,1},{10,... | collective-permute-start | bytes 110600 | tf_op jit(solution)/shard_map/ppermute | solution.py:385

commit v5 on v4

--- a/solution.py
+++ b/solution.py
@@ -397,9 +397,12 @@
     ]
     for copy in copies:
         copy.start()
-    for copy in copies:
+    for copy, target, first in zip(copies, targets, (0, 5)):
         copy.wait()
-    store_faces(read_all(targets[0]) + read_all(targets[1]), out_refs, counts)
+        count = target.shape[0]
+        store_faces(read_all(target), [ref.at[first : first + count] for ref in out_refs], counts)
+    for copy in copies[2:]:
+        copy.wait()
 
 
 def partners(count):

time: 20.4 us -> 20.3 us (level)
  no operation moved by 1% of the time
where the time goes in v5:
time: 20.3 us; the launch traced here: 20.2 us
  starting transfers between devices  11.3 us (56%)
  Pallas kernels  4.79 us (24%)
  waiting for transfers between devices  3.36 us (17%)
  between operations  0.75 us (4%)
    ppermute x10, starting transfers between devices, exchange(): lax.ppermute(face, axes, way)  9.33 us
    ppermute x3, starting transfers between devices, local(): moved.append(pieces[k] if still else lax.ppermute(pieces[k], 'gx', sets[k]))  1.94 us
    ppermute x10, waiting for transfers between devices, exchange(): lax.ppermute(face, axes, way)  1.81 us
    ppermute x3, waiting for transfers between devices, local(): moved.append(pieces[k] if still else lax.ppermute(pieces[k], 'gx', sets[k]))  1.55 us
    pallas_call x1, Pallas kernels, local(): call(functools.partial(load_kernel, counts), [HBM] * 5, [jax.ShapeDtypeSt...  1.19 us
    pallas_call x1, Pallas kernels, local(): call(functools.partial(last_kernel, counts, n_faces), [VMEM] * (3 + n_fac...  0.8 us
    pallas_call x1, Pallas kernels, local(): call(functools.partial(first_kernel, counts, n_faces), [VMEM] * (6 + n_fa...  0.77 us
    pallas_call x1, Pallas kernels, local(): call(inner_kernel, [VMEM] * 9, [like(5), like(4), like(3)], 'second_rates...  0.65 us
  transfers between devices with their start and end apart: 13, of which 5 were waited for; matrix products, arithmetic and copies ran while one was open for 0% of the time, Pallas kernels for 11%

profile of v5, /device:TPU:0, one launch (start us, length us, event | category | flops | bytes accessed | tf_op | source)
XLA Modules:
  0.0 20.2 jit_solution(7206361645206415423)
XLA Ops:
  0.6 1.2 %load_and_faces.1 = (f32[5,8,8,128]{3,2,1,0:T(8,128)S(1)}, f32[4,8,8,128]{3,2,1,0:T(8,128)S(1)}, s32[1,1,16]{2,1,0:T(1,128)S(1)}, s32[1,1,16]{2,1,0:T(1,128)S(1)...) custom-call(f32[5,8,8,128]{3,2,1,0:T(8,128)} %refs_0_.1, ...), custom_call_target="tpu_custom_call" | custom-call | flops 100000 | bytes 800000 | tf_op jit(solution)/shard_map/load_and_faces/pallas_call | solution.py:743
  1.8 3.0 %collective-permute-start = (f32[9,8,128]{2,1,0:T(8,128)S(1)}, f32[9,8,128]{2,1,0:T(8,128)S(1)}, u32[]{:S(2)}, u32[]{:S(2)}) collective-permute-start(f32[9,8,128]{2,1,0:T(8,128)S(1)} %get-tuple-element.47), channel_id=1, source_target_pairs={{0,1},{1,0},{2,3},{3,2},{4,28},{5,29},{6,30},{7,31},{8,9},{9,8},{1... | collective-permute-start | bytes 110600 | tf_op jit(solution)/shard_map/ppermute | solution.py:385
  4.8 0.7 %collective-permute-start.1 = (f32[9,8,128]{2,1,0:T(8,128)S(1)}, f32[9,8,128]{2,1,0:T(8,128)S(1)}, u32[]{:S(2)}, u32[]{:S(2)}) collective-permute-start(f32[9,8,128]{2,1,0:T(8,128)S(1)} %get-tuple-element.48), channel_id=1, source_target_pairs={{0,24},{1,25},{2,26},{3,27},{4,5},{5,4},{6,7},{7,6},{8,16},{9,17},... | collective-permute-start | bytes 110600 | tf_op jit(solution)/shard_map/ppermute | solution.py:385
  5.5 1.6 %collective-permute-start.2 = (f32[9,8,128]{2,1,0:T(8,128)S(1)}, f32[9,8,128]{2,1,0:T(8,128)S(1)}, u32[]{:S(2)}, u32[]{:S(2)}) collective-permute-start(f32[9,8,128]{2,1,0:T(8,128)S(1)} %get-tuple-element.49), channel_id=1, source_target_pairs={{0,2},{1,3},{2,0},{3,1},{4,12},{5,13},{6,14},{7,15},{8,10},{9,11},... | collective-permute-start | bytes 110600 | tf_op jit(solution)/shard_map/ppermute | solution.py:385
  7.1 0.7 %collective-permute-start.3 = (f32[9,8,128]{2,1,0:T(8,128)S(1)}, f32[9,8,128]{2,1,0:T(8,128)S(1)}, u32[]{:S(2)}, u32[]{:S(2)}) collective-permute-start(f32[9,8,128]{2,1,0:T(8,128)S(1)} %get-tuple-element.50), channel_id=1, source_target_pairs={{0,8},{1,9},{2,4},{3,5},{4,2},{5,3},{6,14},{7,15},{8,0},{9,1},{10,... | collective-permute-start | bytes 110600 | tf_op jit(solution)/shard_map/ppermute | solution.py:385
  7.8 0.0 collective-permute-start.4
  7.8 0.1 vorticity.1
  7.9 0.3 %plan.1 = (s32[4,8,128]{2,1,0:T(8,128)S(1)}, f32[4,8,128]{2,1,0:T(8,128)S(1)}, f32[64,8,128]{2,1,0:T(8,128)S(1)}, f32[8,8,128]{2,1,0:T(8,128)S(1)}, f32[2,8,128]{2,1,0:T(8,128)S(1)}) custom-call(s32[1,1,16]{2,1,0:T(1,128)S(1)} %get-tuple-element.54.owner_ref, s32[1,1,16]{2,1,0:T(1,128)S(1)} %get-tuple-element.55.slot_ref, f32[8,8]{1,0:T(8,128)S(1)} %get-tuple-element.56.proj_ref), custom_call_target="tpu_custom_call" | custom-call | flops 1000000 | bytes 800000 | tf_op jit(solution)/shard_map/plan/pallas_call | solution.py:755
  8.2 0.0 collective-permute-done.refs_0_
  8.2 0.3 %collective-permute-done.1.refs_1_ = f32[9,8,128]{2,1,0:T(8,128)S(1)} collective-permute-done((f32[9,8,128]{2,1,0:T(8,128)S(1)}, f32[9,8,128]{2,1,0:T(8,128)S(1)}, u32[]{:S(2)}, u32[]{:S(2)}) %collective-permute-start.1) | collective-permute-done | bytes 36896 | tf_op jit(solution)/shard_map/ppermute | solution.py:385
  8.5 0.2 vorticity_z.1.vort_ref
  8.7 1.1 %collective-permute-done.2.refs_2_ = f32[9,8,128]{2,1,0:T(8,128)S(1)} collective-permute-done((f32[9,8,128]{2,1,0:T(8,128)S(1)}, f32[9,8,128]{2,1,0:T(8,128)S(1)}, u32[]{:S(2)}, u32[]{:S(2)}) %collective-permute-start.2) | collective-permute-done | bytes 36896 | tf_op jit(solution)/shard_map/ppermute | solution.py:385
  9.9 0.0 copy-start.1
  9.9 0.0 copy-start.2
  9.9 0.3 %lamb_blocks.1 = (f32[7,8,128]{2,1,0:T(8,128)S(1)}, f32[7,8,128]{2,1,0:T(8,128)S(1)}, f32[7,8,128]{2,1,0:T(8,128)S(1)}, f32[7,8,128]{2,1,0:T(8,128)S(1)}) custom-call(s32[4,8,128]{2,1,0:T(8,128)S(1)} %get-tuple-element.58.order_ref, f32[4,8,128]{2,1,0:T(8,128)S(1)} %get-tuple-element.59.marks_ref, f32[64,8,128]{2,1,0:T(8,128)S(1)} %get-tuple-element.60.along_x_ref, ...), custom_call_target="tpu_custom_call" | custom-call | flops 10000000 | bytes 800000 | tf_op jit(solution)/shard_map/lamb_blocks/pallas_call | solution.py:778
  10.1 0.0 copy-start.3
  10.2 0.1 collective-permute-start.5
  10.2 1.7 %collective-permute-start.6 = (f32[7,8,128]{2,1,0:T(8,128)S(1)}, f32[7,8,128]{2,1,0:T(8,128)S(1)}, u32[]{:S(2)}, u32[]{:S(2)}) collective-permute-start(f32[7,8,128]{2,1,0:T(8,128)S(1)} %get-tuple-element.65), channel_id=1, source_target_pairs={{0,16},{8,24},{16,0},{24,8},{1,17},{9,25},{17,1},{25,9},{2,18},{10... | collective-permute-start | bytes 86024 | tf_op jit(solution)/shard_map/ppermute | solution.py:788
  12.0 0.1 collective-permute-start.7
  12.1 0.8 %first_rates.1 = (f32[5,8,8,128]{3,2,1,0:T(8,128)S(1)}, f32[4,8,8,128]{3,2,1,0:T(8,128)S(1)}, f32[6,3,8,128]{3,2,1,0:T(8,128)S(1)}, f32[6,8,128]{2,1,0:T(8,128)S...) custom-call(f32[8,8]{1,0:T(8,128)S(1)} %copy-done.3, ...), custom_call_target="tpu_custom_call" | custom-call | flops 40000000 | bytes 800000 | tf_op jit(solution)/shard_map/first_rates/pallas_call | solution.py:789
  12.9 0.7 %collective-permute-done.5.refs_0_ = f32[7,8,128]{2,1,0:T(8,128)S(1)} collective-permute-done((f32[7,8,128]{2,1,0:T(8,128)S(1)}, f32[7,8,128]{2,1,0:T(8,128)S(1)}, u32[]{:S(2)}, u32[]{:S(2)}) %collective-permute-start.5) | collective-permute-done | bytes 28704 | tf_op jit(solution)/shard_map/ppermute | solution.py:788
  13.5 0.9 %collective-permute-done.6.refs_1_ = f32[7,8,128]{2,1,0:T(8,128)S(1)} collective-permute-done((f32[7,8,128]{2,1,0:T(8,128)S(1)}, f32[7,8,128]{2,1,0:T(8,128)S(1)}, u32[]{:S(2)}, u32[]{:S(2)}) %collective-permute-start.6) | collective-permute-done | bytes 28704 | tf_op jit(solution)/shard_map/ppermute | solution.py:788
  14.4 0.3 %source_and_faces.1 = (f32[3,8,8,128]{3,2,1,0:T(8,128)S(1)}, f32[9,8,128]{2,1,0:T(8,128)S(1)}, f32[9,8,128]{2,1,0:T(8,128)S(1)}, f32[9,8,128]{2,1,0:T(8,128)S(1)...) custom-call(f32[2,8,128]{2,1,0:T(8,128)S(1)} %get-tuple-element.57.tile_ref, ...), custom_call_target="tpu_custom_call" | custom-call | flops 10000000 | bytes 800000 | tf_op jit(solution)/shard_map/source_and_faces/pallas_call | solution.py:797
  14.8 0.6 %collective-permute-start.8 = (f32[9,8,128]{2,1,0:T(8,128)S(1)}, f32[9,8,128]{2,1,0:T(8,128)S(1)}, u32[]{:S(2)}, u32[]{:S(2)}) collective-permute-start(f32[9,8,128]{2,1,0:T(8,128)S(1)} %get-tuple-element.77), channel_id=1, source_target_pairs={{0,1},{1,0},{2,3},{3,2},{4,28},{5,29},{6,30},{7,31},{8,9},{9,8},{1... | collective-permute-start | bytes 110600 | tf_op jit(solution)/shard_map/ppermute | solution.py:385
  15.4 1.7 %collective-permute-start.10 = (f32[9,8,128]{2,1,0:T(8,128)S(1)}, f32[9,8,128]{2,1,0:T(8,128)S(1)}, u32[]{:S(2)}, u32[]{:S(2)}) collective-permute-start(f32[9,8,128]{2,1,0:T(8,128)S(1)} %get-tuple-element.81), channel_id=1, source_target_pairs={{0,2},{1,3},{2,0},{3,1},{4,12},{5,13},{6,14},{7,15},{8,10},{9,11},... | collective-permute-start | bytes 110600 | tf_op jit(solution)/shard_map/ppermute | solution.py:385
  17.1 1.1 %collective-permute-start.11 = (f32[9,8,128]{2,1,0:T(8,128)S(1)}, f32[9,8,128]{2,1,0:T(8,128)S(1)}, u32[]{:S(2)}, u32[]{:S(2)}) collective-permute-start(f32[9,8,128]{2,1,0:T(8,128)S(1)} %get-tuple-element.82), channel_id=1, source_target_pairs={{0,8},{1,9},{2,4},{3,5},{4,2},{5,3},{6,14},{7,15},{8,0},{9,1},{10,... | collective-permute-start | bytes 110600 | tf_op jit(solution)/shard_map/ppermute | solution.py:385
  18.2 0.6 %second_rates_inner.1 = (f32[5,8,8,128]{3,2,1,0:T(8,128)S(1)}, f32[4,8,8,128]{3,2,1,0:T(8,128)S(1)}, f32[3,8,8,128]{3,2,1,0:T(8,128)}) custom-call(f32[8,8]{1,0:T(8,128)S(1)} %copy-done.3, bf16[128,128]{1,0:T(8,128)(2,1)S(1)} %copy-done.2, bf16[128,128]{1,0:T(8,128)(2,1)S(1)} %copy-done.1, f32[5,8,8,128]{3,2,1,0:T(8,128)S(1)} %get-tuple-element.45.les_ref, ...), custom_call_target="tpu_custom_call" | custom-call | flops 40000000 | bytes 800000 | tf_op jit(solution)/shard_map/second_rates_inner/pallas_call | solution.py:805
  18.9 0.2 %collective-permute-done.9.refs_1_ = f32[9,8,128]{2,1,0:T(8,128)S(1)} collective-permute-done((f32[9,8,128]{2,1,0:T(8,128)S(1)}, f32[9,8,128]{2,1,0:T(8,128)S(1)}, u32[]{:S(2)}, u32[]{:S(2)}) %collective-permute-start.9) | collective-permute-done | bytes 36896 | tf_op jit(solution)/shard_map/ppermute | solution.py:385
  19.1 0.2 %second_rates_z.1 = (f32[5,8,8,128]{3,2,1,0:T(8,128)S(1)}, f32[4,8,8,128]{3,2,1,0:T(8,128)S(1)}) custom-call(f32[5,8,8,128]{3,2,1,0:T(8,128)S(1)} %get-tuple-element.74.les_base_ref, f32[4,8,8,128]{3,2,1,0:T(8,128)S(1)} %get-tuple-element.75.wave_base_ref, f32[6,3,8,128]{3,2,1,0:T(8,128)S(1)} %get-tuple-element.76.mean_faces_ref, ...), custom_call_target="tpu_custom_call" | custom-call | flops 1000000 | bytes 800000 | tf_op jit(solution)/shard_map/second_rates_z/pallas_call | solution.py:816
  19.3 0.0 collective-permute-done.10.refs_2_
  19.4 0.0 collective-permute-done.12.refs_4_
  19.4 0.8 %second_rates_outer.1 = (f32[5,8,8,128]{3,2,1,0:T(8,128)}, f32[4,8,8,128]{3,2,1,0:T(8,128)}) custom-call(f32[5,8,8,128]{3,2,1,0:T(8,128)S(1)} %get-tuple-element.79.les_base_ref, f32[4,8,8,128]{3,2,1,0:T(8,128)S(1)} %get-tuple-element.80.wave_base_ref, f32[6,3,8,128]{3,2,1,0:T(8,128)S(1)} %get-tuple-element.76.mean_faces_ref, ...), custom_call_target="tpu_custom_call" | custom-call | flops 4000000 | bytes 800000 | tf_op jit(solution)/shard_map/second_rates_outer/pallas_call | solution.py:823
  (12 shorter events, 0.0 us)
Async XLA Ops:
  1.8 6.4 %collective-permute-start = (f32[9,8,128]{2,1,0:T(8,128)S(1)}, f32[9,8,128]{2,1,0:T(8,128)S(1)}, u32[]{:S(2)}, u32[]{:S(2)}) collective-permute-start(f32[9,8,128]{2,1,0:T(8,128)S(1)} %get-tuple-element.47), channel_id=1, source_target_pairs={{0,1},{1,0},{2,3},{3,2},{4,28},{5,29},{6,30},{7,31},{8,9},{9,8},{1... | collective-permute-start | bytes 110600 | tf_op jit(solution)/shard_map/ppermute | solution.py:385
  4.8 3.7 %collective-permute-start.1 = (f32[9,8,128]{2,1,0:T(8,128)S(1)}, f32[9,8,128]{2,1,0:T(8,128)S(1)}, u32[]{:S(2)}, u32[]{:S(2)}) collective-permute-start(f32[9,8,128]{2,1,0:T(8,128)S(1)} %get-tuple-element.48), channel_id=1, source_target_pairs={{0,24},{1,25},{2,26},{3,27},{4,5},{5,4},{6,7},{7,6},{8,16},{9,17},... | collective-permute-start | bytes 110600 | tf_op jit(solution)/shard_map/ppermute | solution.py:385
  5.5 4.3 %collective-permute-start.2 = (f32[9,8,128]{2,1,0:T(8,128)S(1)}, f32[9,8,128]{2,1,0:T(8,128)S(1)}, u32[]{:S(2)}, u32[]{:S(2)}) collective-permute-start(f32[9,8,128]{2,1,0:T(8,128)S(1)} %get-tuple-element.49), channel_id=1, source_target_pairs={{0,2},{1,3},{2,0},{3,1},{4,12},{5,13},{6,14},{7,15},{8,10},{9,11},... | collective-permute-start | bytes 110600 | tf_op jit(solution)/shard_map/ppermute | solution.py:385
  7.1 2.8 %collective-permute-start.3 = (f32[9,8,128]{2,1,0:T(8,128)S(1)}, f32[9,8,128]{2,1,0:T(8,128)S(1)}, u32[]{:S(2)}, u32[]{:S(2)}) collective-permute-start(f32[9,8,128]{2,1,0:T(8,128)S(1)} %get-tuple-element.50), channel_id=1, source_target_pairs={{0,8},{1,9},{2,4},{3,5},{4,2},{5,3},{6,14},{7,15},{8,0},{9,1},{10,... | collective-permute-start | bytes 110600 | tf_op jit(solution)/shard_map/ppermute | solution.py:385
  7.8 2.1 %collective-permute-start.4 = (f32[9,8,128]{2,1,0:T(8,128)S(1)}, f32[9,8,128]{2,1,0:T(8,128)S(1)}, u32[]{:S(2)}, u32[]{:S(2)}) collective-permute-start(f32[9,8,128]{2,1,0:T(8,128)S(1)} %get-tuple-element.51), channel_id=1, source_target_pairs={{0,8},{1,9},{2,10},{3,11},{4,6},{5,7},{6,4},{7,5},{8,0},{9,1},{10,... | collective-permute-start | bytes 110600 | tf_op jit(solution)/shard_map/ppermute | solution.py:385
  9.9 2.2 %copy-start = (f32[3,8,8,128]{3,2,1,0:T(8,128)S(1)}, f32[3,8,8,128]{3,2,1,0:T(8,128)}, u32[]{:S(2)}) copy-start(f32[3,8,8,128]{3,2,1,0:T(8,128)} %mean_ref.3) | copy-start | bytes 294916
  9.9 2.2 %copy-start.1 = (bf16[128,128]{1,0:T(8,128)(2,1)S(1)}, bf16[128,128]{1,0:T(8,128)(2,1)}, u32[]{:S(2)}) copy-start(bf16[128,128]{1,0:T(8,128)(2,1)} %constant.8.clone.low_ref) | copy-start | bytes 98308
  9.9 2.2 %copy-start.2 = (bf16[128,128]{1,0:T(8,128)(2,1)S(1)}, bf16[128,128]{1,0:T(8,128)(2,1)}, u32[]{:S(2)}) copy-start(bf16[128,128]{1,0:T(8,128)(2,1)} %constant.7.clone.high_ref) | copy-start | bytes 98308
  10.1 2.0 %copy-start.3 = (f32[8,8]{1,0:T(8,128)S(1)}, f32[8,8]{1,0:T(8,128)}, u32[]{:S(2)}) copy-start(f32[8,8]{1,0:T(8,128)} %constant.6.clone.deriv_ref) | copy-start | bytes 772
  10.2 3.4 %collective-permute-start.5 = (f32[7,8,128]{2,1,0:T(8,128)S(1)}, f32[7,8,128]{2,1,0:T(8,128)S(1)}, u32[]{:S(2)}, u32[]{:S(2)}) collective-permute-start(f32[7,8,128]{2,1,0:T(8,128)S(1)} %get-tuple-element.64), channel_id=1, source_target_pairs={{0,24},{8,16},{16,8},{24,0},{1,25},{9,17},{17,9},{25,1},{2,26},{10... | collective-permute-start | bytes 86024 | tf_op jit(solution)/shard_map/ppermute | solution.py:788
  10.2 4.2 %collective-permute-start.6 = (f32[7,8,128]{2,1,0:T(8,128)S(1)}, f32[7,8,128]{2,1,0:T(8,128)S(1)}, u32[]{:S(2)}, u32[]{:S(2)}) collective-permute-start(f32[7,8,128]{2,1,0:T(8,128)S(1)} %get-tuple-element.65), channel_id=1, source_target_pairs={{0,16},{8,24},{16,0},{24,8},{1,17},{9,25},{17,1},{25,9},{2,18},{10... | collective-permute-start | bytes 86024 | tf_op jit(solution)/shard_map/ppermute | solution.py:788
  12.0 2.5 %collective-permute-start.7 = (f32[7,8,128]{2,1,0:T(8,128)S(1)}, f32[7,8,128]{2,1,0:T(8,128)S(1)}, u32[]{:S(2)}, u32[]{:S(2)}) collective-permute-start(f32[7,8,128]{2,1,0:T(8,128)S(1)} %get-tuple-element.66), channel_id=1, source_target_pairs={{0,8},{8,0},{16,24},{24,16},{1,9},{9,1},{17,25},{25,17},{2,10},{10... | collective-permute-start | bytes 86024 | tf_op jit(solution)/shard_map/ppermute | solution.py:788
  14.8 4.1 %collective-permute-start.8 = (f32[9,8,128]{2,1,0:T(8,128)S(1)}, f32[9,8,128]{2,1,0:T(8,128)S(1)}, u32[]{:S(2)}, u32[]{:S(2)}) collective-permute-start(f32[9,8,128]{2,1,0:T(8,128)S(1)} %get-tuple-element.77), channel_id=1, source_target_pairs={{0,1},{1,0},{2,3},{3,2},{4,28},{5,29},{6,30},{7,31},{8,9},{9,8},{1... | collective-permute-start | bytes 110600 | tf_op jit(solution)/shard_map/ppermute | solution.py:385
  15.4 3.7 %collective-permute-start.9 = (f32[9,8,128]{2,1,0:T(8,128)S(1)}, f32[9,8,128]{2,1,0:T(8,128)S(1)}, u32[]{:S(2)}, u32[]{:S(2)}) collective-permute-start(f32[9,8,128]{2,1,0:T(8,128)S(1)} %get-tuple-element.78), channel_id=1, source_target_pairs={{0,24},{1,25},{2,26},{3,27},{4,5},{5,4},{6,7},{7,6},{8,16},{9,17},... | collective-permute-start | bytes 110600 | tf_op jit(solution)/shard_map/ppermute | solution.py:385
  15.4 4.0 %collective-permute-start.10 = (f32[9,8,128]{2,1,0:T(8,128)S(1)}, f32[9,8,128]{2,1,0:T(8,128)S(1)}, u32[]{:S(2)}, u32[]{:S(2)}) collective-permute-start(f32[9,8,128]{2,1,0:T(8,128)S(1)} %get-tuple-element.81), channel_id=1, source_target_pairs={{0,2},{1,3},{2,0},{3,1},{4,12},{5,13},{6,14},{7,15},{8,10},{9,11},... | collective-permute-start | bytes 110600 | tf_op jit(solution)/shard_map/ppermute | solution.py:385
  17.1 2.2 %collective-permute-start.11 = (f32[9,8,128]{2,1,0:T(8,128)S(1)}, f32[9,8,128]{2,1,0:T(8,128)S(1)}, u32[]{:S(2)}, u32[]{:S(2)}) collective-permute-start(f32[9,8,128]{2,1,0:T(8,128)S(1)} %get-tuple-element.82), channel_id=1, source_target_pairs={{0,8},{1,9},{2,4},{3,5},{4,2},{5,3},{6,14},{7,15},{8,0},{9,1},{10,... | collective-permute-start | bytes 110600 | tf_op jit(solution)/shard_map/ppermute | solution.py:385
  18.2 1.2 %collective-permute-start.12 = (f32[9,8,128]{2,1,0:T(8,128)S(1)}, f32[9,8,128]{2,1,0:T(8,128)S(1)}, u32[]{:S(2)}, u32[]{:S(2)}) collective-permute-start(f32[9,8,128]{2,1,0:T(8,128)S(1)} %get-tuple-element.83), channel_id=1, source_target_pairs={{0,8},{1,9},{2,10},{3,11},{4,6},{5,7},{6,4},{7,5},{8,0},{9,1},{10,... | collective-permute-start | bytes 110600 | tf_op jit(solution)/shard_map/ppermute | solution.py:385

commit v6 on v3

--- a/solution.py
+++ b/solution.py
@@ -394,10 +394,8 @@
     parts = [
         (source.at[low:high], target.at[low:high], first + low, high - low)
         for source, target, low, high, first in (
-            (les_hbm, les_ref, 0, 3, 0),
-            (les_hbm, les_ref, 3, 5, 0),
-            (wave_hbm, wave_ref, 0, 2, 5),
-            (wave_hbm, wave_ref, 2, 4, 5),
+            (les_hbm, les_ref, 0, 5, 0),
+            (wave_hbm, wave_ref, 0, 4, 5),
         )
     ]
     copies = [
@@ -707,16 +705,19 @@
     face_refs, (les_out, wave_out, les_ref, wave_ref, sems) = (
         refs[:n_faces], refs[n_faces:],
     )
-    copies = []
+    copies = [
+        pltpu.make_async_copy(les_ref, les_out, sems.at[0]),
+        pltpu.make_async_copy(wave_ref, wave_out, sems.at[1]),
+    ]
 
     def put(c, planes):
-        kept, target = (les_ref.at[c], les_out.at[c]) if c < 5 else (
-            wave_ref.at[c - 5], wave_out.at[c - 5]
-        )
         for x, plane in enumerate(planes):
-            kept[x] = plane
-        copies.append(pltpu.make_async_copy(kept, target, sems.at[c]))
-        copies[-1].start()
+            if c < 5:
+                les_ref[c, x] = plane
+            else:
+                wave_ref[c - 5, x] = plane
+        if c in (4, 8):
+            copies[c // 8].start()
 
     add_layers(counts, (0, 1), face_refs, mean_faces_ref, les_base_ref, wave_base_ref, put)
     for copy in copies:
@@ -762,7 +763,7 @@
         [like(5), like(4)] + faces,
         "load_and_faces",
         100000,
-        [pltpu.SemaphoreType.DMA((4,))],
+        [pltpu.SemaphoreType.DMA((2,))],
     )(*in_hbm(les, wave))
     got = exchange(sent, counts)
 
@@ -848,7 +849,7 @@
         [
             pltpu.VMEM(les.shape, f32),
             pltpu.VMEM(wave.shape, f32),
-            pltpu.SemaphoreType.DMA((9,)),
+            pltpu.SemaphoreType.DMA((2,)),
         ],
         out_spec=[HBM, HBM],
     )(les_base, wave_base, mean_faces, *got)

time: 20.5 us -> 20.4 us (level)
  no operation moved by 1% of the time
where the time goes in v6:
time: 20.4 us; the launch traced here: 20.2 us
  starting transfers between devices  11.3 us (55%)
  Pallas kernels  5.41 us (27%)
  waiting for transfers between devices  2.71 us (13%)
  between operations  0.76 us (4%)
    ppermute x10, starting transfers between devices, exchange(): lax.ppermute(face, axes, way)  9.33 us
    ppermute x3, starting transfers between devices, local(): moved.append(pieces[k] if still else lax.ppermute(pieces[k], 'gx', sets[k]))  1.94 us
    ppermute x3, waiting for transfers between devices, local(): moved.append(pieces[k] if still else lax.ppermute(pieces[k], 'gx', sets[k]))  1.55 us
    pallas_call x1, Pallas kernels, local(): call(functools.partial(load_kernel, counts), [HBM] * 2, [like(5), like(4)...  1.16 us
    ppermute x10, waiting for transfers between devices, exchange(): lax.ppermute(face, axes, way)  1.15 us
    pallas_call x1, Pallas kernels, local(): call(functools.partial(plan_kernel, counts), [HBM] * 3 + [VMEM], [jax.Sha...  1.06 us
    pallas_call x1, Pallas kernels, local(): call(functools.partial(last_kernel, counts, n_faces), [VMEM] * (3 + n_fac...  0.8 us
    pallas_call x1, Pallas kernels, local(): call(functools.partial(first_kernel, counts, n_faces), [VMEM] * (6 + n_fa...  0.77 us
  transfers between devices with their start and end apart: 13, of which 4 were waited for; matrix products, arithmetic and copies ran while one was open for 0% of the time, Pallas kernels for 14%

profile of v6, /device:TPU:0, one launch (start us, length us, event | category | flops | bytes accessed | tf_op | source)
XLA Modules:
  0.0 20.2 jit_solution(12291961458881698216)
XLA Ops:
  0.6 1.2 %load_and_faces.1 = (f32[5,8,8,128]{3,2,1,0:T(8,128)S(1)}, f32[4,8,8,128]{3,2,1,0:T(8,128)S(1)}, f32[9,8,128]{2,1,0:T(8,128)S(1)}, f32[9,8,128]{2,1,0:T(8,128)S(...) custom-call(f32[5,8,8,128]{3,2,1,0:T(8,128)} %les_hbm.1, f32[4,8,8,128]{3,2,1,0:T(8,128)} %wave_hbm.1), custom_call_target="tpu_custom_call" | custom-call | flops 100000 | bytes 800000 | tf_op jit(solution)/shard_map/load_and_faces/pallas_call | solution.py:760
  1.8 3.0 %collective-permute-start = (f32[9,8,128]{2,1,0:T(8,128)S(1)}, f32[9,8,128]{2,1,0:T(8,128)S(1)}, u32[]{:S(2)}, u32[]{:S(2)}) collective-permute-start(f32[9,8,128]{2,1,0:T(8,128)S(1)} %get-tuple-element.44), channel_id=1, source_target_pairs={{0,1},{1,0},{2,3},{3,2},{4,28},{5,29},{6,30},{7,31},{8,9},{9,8},{1... | collective-permute-start | bytes 110600 | tf_op jit(solution)/shard_map/ppermute | solution.py:385
  4.8 0.7 %collective-permute-start.1 = (f32[9,8,128]{2,1,0:T(8,128)S(1)}, f32[9,8,128]{2,1,0:T(8,128)S(1)}, u32[]{:S(2)}, u32[]{:S(2)}) collective-permute-start(f32[9,8,128]{2,1,0:T(8,128)S(1)} %get-tuple-element.45), channel_id=1, source_target_pairs={{0,24},{1,25},{2,26},{3,27},{4,5},{5,4},{6,7},{7,6},{8,16},{9,17},... | collective-permute-start | bytes 110600 | tf_op jit(solution)/shard_map/ppermute | solution.py:385
  5.5 1.6 %collective-permute-start.2 = (f32[9,8,128]{2,1,0:T(8,128)S(1)}, f32[9,8,128]{2,1,0:T(8,128)S(1)}, u32[]{:S(2)}, u32[]{:S(2)}) collective-permute-start(f32[9,8,128]{2,1,0:T(8,128)S(1)} %get-tuple-element.46), channel_id=1, source_target_pairs={{0,2},{1,3},{2,0},{3,1},{4,12},{5,13},{6,14},{7,15},{8,10},{9,11},... | collective-permute-start | bytes 110600 | tf_op jit(solution)/shard_map/ppermute | solution.py:385
  7.1 0.7 %collective-permute-start.3 = (f32[9,8,128]{2,1,0:T(8,128)S(1)}, f32[9,8,128]{2,1,0:T(8,128)S(1)}, u32[]{:S(2)}, u32[]{:S(2)}) collective-permute-start(f32[9,8,128]{2,1,0:T(8,128)S(1)} %get-tuple-element.47), channel_id=1, source_target_pairs={{0,8},{1,9},{2,4},{3,5},{4,2},{5,3},{6,14},{7,15},{8,0},{9,1},{10,... | collective-permute-start | bytes 110600 | tf_op jit(solution)/shard_map/ppermute | solution.py:385
  7.7 1.1 %plan_and_vorticity.1 = (s32[4,8,128]{2,1,0:T(8,128)S(1)}, f32[4,8,128]{2,1,0:T(8,128)S(1)}, f32[64,8,128]{2,1,0:T(8,128)S(1)}, f32[8,8,128]{2,1,0:T(8,128)S(1)}...) custom-call(s32[1,1,16]{2,1,0:T(1,128)} %owner_hbm.1, ...), custom_call_target="tpu_custom_call" | custom-call | flops 1000000 | bytes 800000 | tf_op jit(solution)/shard_map/plan_and_vorticity/pallas_call | solution.py:773
  8.8 0.0 collective-permute-done.1.refs_1_
  8.8 0.2 vorticity_z.1.vort_ref
  9.0 0.8 %collective-permute-done.2.refs_2_ = f32[9,8,128]{2,1,0:T(8,128)S(1)} collective-permute-done((f32[9,8,128]{2,1,0:T(8,128)S(1)}, f32[9,8,128]{2,1,0:T(8,128)S(1)}, u32[]{:S(2)}, u32[]{:S(2)}) %collective-permute-start.2) | collective-permute-done | bytes 36896 | tf_op jit(solution)/shard_map/ppermute | solution.py:385
  9.8 0.0 collective-permute-done.3.refs_3_
  9.8 0.0 collective-permute-done.4.refs_4_
  9.8 0.0 copy-start.1
  9.8 0.0 copy-start.2
  9.9 0.3 %lamb_blocks.1 = (f32[7,8,128]{2,1,0:T(8,128)S(1)}, f32[7,8,128]{2,1,0:T(8,128)S(1)}, f32[7,8,128]{2,1,0:T(8,128)S(1)}, f32[7,8,128]{2,1,0:T(8,128)S(1)}) custom-call(s32[4,8,128]{2,1,0:T(8,128)S(1)} %get-tuple-element.52.order_ref, f32[4,8,128]{2,1,0:T(8,128)S(1)} %get-tuple-element.53.marks_ref, f32[64,8,128]{2,1,0:T(8,128)S(1)} %get-tuple-element.54.along_x_ref, ...), custom_call_target="tpu_custom_call" | custom-call | flops 10000000 | bytes 800000 | tf_op jit(solution)/shard_map/lamb_blocks/pallas_call | solution.py:798
  10.1 0.0 copy-start.3
  10.1 0.1 collective-permute-start.5
  10.2 1.7 %collective-permute-start.6 = (f32[7,8,128]{2,1,0:T(8,128)S(1)}, f32[7,8,128]{2,1,0:T(8,128)S(1)}, u32[]{:S(2)}, u32[]{:S(2)}) collective-permute-start(f32[7,8,128]{2,1,0:T(8,128)S(1)} %get-tuple-element.59), channel_id=1, source_target_pairs={{0,16},{8,24},{16,0},{24,8},{1,17},{9,25},{17,1},{25,9},{2,18},{10... | collective-permute-start | bytes 86024 | tf_op jit(solution)/shard_map/ppermute | solution.py:808
  11.9 0.1 collective-permute-start.7
  12.1 0.8 %first_rates.1 = (f32[5,8,8,128]{3,2,1,0:T(8,128)S(1)}, f32[4,8,8,128]{3,2,1,0:T(8,128)S(1)}, f32[6,3,8,128]{3,2,1,0:T(8,128)S(1)}, f32[6,8,128]{2,1,0:T(8,128)S...) custom-call(f32[8,8]{1,0:T(8,128)S(1)} %copy-done.3, ...), custom_call_target="tpu_custom_call" | custom-call | flops 40000000 | bytes 800000 | tf_op jit(solution)/shard_map/first_rates/pallas_call | solution.py:809
  12.9 0.7 %collective-permute-done.5.refs_0_ = f32[7,8,128]{2,1,0:T(8,128)S(1)} collective-permute-done((f32[7,8,128]{2,1,0:T(8,128)S(1)}, f32[7,8,128]{2,1,0:T(8,128)S(1)}, u32[]{:S(2)}, u32[]{:S(2)}) %collective-permute-start.5) | collective-permute-done | bytes 28704 | tf_op jit(solution)/shard_map/ppermute | solution.py:808
  13.5 0.9 %collective-permute-done.6.refs_1_ = f32[7,8,128]{2,1,0:T(8,128)S(1)} collective-permute-done((f32[7,8,128]{2,1,0:T(8,128)S(1)}, f32[7,8,128]{2,1,0:T(8,128)S(1)}, u32[]{:S(2)}, u32[]{:S(2)}) %collective-permute-start.6) | collective-permute-done | bytes 28704 | tf_op jit(solution)/shard_map/ppermute | solution.py:808
  14.4 0.3 %source_and_faces.1 = (f32[3,8,8,128]{3,2,1,0:T(8,128)S(1)}, f32[9,8,128]{2,1,0:T(8,128)S(1)}, f32[9,8,128]{2,1,0:T(8,128)S(1)}, f32[9,8,128]{2,1,0:T(8,128)S(1)...) custom-call(f32[2,8,128]{2,1,0:T(8,128)S(1)} %get-tuple-element.51.tile_ref, ...), custom_call_target="tpu_custom_call" | custom-call | flops 10000000 | bytes 800000 | tf_op jit(solution)/shard_map/source_and_faces/pallas_call | solution.py:817
  14.8 0.6 %collective-permute-start.8 = (f32[9,8,128]{2,1,0:T(8,128)S(1)}, f32[9,8,128]{2,1,0:T(8,128)S(1)}, u32[]{:S(2)}, u32[]{:S(2)}) collective-permute-start(f32[9,8,128]{2,1,0:T(8,128)S(1)} %get-tuple-element.71), channel_id=1, source_target_pairs={{0,1},{1,0},{2,3},{3,2},{4,28},{5,29},{6,30},{7,31},{8,9},{9,8},{1... | collective-permute-start | bytes 110600 | tf_op jit(solution)/shard_map/ppermute | solution.py:385
  15.4 0.0 collective-permute-start.9
  15.4 1.7 %collective-permute-start.10 = (f32[9,8,128]{2,1,0:T(8,128)S(1)}, f32[9,8,128]{2,1,0:T(8,128)S(1)}, u32[]{:S(2)}, u32[]{:S(2)}) collective-permute-start(f32[9,8,128]{2,1,0:T(8,128)S(1)} %get-tuple-element.75), channel_id=1, source_target_pairs={{0,2},{1,3},{2,0},{3,1},{4,12},{5,13},{6,14},{7,15},{8,10},{9,11},... | collective-permute-start | bytes 110600 | tf_op jit(solution)/shard_map/ppermute | solution.py:385
  17.1 1.1 %collective-permute-start.11 = (f32[9,8,128]{2,1,0:T(8,128)S(1)}, f32[9,8,128]{2,1,0:T(8,128)S(1)}, u32[]{:S(2)}, u32[]{:S(2)}) collective-permute-start(f32[9,8,128]{2,1,0:T(8,128)S(1)} %get-tuple-element.76), channel_id=1, source_target_pairs={{0,8},{1,9},{2,4},{3,5},{4,2},{5,3},{6,14},{7,15},{8,0},{9,1},{10,... | collective-permute-start | bytes 110600 | tf_op jit(solution)/shard_map/ppermute | solution.py:385
  18.2 0.6 %second_rates_inner.1 = (f32[5,8,8,128]{3,2,1,0:T(8,128)S(1)}, f32[4,8,8,128]{3,2,1,0:T(8,128)S(1)}, f32[3,8,8,128]{3,2,1,0:T(8,128)}) custom-call(f32[8,8]{1,0:T(8,128)S(1)} %copy-done.3, bf16[128,128]{1,0:T(8,128)(2,1)S(1)} %copy-done.1, bf16[128,128]{1,0:T(8,128)(2,1)S(1)} %copy-done.2, f32[5,8,8,128]{3,2,1,0:T(8,128)S(1)} %get-tuple-element.42.les_ref, ...), custom_call_target="tpu_custom_call" | custom-call | flops 40000000 | bytes 800000 | tf_op jit(solution)/shard_map/second_rates_inner/pallas_call | solution.py:825
  18.8 0.2 %collective-permute-done.9.refs_1_ = f32[9,8,128]{2,1,0:T(8,128)S(1)} collective-permute-done((f32[9,8,128]{2,1,0:T(8,128)S(1)}, f32[9,8,128]{2,1,0:T(8,128)S(1)}, u32[]{:S(2)}, u32[]{:S(2)}) %collective-permute-start.9) | collective-permute-done | bytes 36896 | tf_op jit(solution)/shard_map/ppermute | solution.py:385
  19.1 0.2 %second_rates_z.1 = (f32[5,8,8,128]{3,2,1,0:T(8,128)S(1)}, f32[4,8,8,128]{3,2,1,0:T(8,128)S(1)}) custom-call(f32[5,8,8,128]{3,2,1,0:T(8,128)S(1)} %get-tuple-element.68.les_base_ref, f32[4,8,8,128]{3,2,1,0:T(8,128)S(1)} %get-tuple-element.69.wave_base_ref, f32[6,3,8,128]{3,2,1,0:T(8,128)S(1)} %get-tuple-element.70.mean_faces_ref, ...), custom_call_target="tpu_custom_call" | custom-call | flops 1000000 | bytes 800000 | tf_op jit(solution)/shard_map/second_rates_z/pallas_call | solution.py:836
  19.3 0.0 collective-permute-done.10.refs_2_
  19.3 0.0 collective-permute-done.12.refs_4_
  19.4 0.8 %second_rates_outer.1 = (f32[5,8,8,128]{3,2,1,0:T(8,128)}, f32[4,8,8,128]{3,2,1,0:T(8,128)}) custom-call(f32[5,8,8,128]{3,2,1,0:T(8,128)S(1)} %get-tuple-element.73.les_base_ref, f32[4,8,8,128]{3,2,1,0:T(8,128)S(1)} %get-tuple-element.74.wave_base_ref, f32[6,3,8,128]{3,2,1,0:T(8,128)S(1)} %get-tuple-element.70.mean_faces_ref, ...), custom_call_target="tpu_custom_call" | custom-call | flops 4000000 | bytes 800000 | tf_op jit(solution)/shard_map/second_rates_outer/pallas_call | solution.py:843
  (11 shorter events, 0.0 us)
Async XLA Ops:
  1.8 7.0 %collective-permute-start = (f32[9,8,128]{2,1,0:T(8,128)S(1)}, f32[9,8,128]{2,1,0:T(8,128)S(1)}, u32[]{:S(2)}, u32[]{:S(2)}) collective-permute-start(f32[9,8,128]{2,1,0:T(8,128)S(1)} %get-tuple-element.44), channel_id=1, source_target_pairs={{0,1},{1,0},{2,3},{3,2},{4,28},{5,29},{6,30},{7,31},{8,9},{9,8},{1... | collective-permute-start | bytes 110600 | tf_op jit(solution)/shard_map/ppermute | solution.py:385
  4.8 4.0 %collective-permute-start.1 = (f32[9,8,128]{2,1,0:T(8,128)S(1)}, f32[9,8,128]{2,1,0:T(8,128)S(1)}, u32[]{:S(2)}, u32[]{:S(2)}) collective-permute-start(f32[9,8,128]{2,1,0:T(8,128)S(1)} %get-tuple-element.45), channel_id=1, source_target_pairs={{0,24},{1,25},{2,26},{3,27},{4,5},{5,4},{6,7},{7,6},{8,16},{9,17},... | collective-permute-start | bytes 110600 | tf_op jit(solution)/shard_map/ppermute | solution.py:385
  5.5 4.3 %collective-permute-start.2 = (f32[9,8,128]{2,1,0:T(8,128)S(1)}, f32[9,8,128]{2,1,0:T(8,128)S(1)}, u32[]{:S(2)}, u32[]{:S(2)}) collective-permute-start(f32[9,8,128]{2,1,0:T(8,128)S(1)} %get-tuple-element.46), channel_id=1, source_target_pairs={{0,2},{1,3},{2,0},{3,1},{4,12},{5,13},{6,14},{7,15},{8,10},{9,11},... | collective-permute-start | bytes 110600 | tf_op jit(solution)/shard_map/ppermute | solution.py:385
  7.1 2.8 %collective-permute-start.3 = (f32[9,8,128]{2,1,0:T(8,128)S(1)}, f32[9,8,128]{2,1,0:T(8,128)S(1)}, u32[]{:S(2)}, u32[]{:S(2)}) collective-permute-start(f32[9,8,128]{2,1,0:T(8,128)S(1)} %get-tuple-element.47), channel_id=1, source_target_pairs={{0,8},{1,9},{2,4},{3,5},{4,2},{5,3},{6,14},{7,15},{8,0},{9,1},{10,... | collective-permute-start | bytes 110600 | tf_op jit(solution)/shard_map/ppermute | solution.py:385
  7.7 2.1 %collective-permute-start.4 = (f32[9,8,128]{2,1,0:T(8,128)S(1)}, f32[9,8,128]{2,1,0:T(8,128)S(1)}, u32[]{:S(2)}, u32[]{:S(2)}) collective-permute-start(f32[9,8,128]{2,1,0:T(8,128)S(1)} %get-tuple-element.48), channel_id=1, source_target_pairs={{0,8},{1,9},{2,10},{3,11},{4,6},{5,7},{6,4},{7,5},{8,0},{9,1},{10,... | collective-permute-start | bytes 110600 | tf_op jit(solution)/shard_map/ppermute | solution.py:385
  9.8 2.2 %copy-start = (f32[3,8,8,128]{3,2,1,0:T(8,128)S(1)}, f32[3,8,8,128]{3,2,1,0:T(8,128)}, u32[]{:S(2)}) copy-start(f32[3,8,8,128]{3,2,1,0:T(8,128)} %mean_ref.3) | copy-start | bytes 294916
  9.8 2.2 %copy-start.1 = (bf16[128,128]{1,0:T(8,128)(2,1)S(1)}, bf16[128,128]{1,0:T(8,128)(2,1)}, u32[]{:S(2)}) copy-start(bf16[128,128]{1,0:T(8,128)(2,1)} %constant.7.clone.high_ref) | copy-start | bytes 98308
  9.8 2.2 %copy-start.2 = (bf16[128,128]{1,0:T(8,128)(2,1)S(1)}, bf16[128,128]{1,0:T(8,128)(2,1)}, u32[]{:S(2)}) copy-start(bf16[128,128]{1,0:T(8,128)(2,1)} %constant.8.clone.low_ref) | copy-start | bytes 98308
  10.1 2.0 %copy-start.3 = (f32[8,8]{1,0:T(8,128)S(1)}, f32[8,8]{1,0:T(8,128)}, u32[]{:S(2)}) copy-start(f32[8,8]{1,0:T(8,128)} %constant.6.clone.deriv_ref) | copy-start | bytes 772
  10.1 3.4 %collective-permute-start.5 = (f32[7,8,128]{2,1,0:T(8,128)S(1)}, f32[7,8,128]{2,1,0:T(8,128)S(1)}, u32[]{:S(2)}, u32[]{:S(2)}) collective-permute-start(f32[7,8,128]{2,1,0:T(8,128)S(1)} %get-tuple-element.58), channel_id=1, source_target_pairs={{0,24},{8,16},{16,8},{24,0},{1,25},{9,17},{17,9},{25,1},{2,26},{10... | collective-permute-start | bytes 86024 | tf_op jit(solution)/shard_map/ppermute | solution.py:808
  10.2 4.2 %collective-permute-start.6 = (f32[7,8,128]{2,1,0:T(8,128)S(1)}, f32[7,8,128]{2,1,0:T(8,128)S(1)}, u32[]{:S(2)}, u32[]{:S(2)}) collective-permute-start(f32[7,8,128]{2,1,0:T(8,128)S(1)} %get-tuple-element.59), channel_id=1, source_target_pairs={{0,16},{8,24},{16,0},{24,8},{1,17},{9,25},{17,1},{25,9},{2,18},{10... | collective-permute-start | bytes 86024 | tf_op jit(solution)/shard_map/ppermute | solution.py:808
  11.9 2.5 %collective-permute-start.7 = (f32[7,8,128]{2,1,0:T(8,128)S(1)}, f32[7,8,128]{2,1,0:T(8,128)S(1)}, u32[]{:S(2)}, u32[]{:S(2)}) collective-permute-start(f32[7,8,128]{2,1,0:T(8,128)S(1)} %get-tuple-element.60), channel_id=1, source_target_pairs={{0,8},{8,0},{16,24},{24,16},{1,9},{9,1},{17,25},{25,17},{2,10},{10... | collective-permute-start | bytes 86024 | tf_op jit(solution)/shard_map/ppermute | solution.py:808
  14.8 4.1 %collective-permute-start.8 = (f32[9,8,128]{2,1,0:T(8,128)S(1)}, f32[9,8,128]{2,1,0:T(8,128)S(1)}, u32[]{:S(2)}, u32[]{:S(2)}) collective-permute-start(f32[9,8,128]{2,1,0:T(8,128)S(1)} %get-tuple-element.71), channel_id=1, source_target_pairs={{0,1},{1,0},{2,3},{3,2},{4,28},{5,29},{6,30},{7,31},{8,9},{9,8},{1... | collective-permute-start | bytes 110600 | tf_op jit(solution)/shard_map/ppermute | solution.py:385
  15.4 3.7 %collective-permute-start.9 = (f32[9,8,128]{2,1,0:T(8,128)S(1)}, f32[9,8,128]{2,1,0:T(8,128)S(1)}, u32[]{:S(2)}, u32[]{:S(2)}) collective-permute-start(f32[9,8,128]{2,1,0:T(8,128)S(1)} %get-tuple-element.72), channel_id=1, source_target_pairs={{0,24},{1,25},{2,26},{3,27},{4,5},{5,4},{6,7},{7,6},{8,16},{9,17},... | collective-permute-start | bytes 110600 | tf_op jit(solution)/shard_map/ppermute | solution.py:385
  15.4 4.0 %collective-permute-start.10 = (f32[9,8,128]{2,1,0:T(8,128)S(1)}, f32[9,8,128]{2,1,0:T(8,128)S(1)}, u32[]{:S(2)}, u32[]{:S(2)}) collective-permute-start(f32[9,8,128]{2,1,0:T(8,128)S(1)} %get-tuple-element.75), channel_id=1, source_target_pairs={{0,2},{1,3},{2,0},{3,1},{4,12},{5,13},{6,14},{7,15},{8,10},{9,11},... | collective-permute-start | bytes 110600 | tf_op jit(solution)/shard_map/ppermute | solution.py:385
  17.1 2.2 %collective-permute-start.11 = (f32[9,8,128]{2,1,0:T(8,128)S(1)}, f32[9,8,128]{2,1,0:T(8,128)S(1)}, u32[]{:S(2)}, u32[]{:S(2)}) collective-permute-start(f32[9,8,128]{2,1,0:T(8,128)S(1)} %get-tuple-element.76), channel_id=1, source_target_pairs={{0,8},{1,9},{2,4},{3,5},{4,2},{5,3},{6,14},{7,15},{8,0},{9,1},{10,... | collective-permute-start | bytes 110600 | tf_op jit(solution)/shard_map/ppermute | solution.py:385
  18.2 1.2 %collective-permute-start.12 = (f32[9,8,128]{2,1,0:T(8,128)S(1)}, f32[9,8,128]{2,1,0:T(8,128)S(1)}, u32[]{:S(2)}, u32[]{:S(2)}) collective-permute-start(f32[9,8,128]{2,1,0:T(8,128)S(1)} %get-tuple-element.77), channel_id=1, source_target_pairs={{0,8},{1,9},{2,10},{3,11},{4,6},{5,7},{6,4},{7,5},{8,0},{9,1},{10,... | collective-permute-start | bytes 110600 | tf_op jit(solution)/shard_map/ppermute | solution.py:385
